TPU v7x, 32 devices: a whole 2x2x4 slice. The times are simulated.
32 devices in a mesh: gx: 2 (over x), gy: 8 (over z, core), gz: 2 (over y).
Axes of the slice: x: 2, y: 2, z: 4, core: 2. Of those that a mesh axis runs over, the one named last changes fastest.
Arguments:
- forward_e: bfloat16 [3, 64, 128, 512], P(None, 'gz', 'gy', 'gx'), may hold values from -3 to 3
- forward_h: bfloat16 [3, 64, 128, 512], P(None, 'gz', 'gy', 'gx'), may hold values from -3 to 3
- adjoint_e: bfloat16 [3, 64, 128, 512], P(None, 'gz', 'gy', 'gx'), may hold values from -3 to 3
- adjoint_h: bfloat16 [3, 64, 128, 512], P(None, 'gz', 'gy', 'gx'), may hold values from -3 to 3
- material: int32 [64, 128, 512], P('gz', 'gy', 'gx'), may hold values from 0 to 3
- inv_permittivity: float32 [4], replicated, may hold values from 0.15 to 1
- height: int32 [128, 512], P('gy', 'gx'), may hold values from 0 to 64
Outputs:
- column_grad: float32 [128, 512], P('gy', 'gx')
- dual_h: float32 [3, 64, 128, 512], P(None, 'gz', 'gy', 'gx')
All inputs are finite; a program needn't handle non-finite values.
Results may differ from a plain program's by a relative error of at most 0.0003.
Values sent between devices are 32-bit elements; how exact they have to be, the bound alone decides.
No kernel may reach another device: no remote copies, remote signals or barrier semaphores. Data moves between devices by JAX's collectives and lax.ppermute only.
A program may use at most 320 MiB of HBM per device.

v0:
```python
import jax
import jax.numpy as jnp
from jax import lax
from jax.sharding import PartitionSpec as P

STEPS = 3


courant = 0.5


def from_behind(array, axis, by):
    length = lax.axis_size(axis)
    pairs = [(i, i + by) for i in range(length) if 0 <= i + by < length]
    return lax.ppermute(array, axis, pairs)


def upper_gap(stacked, dimension, arrived):
    remainder = lax.slice_in_dim(stacked, 1, stacked.shape[dimension], axis=dimension)
    return jnp.concatenate([remainder, arrived], axis=dimension) - stacked


def lower_gap(stacked, dimension, arrived):
    remainder = lax.slice_in_dim(stacked, 0, stacked.shape[dimension] - 1, axis=dimension)
    return stacked - jnp.concatenate([arrived, remainder], axis=dimension)


def first_layer(stacked, dimension):
    return lax.slice_in_dim(stacked, 0, 1, axis=dimension)


def last_layer(stacked, dimension):
    extent = stacked.shape[dimension]
    return lax.slice_in_dim(stacked, extent - 1, extent, axis=dimension)


def split_parts(stacked):
    groups = stacked.shape[0] // 3
    pieces_y = []
    pieces_x = stacked[1:3]
    pieces_y.append(stacked[0:1])
    pieces_y.append(stacked[2:3])
    pieces_z = stacked[0:2]
    part_y = jnp.concatenate(pieces_y, axis=0)
    return (groups, pieces_x, part_y, pieces_z)


def join_parts(along_x, along_y, along_z):
    pieces = []
    pieces.append(along_y[1:2] - along_z[1:2])
    pieces.append(along_z[0:1] - along_x[1:2])
    pieces.append(along_x[0:1] - along_y[0:1])
    return jnp.concatenate(pieces, axis=0)


def stacked_curl(stacked, upward):
    groups, part_x, part_y, part_z = split_parts(stacked)
    if upward:
        along_x = upper_gap(part_x, 3, from_behind(first_layer(part_x, 3), "gx", -1))
        along_y = upper_gap(part_y, 2, from_behind(first_layer(part_y, 2), "gy", -1))
        along_z = upper_gap(part_z, 1, from_behind(first_layer(part_z, 1), "gz", -1))
    else:
        along_x = lower_gap(part_x, 3, from_behind(last_layer(part_x, 3), "gx", 1))
        along_y = lower_gap(part_y, 2, from_behind(last_layer(part_y, 2), "gy", 1))
        along_z = lower_gap(part_z, 1, from_behind(last_layer(part_z, 1), "gz", 1))
    return join_parts(along_x, along_y, along_z)


def local(forward_e, forward_h, adjoint_e, adjoint_h, material, inv_permittivity, height):
    depth_cells, rows_cells, cols_cells = material.shape
    coefficient = jnp.zeros(material.shape, jnp.float32)
    for number in range(inv_permittivity.shape[0]):
        coefficient = coefficient + jnp.where(
            material == number, inv_permittivity[number], jnp.float32(0.0)
        )
    field_e = forward_e.astype(jnp.float32)
    field_h = forward_h.astype(jnp.float32)
    dual_e = adjoint_e.astype(jnp.float32)
    dual_h = adjoint_h.astype(jnp.float32)
    stored = [dual_e]
    forward_stored = []
    for number in range(STEPS):
        dual_h = dual_h + courant * stacked_curl(dual_e, True)
        dual_e = dual_e - courant * coefficient * stacked_curl(dual_h, False)
        if number + 1 < STEPS:
            stored.append(dual_e)
    for number in range(STEPS):
        field_h = field_h - courant * stacked_curl(field_e, True)
        field_e = field_e + courant * coefficient * stacked_curl(field_h, False)
        forward_stored.append(field_e)
    summed = jnp.zeros(material.shape, jnp.float32)
    for number in range(STEPS):
        current = forward_stored[number]
        partner = stored[STEPS - 1 - number]
        product = current[0] * partner[0] + current[1] * partner[1] + current[2] * partner[2]
        summed = summed + product
    depth_index = lax.axis_index("gz") * depth_cells + lax.broadcasted_iota(
        jnp.int32, material.shape, 0
    )
    texture = depth_index < height[None]
    local_sum = jnp.sum(jnp.where(texture, summed, jnp.float32(0.0)), axis=0)
    column_grad = lax.psum(local_sum, "gz")
    return (column_grad, dual_h)


def solution(mesh):
    return jax.shard_map(
        local,
        mesh=mesh,
        in_specs=(
            P(None, "gz", "gy", "gx"),
            P(None, "gz", "gy", "gx"),
            P(None, "gz", "gy", "gx"),
            P(None, "gz", "gy", "gx"),
            P("gz", "gy", "gx"),
            P(),
            P("gy", "gx"),
        ),
        out_specs=(P("gy", "gx"), P(None, "gz", "gy", "gx")),
        check_vma=False,
    )
```

profile of v0, /device:TPU:0, one launch (start us, length us, event | category | flops | bytes accessed | tf_op | source)
XLA Modules:
  0.0 182.1 jit_solution(15583553594966462967)
XLA Ops:
  2.7 1.8 slice.856
  14.0 3.8 %add_multiply_fusion = f32[32,16,256]{2,1,0:T(8,128)S(1)} fusion(s32[32,16,256]{2,1,0:T(8,128)} %param.11, f32[]{:T(128)} %bitcast.3, f32[]{:T(128)} %bitcast.2, f32[]{:T(128)} %bitcast.1, f32[]{:T(128)} %bitcast), kind=kLoop, calls=%fused_computation.170 | loop fusion | flops 1572864 | bytes 1048592 | tf_op jit(solution)/shard_map/mul | solution.py:89
  19.0 3.0 %collective-permute-done.8 = f32[2,32,16,1]{3,2,1,0:T(8,128)} collective-permute-done((f32[2,32,16,1]{3,2,1,0:T(8,128)}, f32[2,32,16,1]{3,2,1,0:T(8,128)}, u32[]{:S(2)}, u32[]{:S(2)}) %collective-permute-start.8) | collective-permute-done | bytes 4128 | tf_op jit(solution)/shard_map/ppermute | solution.py:15
  23.2 1.5 slice_subtract_fusion.17
  24.7 7.6 %collective-permute-done.2 = f32[2,32,16,1]{3,2,1,0:T(8,128)} collective-permute-done((f32[2,32,16,1]{3,2,1,0:T(8,128)}, f32[2,32,16,1]{3,2,1,0:T(8,128)}, u32[]{:S(2)}, u32[]{:S(2)}) %collective-permute-start.2) | collective-permute-done | bytes 4128 | tf_op jit(solution)/shard_map/ppermute | solution.py:15
  32.4 1.5 slice_subtract_fusion.21
  35.9 4.3 %collective-permute-start.10 = (f32[2,1,16,256]{3,2,1,0:T(8,128)S(1)}, f32[2,1,16,256]{3,2,1,0:T(8,128)S(1)}, u32[]{:S(2)}, u32[]{:S(2)}) collective-permute-start(f32[2,1,16,256]{3,2,1,0:T(8,128)S(1)} %slice.869), channel_id=1, source_target_pairs={{0,1},{2,3},{4,5},{6,7},{8,9},{10,11},{12,13},{14,15},{16,17},{18,... | collective-permute-start | bytes 98312 | tf_op jit(solution)/shard_map/ppermute | solution.py:15
  49.2 2.5 %collective-permute-done.11 = f32[2,32,16,1]{3,2,1,0:T(8,128)S(1)} collective-permute-done((f32[2,32,16,1]{3,2,1,0:T(8,128)S(1)}, f32[2,32,16,1]{3,2,1,0:T(8,128)S(1)}, u32[]{:S(2)}, u32[]{:S(2)}) %collective-permute-start.11) | collective-permute-done | bytes 4128 | tf_op jit(solution)/shard_map/ppermute | solution.py:15
  51.8 2.5 %collective-permute-start.3 = (f32[2,32,1,256]{3,2,1,0:T(1,128)S(1)}, f32[2,32,1,256]{3,2,1,0:T(1,128)S(1)}, u32[]{:S(2)}, u32[]{:S(2)}) collective-permute-start(f32[2,32,1,256]{3,2,1,0:T(1,128)S(1)} %fusion.53), channel_id=1, source_target_pairs={{0,2},{2,4},{4,6},{6,8},{8,10},{10,12},{12,14},{1,3},{3,5},{5,7},{... | collective-permute-start | bytes 196616 | tf_op jit(solution)/shard_map/ppermute | solution.py:15
  54.9 7.1 %collective-permute-done.5 = f32[2,32,16,1]{3,2,1,0:T(8,128)S(1)} collective-permute-done((f32[2,32,16,1]{3,2,1,0:T(8,128)S(1)}, f32[2,32,16,1]{3,2,1,0:T(8,128)S(1)}, u32[]{:S(2)}, u32[]{:S(2)}) %collective-permute-start.5) | collective-permute-done | bytes 4128 | tf_op jit(solution)/shard_map/ppermute | solution.py:15
  72.4 10.3 %collective-permute-done.14 = f32[2,32,16,1]{3,2,1,0:T(8,128)S(1)} collective-permute-done((f32[2,32,16,1]{3,2,1,0:T(8,128)S(1)}, f32[2,32,16,1]{3,2,1,0:T(8,128)S(1)}, u32[]{:S(2)}, u32[]{:S(2)}) %collective-permute-start.14) | collective-permute-done | bytes 4128 | tf_op jit(solution)/shard_map/ppermute | solution.py:15
  84.6 9.3 %collective-permute-done.20 = f32[2,32,16,1]{3,2,1,0:T(8,128)S(1)} collective-permute-done((f32[2,32,16,1]{3,2,1,0:T(8,128)S(1)}, f32[2,32,16,1]{3,2,1,0:T(8,128)S(1)}, u32[]{:S(2)}, u32[]{:S(2)}) %collective-permute-start.20) | collective-permute-done | bytes 4128 | tf_op jit(solution)/shard_map/ppermute | solution.py:15
  95.8 4.6 %collective-permute-start.16 = (f32[2,1,16,256]{3,2,1,0:T(8,128)S(1)}, f32[2,1,16,256]{3,2,1,0:T(8,128)S(1)}, u32[]{:S(2)}, u32[]{:S(2)}) collective-permute-start(f32[2,1,16,256]{3,2,1,0:T(8,128)S(1)} %slice.905), channel_id=1, source_target_pairs={{0,1},{2,3},{4,5},{6,7},{8,9},{10,11},{12,13},{14,15},{16,17},{18,... | collective-permute-start | bytes 98312 | tf_op jit(solution)/shard_map/ppermute | solution.py:15
  100.4 1.5 collective-permute-start.17
  105.5 1.6 collective-permute-start.22
  108.5 5.7 %collective-permute-done.17 = f32[2,32,16,1]{3,2,1,0:T(8,128)S(1)} collective-permute-done((f32[2,32,16,1]{3,2,1,0:T(8,128)S(1)}, f32[2,32,16,1]{3,2,1,0:T(8,128)S(1)}, u32[]{:S(2)}, u32[]{:S(2)}) %collective-permute-start.17) | collective-permute-done | bytes 4128 | tf_op jit(solution)/shard_map/ppermute | solution.py:15
  116.0 8.2 %collective-permute-done.23 = f32[2,32,16,1]{3,2,1,0:T(8,128)S(1)} collective-permute-done((f32[2,32,16,1]{3,2,1,0:T(8,128)S(1)}, f32[2,32,16,1]{3,2,1,0:T(8,128)S(1)}, u32[]{:S(2)}, u32[]{:S(2)}) %collective-permute-start.23) | collective-permute-done | bytes 4128 | tf_op jit(solution)/shard_map/ppermute | solution.py:15
  135.0 10.4 %collective-permute-done.26 = f32[2,32,16,1]{3,2,1,0:T(8,128)S(1)} collective-permute-done((f32[2,32,16,1]{3,2,1,0:T(8,128)S(1)}, f32[2,32,16,1]{3,2,1,0:T(8,128)S(1)}, u32[]{:S(2)}, u32[]{:S(2)}) %collective-permute-start.26) | collective-permute-done | bytes 4128 | tf_op jit(solution)/shard_map/ppermute | solution.py:15
  145.4 1.5 collective-permute-start.30
  147.4 7.3 %collective-permute-done.32 = f32[2,32,16,1]{3,2,1,0:T(8,128)S(1)} collective-permute-done((f32[2,32,16,1]{3,2,1,0:T(8,128)S(1)}, f32[2,32,16,1]{3,2,1,0:T(8,128)S(1)}, u32[]{:S(2)}, u32[]{:S(2)}) %collective-permute-start.32) | collective-permute-done | bytes 4128 | tf_op jit(solution)/shard_map/ppermute | solution.py:15
  156.8 4.3 %collective-permute-start.28 = (f32[2,1,16,256]{3,2,1,0:T(8,128)S(1)}, f32[2,1,16,256]{3,2,1,0:T(8,128)S(1)}, u32[]{:S(2)}, u32[]{:S(2)}) collective-permute-start(f32[2,1,16,256]{3,2,1,0:T(8,128)S(1)} %slice.982), channel_id=1, source_target_pairs={{0,1},{2,3},{4,5},{6,7},{8,9},{10,11},{12,13},{14,15},{16,17},{18,... | collective-permute-start | bytes 98312 | tf_op jit(solution)/shard_map/ppermute | solution.py:15
  164.6 1.8 fusion.10
  166.6 5.0 %collective-permute-done.29 = f32[2,32,16,1]{3,2,1,0:T(8,128)S(1)} collective-permute-done((f32[2,32,16,1]{3,2,1,0:T(8,128)S(1)}, f32[2,32,16,1]{3,2,1,0:T(8,128)S(1)}, u32[]{:S(2)}, u32[]{:S(2)}) %collective-permute-start.29) | collective-permute-done | bytes 4128 | tf_op jit(solution)/shard_map/ppermute | solution.py:15
  174.8 7.3 %psum.7 = f32[16,256]{1,0:T(8,128)} all-reduce(f32[16,256]{1,0:T(8,128)S(1)} %fusion.37), channel_id=1, replica_groups=mesh['gx'=2,'gy'=8,'gz'=2] {'gz'}, use_global_device_ids=true, to_apply=%region_1.2 | all-reduce | flops 4096 | bytes 32768 | tf_op jit(solution)/shard_map/psum | solution.py:102
  (187 shorter events, 65.8 us)
Async XLA Ops:
  1.4 21.8 %collective-permute-start.7 = (f32[2,1,16,256]{3,2,1,0:T(8,128)S(1)}, f32[2,1,16,256]{3,2,1,0:T(8,128)S(1)}, u32[]{:S(2)}, u32[]{:S(2)}) collective-permute-start(f32[2,1,16,256]{3,2,1,0:T(8,128)S(1)} %slice.851), channel_id=1, source_target_pairs={{1,0},{3,2},{5,4},{7,6},{9,8},{11,10},{13,12},{15,14},{17,16},{19,... | collective-permute-start | bytes 98312 | tf_op jit(solution)/shard_map/ppermute | solution.py:15
  4.5 17.4 %collective-permute-start.8 = (f32[2,32,16,1]{3,2,1,0:T(8,128)}, f32[2,32,16,1]{3,2,1,0:T(8,128)}, u32[]{:S(2)}, u32[]{:S(2)}) collective-permute-start(f32[2,32,16,1]{3,2,1,0:T(8,128)} %slice.856), channel_id=1, source_target_pairs={{16,0},{17,1},{18,2},{19,3},{20,4},{21,5},{22,6},{23,7},{24,8},{25... | collective-permute-start | bytes 12296 | tf_op jit(solution)/shard_map/ppermute | solution.py:15
  6.1 27.7 %collective-permute-start.6 = (f32[2,32,1,256]{3,2,1,0:T(1,128)S(1)}, f32[2,32,1,256]{3,2,1,0:T(1,128)S(1)}, u32[]{:S(2)}, u32[]{:S(2)}) collective-permute-start(f32[2,32,1,256]{3,2,1,0:T(1,128)S(1)} %fusion.52), channel_id=1, source_target_pairs={{2,0},{4,2},{6,4},{8,6},{10,8},{12,10},{14,12},{3,1},{5,3},{7,5},{... | collective-permute-start | bytes 196616 | tf_op jit(solution)/shard_map/ppermute | solution.py:15
  7.5 24.9 %collective-permute-start.1 = (f32[2,1,16,256]{3,2,1,0:T(8,128)S(1)}, f32[2,1,16,256]{3,2,1,0:T(8,128)S(1)}, u32[]{:S(2)}, u32[]{:S(2)}) collective-permute-start(f32[2,1,16,256]{3,2,1,0:T(8,128)S(1)} %slice.814), channel_id=1, source_target_pairs={{1,0},{3,2},{5,4},{7,6},{9,8},{11,10},{13,12},{15,14},{17,16},{19,... | collective-permute-start | bytes 98312 | tf_op jit(solution)/shard_map/ppermute | solution.py:15
  9.6 22.8 %collective-permute-start.2 = (f32[2,32,16,1]{3,2,1,0:T(8,128)}, f32[2,32,16,1]{3,2,1,0:T(8,128)}, u32[]{:S(2)}, u32[]{:S(2)}) collective-permute-start(f32[2,32,16,1]{3,2,1,0:T(8,128)} %slice.819), channel_id=1, source_target_pairs={{16,0},{17,1},{18,2},{19,3},{20,4},{21,5},{22,6},{23,7},{24,8},{25... | collective-permute-start | bytes 12296 | tf_op jit(solution)/shard_map/ppermute | solution.py:15
  21.9 19.9 %collective-permute-start = (f32[2,32,1,256]{3,2,1,0:T(1,128)S(1)}, f32[2,32,1,256]{3,2,1,0:T(1,128)S(1)}, u32[]{:S(2)}, u32[]{:S(2)}) collective-permute-start(f32[2,32,1,256]{3,2,1,0:T(1,128)S(1)} %fusion.54), channel_id=1, source_target_pairs={{2,0},{4,2},{6,4},{8,6},{10,8},{12,10},{14,12},{3,1},{5,3},{7,5},{... | collective-permute-start | bytes 196616 | tf_op jit(solution)/shard_map/ppermute | solution.py:15
  35.9 18.4 %collective-permute-start.10 = (f32[2,1,16,256]{3,2,1,0:T(8,128)S(1)}, f32[2,1,16,256]{3,2,1,0:T(8,128)S(1)}, u32[]{:S(2)}, u32[]{:S(2)}) collective-permute-start(f32[2,1,16,256]{3,2,1,0:T(8,128)S(1)} %slice.869), channel_id=1, source_target_pairs={{0,1},{2,3},{4,5},{6,7},{8,9},{10,11},{12,13},{14,15},{16,17},{18,... | collective-permute-start | bytes 98312 | tf_op jit(solution)/shard_map/ppermute | solution.py:15
  45.3 17.2 %collective-permute-start.9 = (f32[2,32,1,256]{3,2,1,0:T(1,128)S(1)}, f32[2,32,1,256]{3,2,1,0:T(1,128)S(1)}, u32[]{:S(2)}, u32[]{:S(2)}) collective-permute-start(f32[2,32,1,256]{3,2,1,0:T(1,128)S(1)} %fusion.51), channel_id=1, source_target_pairs={{0,2},{2,4},{4,6},{6,8},{8,10},{10,12},{12,14},{1,3},{3,5},{5,7},{... | collective-permute-start | bytes 196616 | tf_op jit(solution)/shard_map/ppermute | solution.py:15
  64.8 19.3 %collective-permute-start.13 = (f32[2,1,16,256]{3,2,1,0:T(8,128)S(1)}, f32[2,1,16,256]{3,2,1,0:T(8,128)S(1)}, u32[]{:S(2)}, u32[]{:S(2)}) collective-permute-start(f32[2,1,16,256]{3,2,1,0:T(8,128)S(1)} %slice.887), channel_id=1, source_target_pairs={{1,0},{3,2},{5,4},{7,6},{9,8},{11,10},{13,12},{15,14},{17,16},{19,... | collective-permute-start | bytes 98312 | tf_op jit(solution)/shard_map/ppermute | solution.py:15
  66.2 16.5 %collective-permute-start.14 = (f32[2,32,16,1]{3,2,1,0:T(8,128)S(1)}, f32[2,32,16,1]{3,2,1,0:T(8,128)S(1)}, u32[]{:S(2)}, u32[]{:S(2)}) collective-permute-start(f32[2,32,16,1]{3,2,1,0:T(8,128)S(1)} %slice.892), channel_id=1, source_target_pairs={{16,0},{17,1},{18,2},{19,3},{20,4},{21,5},{22,6},{23,7},{24,8},{25... | collective-permute-start | bytes 12296 | tf_op jit(solution)/shard_map/ppermute | solution.py:15
  68.5 25.9 %collective-permute-start.12 = (f32[2,32,1,256]{3,2,1,0:T(1,128)S(1)}, f32[2,32,1,256]{3,2,1,0:T(1,128)S(1)}, u32[]{:S(2)}, u32[]{:S(2)}) collective-permute-start(f32[2,32,1,256]{3,2,1,0:T(1,128)S(1)} %fusion.50), channel_id=1, source_target_pairs={{2,0},{4,2},{6,4},{8,6},{10,8},{12,10},{14,12},{3,1},{5,3},{7,5},{... | collective-permute-start | bytes 196616 | tf_op jit(solution)/shard_map/ppermute | solution.py:15
  69.8 24.1 %collective-permute-start.19 = (f32[2,1,16,256]{3,2,1,0:T(8,128)S(1)}, f32[2,1,16,256]{3,2,1,0:T(8,128)S(1)}, u32[]{:S(2)}, u32[]{:S(2)}) collective-permute-start(f32[2,1,16,256]{3,2,1,0:T(8,128)S(1)} %slice.926), channel_id=1, source_target_pairs={{1,0},{3,2},{5,4},{7,6},{9,8},{11,10},{13,12},{15,14},{17,16},{19,... | collective-permute-start | bytes 98312 | tf_op jit(solution)/shard_map/ppermute | solution.py:15
  71.1 22.8 %collective-permute-start.20 = (f32[2,32,16,1]{3,2,1,0:T(8,128)S(1)}, f32[2,32,16,1]{3,2,1,0:T(8,128)S(1)}, u32[]{:S(2)}, u32[]{:S(2)}) collective-permute-start(f32[2,32,16,1]{3,2,1,0:T(8,128)S(1)} %slice.931), channel_id=1, source_target_pairs={{16,0},{17,1},{18,2},{19,3},{20,4},{21,5},{22,6},{23,7},{24,8},{25... | collective-permute-start | bytes 12296 | tf_op jit(solution)/shard_map/ppermute | solution.py:15
  82.7 19.4 %collective-permute-start.18 = (f32[2,32,1,256]{3,2,1,0:T(1,128)S(1)}, f32[2,32,1,256]{3,2,1,0:T(1,128)S(1)}, u32[]{:S(2)}, u32[]{:S(2)}) collective-permute-start(f32[2,32,1,256]{3,2,1,0:T(1,128)S(1)} %fusion.48), channel_id=1, source_target_pairs={{2,0},{4,2},{6,4},{8,6},{10,8},{12,10},{14,12},{3,1},{5,3},{7,5},{... | collective-permute-start | bytes 196616 | tf_op jit(solution)/shard_map/ppermute | solution.py:15
  95.8 19.7 %collective-permute-start.16 = (f32[2,1,16,256]{3,2,1,0:T(8,128)S(1)}, f32[2,1,16,256]{3,2,1,0:T(8,128)S(1)}, u32[]{:S(2)}, u32[]{:S(2)}) collective-permute-start(f32[2,1,16,256]{3,2,1,0:T(8,128)S(1)} %slice.905), channel_id=1, source_target_pairs={{0,1},{2,3},{4,5},{6,7},{8,9},{10,11},{12,13},{14,15},{16,17},{18,... | collective-permute-start | bytes 98312 | tf_op jit(solution)/shard_map/ppermute | solution.py:15
  104.0 20.9 %collective-permute-start.15 = (f32[2,32,1,256]{3,2,1,0:T(1,128)S(1)}, f32[2,32,1,256]{3,2,1,0:T(1,128)S(1)}, u32[]{:S(2)}, u32[]{:S(2)}) collective-permute-start(f32[2,32,1,256]{3,2,1,0:T(1,128)S(1)} %fusion.49), channel_id=1, source_target_pairs={{0,2},{2,4},{4,6},{6,8},{8,10},{10,12},{12,14},{1,3},{3,5},{5,7},{... | collective-permute-start | bytes 196616 | tf_op jit(solution)/shard_map/ppermute | solution.py:15
  105.5 18.8 %collective-permute-start.22 = (f32[2,1,16,256]{3,2,1,0:T(8,128)S(1)}, f32[2,1,16,256]{3,2,1,0:T(8,128)S(1)}, u32[]{:S(2)}, u32[]{:S(2)}) collective-permute-start(f32[2,1,16,256]{3,2,1,0:T(8,128)S(1)} %slice.944), channel_id=1, source_target_pairs={{0,1},{2,3},{4,5},{6,7},{8,9},{10,11},{12,13},{14,15},{16,17},{18,... | collective-permute-start | bytes 98312 | tf_op jit(solution)/shard_map/ppermute | solution.py:15
  107.0 17.2 %collective-permute-start.23 = (f32[2,32,16,1]{3,2,1,0:T(8,128)S(1)}, f32[2,32,16,1]{3,2,1,0:T(8,128)S(1)}, u32[]{:S(2)}, u32[]{:S(2)}) collective-permute-start(f32[2,32,16,1]{3,2,1,0:T(8,128)S(1)} %slice.949), channel_id=1, source_target_pairs={{0,16},{1,17},{2,18},{3,19},{4,20},{5,21},{6,22},{7,23},{8,24},{9,... | collective-permute-start | bytes 12296 | tf_op jit(solution)/shard_map/ppermute | solution.py:15
  127.4 19.6 %collective-permute-start.25 = (f32[2,1,16,256]{3,2,1,0:T(8,128)S(1)}, f32[2,1,16,256]{3,2,1,0:T(8,128)S(1)}, u32[]{:S(2)}, u32[]{:S(2)}) collective-permute-start(f32[2,1,16,256]{3,2,1,0:T(8,128)S(1)} %slice.964), channel_id=1, source_target_pairs={{1,0},{3,2},{5,4},{7,6},{9,8},{11,10},{13,12},{15,14},{17,16},{19,... | collective-permute-start | bytes 98312 | tf_op jit(solution)/shard_map/ppermute | solution.py:15
  128.7 16.8 %collective-permute-start.26 = (f32[2,32,16,1]{3,2,1,0:T(8,128)S(1)}, f32[2,32,16,1]{3,2,1,0:T(8,128)S(1)}, u32[]{:S(2)}, u32[]{:S(2)}) collective-permute-start(f32[2,32,16,1]{3,2,1,0:T(8,128)S(1)} %slice.969), channel_id=1, source_target_pairs={{16,0},{17,1},{18,2},{19,3},{20,4},{21,5},{22,6},{23,7},{24,8},{25... | collective-permute-start | bytes 12296 | tf_op jit(solution)/shard_map/ppermute | solution.py:15
  131.1 24.1 %collective-permute-start.24 = (f32[2,32,1,256]{3,2,1,0:T(1,128)S(1)}, f32[2,32,1,256]{3,2,1,0:T(1,128)S(1)}, u32[]{:S(2)}, u32[]{:S(2)}) collective-permute-start(f32[2,32,1,256]{3,2,1,0:T(1,128)S(1)} %fusion.46), channel_id=1, source_target_pairs={{2,0},{4,2},{6,4},{8,6},{10,8},{12,10},{14,12},{3,1},{5,3},{7,5},{... | collective-permute-start | bytes 196616 | tf_op jit(solution)/shard_map/ppermute | solution.py:15
  132.4 22.3 %collective-permute-start.31 = (f32[2,1,16,256]{3,2,1,0:T(8,128)S(1)}, f32[2,1,16,256]{3,2,1,0:T(8,128)S(1)}, u32[]{:S(2)}, u32[]{:S(2)}) collective-permute-start(f32[2,1,16,256]{3,2,1,0:T(8,128)S(1)} %slice.1002), channel_id=1, source_target_pairs={{1,0},{3,2},{5,4},{7,6},{9,8},{11,10},{13,12},{15,14},{17,16},{19,... | collective-permute-start | bytes 98312 | tf_op jit(solution)/shard_map/ppermute | solution.py:15
  133.7 21.0 %collective-permute-start.32 = (f32[2,32,16,1]{3,2,1,0:T(8,128)S(1)}, f32[2,32,16,1]{3,2,1,0:T(8,128)S(1)}, u32[]{:S(2)}, u32[]{:S(2)}) collective-permute-start(f32[2,32,16,1]{3,2,1,0:T(8,128)S(1)} %slice.1007), channel_id=1, source_target_pairs={{16,0},{17,1},{18,2},{19,3},{20,4},{21,5},{22,6},{23,7},{24,8},{25... | collective-permute-start | bytes 12296 | tf_op jit(solution)/shard_map/ppermute | solution.py:15
  145.4 18.5 %collective-permute-start.30 = (f32[2,32,1,256]{3,2,1,0:T(1,128)S(1)}, f32[2,32,1,256]{3,2,1,0:T(1,128)S(1)}, u32[]{:S(2)}, u32[]{:S(2)}) collective-permute-start(f32[2,32,1,256]{3,2,1,0:T(1,128)S(1)} %fusion.44), channel_id=1, source_target_pairs={{2,0},{4,2},{6,4},{8,6},{10,8},{12,10},{14,12},{3,1},{5,3},{7,5},{... | collective-permute-start | bytes 196616 | tf_op jit(solution)/shard_map/ppermute | solution.py:15
  (19 other events, 149.2 us)
where the time goes:
time: 183 us; the launch traced here: 182 us
  waiting for transfers between devices  76.5 us (42%)
  starting transfers between devices  54.8 us (30%)
  other arithmetic  29.5 us (16%)
  local copies, waits for them, and re-layouts  12.1 us (7%)
  blocking collectives  7.32 us (4%)
  between operations  1.88 us (1%)
    ppermute x33, waiting for transfers between devices, from_behind(): return lax.ppermute(array, axis, pairs)  76.5 us
    ppermute x33, starting transfers between devices, from_behind(): return lax.ppermute(array, axis, pairs)  54.8 us
    psum x1, blocking collectives, local(): column_grad = lax.psum(local_sum, 'gz')  7.32 us
    sub x12, other arithmetic, upper_gap(): return jnp.concatenate([remainder, arrived], axis=dimension) - stacked  6.56 us
    sub x10, other arithmetic, lower_gap(): return stacked - jnp.concatenate([arrived, remainder], axis=dimension)  4.11 us
    sub x11, other arithmetic, join_parts(): pieces.append(along_y[1:2] - along_z[1:2])  4.02 us
    mul x1, other arithmetic, local(): field_e = field_e + courant * coefficient * stacked_curl(field_h, False)  3.8 us
    concatenate x22, other arithmetic, split_parts(): part_y = jnp.concatenate(pieces_y, axis=0)  3.68 us
  transfers between devices with their start and end apart: 33, of which 11 were waited for; matrix products, arithmetic and copies ran while one was open for 18% of the time, Pallas kernels for 0%

commit v1 on v0

v1 whole, which is shorter than its diff:
```python
import functools

import jax
import jax.numpy as jnp
import numpy as np
from jax import lax
from jax.experimental import pallas as pl
from jax.experimental.pallas import tpu as pltpu
from jax.sharding import PartitionSpec as P

STEPS = 3
COURANT = 0.5
LANES = 128
TILE = 8
WIDE = 3
SHIFT = 4
COUNT = 13
FE, FH, AE, AH, KAPPA = 0, 3, 6, 9, 12
LOW_DEPTH = [3] * 3 + [3] * 3 + [2] * 3 + [2] * 3 + [2]
HIGH_DEPTH = [3] * 3 + [2] * 3 + [3] * 3 + [2] * 3 + [2]
LAYERS = sum(LOW_DEPTH)
SCALE = [1.0] * 3 + [-1.0 / COURANT] * 3 + [1.0] * 3 + [1.0 / COURANT] * 3 + [1.0]
F32 = jnp.float32
BF16 = jnp.bfloat16


def layers_to_next(length):
    return [(c, length - d + k, k - d) for c, d in enumerate(LOW_DEPTH) for k in range(d)]


def layers_to_previous(length):
    return [(c, k, length + k) for c, d in enumerate(HIGH_DEPTH) for k in range(d)]


def swap_pairs(length, offset):
    pairs = []
    for i in range(offset, length - 1, 2):
        pairs += [(i, i + 1), (i + 1, i)]
    return pairs


def swap(array, axis, offset):
    return lax.ppermute(array, axis, swap_pairs(lax.axis_size(axis), offset))


def row_picker(rows):
    to_next = np.zeros((LAYERS, COUNT * rows), np.float32)
    to_previous = np.zeros((LAYERS, COUNT * rows), np.float32)
    for n, (c, own, _) in enumerate(layers_to_next(rows)):
        to_next[n, c * rows + own] = 1
    for n, (c, own, _) in enumerate(layers_to_previous(rows)):
        to_previous[n, c * rows + own] = 1
    even = np.concatenate([to_next, to_previous])
    odd = np.concatenate([to_previous, to_next])
    return even, odd


def row_placer(rows):
    low = np.zeros((COUNT * TILE, LAYERS), np.float32)
    high = np.zeros((COUNT * TILE, LAYERS), np.float32)
    for n, (c, _, there) in enumerate(layers_to_next(rows)):
        low[c * TILE + there + SHIFT, n] = SCALE[c]
    for n, (c, _, there) in enumerate(layers_to_previous(rows)):
        high[c * TILE + there - rows + SHIFT, n] = SCALE[c]
    even = np.concatenate([high, low], axis=1)
    odd = np.concatenate([low, high], axis=1)
    return even, odd


def lane_of(shape):
    return lax.broadcasted_iota(jnp.int32, shape, len(shape) - 1)


def row_of(shape):
    return lax.broadcasted_iota(jnp.int32, shape, len(shape) - 2)


def own_field(refs, c, z):
    fe, fh, ae, ah, material = refs
    if c == KAPPA:
        return (material[z] + 1).astype(F32).astype(BF16)
    return (fe, fh, ae, ah)[c // 3][c % 3, z]


def pack_kernel(x_messages, flags, fe, fh, ae, ah, material, picker, *outs):
    depth, rows, cols = material.shape
    refs = (fe, fh, ae, ah, material)
    x_out = outs[:x_messages]
    z_out, ya_out, yb_out = outs[x_messages:]
    chunk = 8
    odd_x, odd_z = flags[0], flags[1]

    for number in range(x_messages):
        first = jnp.where(odd_x == number, 1, 0)
        offset = pl.multiple_of(first * (cols - LANES), LANES)
        row = row_of((LANES, LANES))
        lane = lane_of((LANES, LANES))
        spot = lane % TILE
        top = jnp.where(spot >= TILE - WIDE, LANES - TILE + spot, -1)
        bottom = jnp.where(spot < WIDE, spot, -1)
        picked = row == jnp.where(first == 1, top, bottom)
        pickers = [
            jnp.where(picked & (lane // TILE == c), 1.0, 0.0).astype(BF16) for c in range(COUNT)
        ]

        def columns(step, _):
            start = step * chunk
            total = jnp.zeros((chunk * rows, LANES), F32)
            for c in range(COUNT):
                if c == KAPPA:
                    part = material[pl.ds(start, chunk), :, pl.ds(offset, LANES)]
                    part = (part + 1).astype(F32).astype(BF16)
                else:
                    part = (fe, fh, ae, ah)[c // 3][
                        c % 3, pl.ds(start, chunk), :, pl.ds(offset, LANES)
                    ]
                total += jnp.dot(
                    part.reshape(chunk * rows, LANES), pickers[c], preferred_element_type=F32
                )
            x_out[number][pl.ds(start, chunk)] = total.reshape(chunk, rows, LANES)
            return 0

        lax.fori_loop(0, depth // chunk, columns, 0)

    @pl.when(odd_z == 0)
    def _():
        for n, (c, own, _) in enumerate(layers_to_next(depth)):
            z_out[n] = own_field(refs, c, own).astype(F32)

    @pl.when(odd_z == 1)
    def _():
        for n, (c, own, _) in enumerate(layers_to_previous(depth)):
            z_out[n] = own_field(refs, c, own).astype(F32)

    def plane(z, _):
        stacked = jnp.concatenate([own_field(refs, c, z) for c in range(COUNT)], axis=0)
        picked = jnp.dot(picker[...], stacked, preferred_element_type=F32)
        ya_out[z] = picked[:LAYERS]
        yb_out[z] = picked[LAYERS:]
        return 0

    lax.fori_loop(0, depth, plane, 0)


def edge_rows(array, odd, message):
    rows = array.shape[0]
    row = row_of((TILE, LANES))
    last = pltpu.roll(array[rows - TILE:], 4, 0)
    first = pltpu.roll(array[:TILE], 4, 0)
    last = jnp.where((row >= 1) & (row < 4), last, 0.0)
    first = jnp.where((row >= 4) & (row < 7), first, 0.0)
    return jnp.where(odd == message, last, first)


def corner_kernel(flags, xp, xz, zr, a_out, b_out):
    depth, rows, _ = xp.shape
    cols = zr.shape[2]
    tiles = cols // LANES
    odd_y, odd_z = flags[2], flags[1]
    base = LAYERS * tiles
    for message, out in ((0, a_out), (1, b_out)):
        for n in range(LAYERS):
            for t in range(tiles):
                out[n * tiles + t] = edge_rows(
                    zr[n, :, t * LANES:(t + 1) * LANES], odd_y, message
                )

        def plane(z, _):
            out[base + WIDE + z] = edge_rows(xp[z], odd_y, message)
            return 0

        lax.fori_loop(0, depth, plane, 0)
        there = jnp.where(odd_z == 1, 0, depth + WIDE)
        for k in range(WIDE):
            out[base + there + k] = edge_rows(xz[k], odd_y, message)
            out[base + depth + WIDE - there + k] = jnp.zeros((TILE, LANES), F32)


def spread(tiles, halo):
    low = row_of((TILE, LANES)) < SHIFT
    turned = [pltpu.roll(t, SHIFT, 0) for t in tiles]
    out = [jnp.where(low, halo, turned[0])]
    for before, after in zip(turned, turned[1:]):
        out.append(jnp.where(low, before, after))
    out.append(jnp.where(low, turned[-1], halo))
    return out


def gather(tiles):
    low = row_of((TILE, LANES)) < SHIFT
    turned = [pltpu.roll(t, SHIFT, 0) for t in tiles]
    return [jnp.where(low, before, after) for before, after in zip(turned, turned[1:])]


def window_kernel(
    flags, inverse, fe, fh, ae, ah, material, height, xp, xz, zr, ya, yb, corner_a, corner_b,
    placer, grad_out, dual_out, field, stored, wide_x,
):
    depth, rows, cols = material.shape
    own = cols // LANES
    tiles = own + 1
    blocks = rows // TILE + 1
    planes = depth + 2 * WIDE
    refs = (fe, fh, ae, ah, material)
    odd_z = flags[1]
    has_low, has_high = flags[5], flags[6]
    start_z = flags[7]
    row = row_of((TILE, LANES))
    lane = lane_of((TILE, LANES))

    def lane_tile(array, t):
        return array[:, t * LANES:(t + 1) * LANES]

    zero = jnp.zeros((TILE, LANES), F32)
    for t in range(tiles):
        for b in range(blocks):
            for c in range(3):
                field[FH + c, WIDE - 1, t, pl.ds(b * TILE, TILE)] = zero
                field[AH + c, WIDE - 1, t, pl.ds(b * TILE, TILE)] = zero
                field[FE + c, depth + WIDE, t, pl.ds(b * TILE, TILE)] = zero
                field[AE + c, depth + WIDE, t, pl.ds(b * TILE, TILE)] = zero
                stored[c, depth + WIDE, t, pl.ds(b * TILE, TILE)] = zero
                stored[3 + c, depth + WIDE, t, pl.ds(b * TILE, TILE)] = zero

    base = LAYERS * own

    def put_wide(slot, own_rows):
        halo = corner_a[base + slot] + corner_b[base + slot]
        parts = spread([own_rows[b * TILE:(b + 1) * TILE] for b in range(blocks - 1)], halo)
        for b, part in enumerate(parts):
            wide_x[slot, pl.ds(b * TILE, TILE)] = part

    def wide_plane(z, _):
        put_wide(z + WIDE, xp[z])
        return 0

    lax.fori_loop(0, depth, wide_plane, 0)
    there = jnp.where(odd_z == 1, 0, depth + WIDE)
    for k in range(WIDE):
        put_wide(there + k, xz[k])
        put_wide(depth + WIDE - there + k, jnp.zeros((rows, LANES), F32))

    def place_columns(c, _):
        scale = jnp.where(
            (c >= FH) & (c < FH + 3), SCALE[FH], jnp.where((c >= AH) & (c < AH + 3), SCALE[AH], 1.0)
        )
        source = row_of((LANES, LANES))
        target = lane_of((LANES, LANES))
        spot = source % TILE
        lands = jnp.where(spot < TILE // 2, spot, LANES - TILE + spot)
        placed = (target == lands) & (source // TILE == c)
        matrix = jnp.where(placed, scale, 0.0).astype(BF16)
        block = wide_x[...].reshape(planes * blocks * TILE, LANES).astype(BF16)
        result = jnp.dot(block, matrix, preferred_element_type=F32)
        field[c, :, own] = result.reshape(planes, blocks * TILE, LANES)
        return 0

    lax.fori_loop(0, COUNT, place_columns, 0)

    def put(c, slot, t, own_tiles, halo):
        for b, part in enumerate(spread(own_tiles, halo)):
            field[c, slot, t, pl.ds(b * TILE, TILE)] = part

    def halo_planes(layers):
        for n, (c, _, position) in enumerate(layers):
            for t in range(own):
                whole = lane_tile(zr[n], t)
                halo = corner_a[n * own + t] + corner_b[n * own + t]
                pieces = [whole[b * TILE:(b + 1) * TILE] for b in range(blocks - 1)]
                if SCALE[c] != 1.0:
                    pieces = [p * SCALE[c] for p in pieces]
                    halo = halo * SCALE[c]
                put(c, position + WIDE, t, pieces, halo)

    @pl.when(odd_z == 0)
    def _():
        halo_planes(layers_to_previous(depth))

    @pl.when(odd_z == 1)
    def _():
        halo_planes(layers_to_next(depth))

    def own_plane(z, _):
        arrived = jnp.concatenate([ya[z], yb[z]], axis=0).astype(BF16)
        halos = jnp.dot(placer[...], arrived, preferred_element_type=F32)
        for c in range(COUNT):
            whole = own_field(refs, c, z).astype(F32)
            for t in range(own):
                halo = lane_tile(halos[c * TILE:(c + 1) * TILE], t)
                part = lane_tile(whole, t)
                pieces = [part[b * TILE:(b + 1) * TILE] for b in range(blocks - 1)]
                if SCALE[c] != 1.0:
                    pieces = [p * SCALE[c] for p in pieces]
                put(c, z + WIDE, t, pieces, halo)
        return 0

    lax.fori_loop(0, depth, own_plane, 0)

    squared = [inverse[m] * (COURANT * COURANT) for m in range(inverse.shape[0])]

    def factor_plane(slot, _):
        for t in range(tiles):
            for b in range(blocks):
                at = (KAPPA, slot, t, pl.ds(b * TILE, TILE))
                number = field[at]
                value = jnp.zeros((TILE, LANES), F32)
                for m, weight in enumerate(squared):
                    value = jnp.where(number == m + 1, weight, value)
                field[at] = value
        return 0

    lax.fori_loop(1, planes - 1, factor_plane, 0)

    keep_row = jnp.where((row < SHIFT) & (flags[3] == 1), 0.0, 1.0)
    keep_lane = jnp.where((lane >= LANES // 2) & (flags[4] == 1), 0.0, 1.0)

    def mask(value, t, b):
        if b == 0:
            value = value * keep_row
        if t == own:
            value = value * keep_lane
        return value

    def ahead_rows(ref, c, slot, t, b, tile):
        if b == blocks - 1:
            return pltpu.roll(tile, TILE - 1, 0)
        return ref[c, slot, t, pl.ds(b * TILE + 1, TILE)]

    def behind_rows(ref, c, slot, t, b, tile):
        if b == 0:
            return pltpu.roll(tile, 1, 0)
        return ref[c, slot, t, pl.ds(b * TILE - 1, TILE)]

    def ahead_lanes(parts):
        turned = [pltpu.roll(p, LANES - 1, 1) for p in parts]
        return [jnp.where(lane == LANES - 1, turned[(t + 1) % tiles], turned[t]) for t in range(tiles)]

    def behind_lanes(parts):
        turned = [pltpu.roll(p, 1, 1) for p in parts]
        return [jnp.where(lane == 0, turned[(t - 1) % tiles], turned[t]) for t in range(tiles)]

    def span(low, high):
        return WIDE + jnp.where(has_low == 1, low, 0), WIDE + depth + jnp.where(has_high == 1, high, 0)

    def rows_at(b):
        return pl.ds(b * TILE, TILE)

    def magnetic(e, g, low, high, emit=None):
        e_ref, e0 = e
        g0 = g
        width = own if emit is not None else tiles

        def plane(slot, _):
            results = {}
            for b in range(blocks):
                at = rows_at(b)
                here = [[e_ref[e0 + c, slot, t, at] for t in range(tiles)] for c in range(3)]
                y_x = ahead_lanes(here[1])
                z_x = ahead_lanes(here[2])
                for t in range(width):
                    ex, ey, ez = here[0][t], here[1][t], here[2][t]
                    ex_y = ahead_rows(e_ref, e0, slot, t, b, ex)
                    ez_y = ahead_rows(e_ref, e0 + 2, slot, t, b, ez)
                    ex_z = e_ref[e0, slot + 1, t, at]
                    ey_z = e_ref[e0 + 1, slot + 1, t, at]
                    curl = (
                        (ez_y - ez) - (ey_z - ey),
                        (ex_z - ex) - (z_x[t] - ez),
                        (y_x[t] - ey) - (ex_y - ex),
                    )
                    for c in range(3):
                        value = field[g0 + c, slot, t, at] + curl[c]
                        if emit is None:
                            field[g0 + c, slot, t, at] = mask(value, t, b)
                        else:
                            results[c, t, b] = value
            if emit is not None:
                emit(slot, results)
            return 0

        begin, end = span(low, high)
        lax.fori_loop(begin, end, plane, 0)

    def electric(e, g, to, low, high, partner=None, totals=None):
        e_ref, e0 = e
        to_ref, to0 = to
        g0 = g

        def plane(slot, carry):
            carry = list(carry)
            if partner is not None:
                p_ref, p0 = partner
                position = slot - WIDE
                inside = (position >= 0) & (position < depth)
                position = jnp.where(inside, position + start_z, jnp.int32(2**30))
            for b in range(blocks):
                at = rows_at(b)
                here = [[field[g0 + c, slot, t, at] for t in range(tiles)] for c in range(3)]
                y_x = behind_lanes(here[1])
                z_x = behind_lanes(here[2])
                for t in range(tiles):
                    gx, gy, gz = here[0][t], here[1][t], here[2][t]
                    gx_y = behind_rows(field, g0, slot, t, b, gx)
                    gz_y = behind_rows(field, g0 + 2, slot, t, b, gz)
                    gx_z = field[g0, slot - 1, t, at]
                    gy_z = field[g0 + 1, slot - 1, t, at]
                    curl = (
                        (gz - gz_y) - (gy - gy_z),
                        (gx - gx_z) - (gz - z_x[t]),
                        (gy - y_x[t]) - (gx - gx_y),
                    )
                    factor = field[KAPPA, slot, t, at]
                    product = None
                    for c in range(3):
                        value = e_ref[e0 + c, slot, t, at] - factor * curl[c]
                        to_ref[to0 + c, slot, t, at] = value
                        if partner is not None and t < own:
                            term = value * p_ref[p0 + c, slot, t, at]
                            product = term if product is None else product + term
                    if product is not None:
                        inside = position < limits[t * blocks + b]
                        carry[t * blocks + b] += jnp.where(inside, product, 0.0)
            return tuple(carry)

        begin, end = span(low, high)
        return lax.fori_loop(begin, end, plane, totals if totals is not None else ())

    first = (field, AE)
    second = (stored, 0)
    third = (stored, 3)
    forward = (field, FE)

    def emit_dual(slot, results):
        for c in range(3):
            for t in range(own):
                values = gather([results[c, t, b] for b in range(blocks)])
                for b, value in enumerate(values):
                    dual_out[c, slot - WIDE, rows_at(b), t * LANES:(t + 1) * LANES] = value * COURANT

    magnetic(first, AH, -2, 2)
    electric(first, AH, second, -1, 2)
    magnetic(second, AH, -1, 1)
    electric(second, AH, third, 0, 1)
    magnetic(third, AH, 0, 0, emit_dual)

    none = jnp.zeros((TILE, LANES), jnp.int32)
    limits = []
    for t in range(own):
        part = lane_tile(height[...], t)
        limits += spread([part[b * TILE:(b + 1) * TILE] for b in range(blocks - 1)], none)
    totals = (zero,) * (own * blocks)
    magnetic(forward, FH, -3, 2)
    totals = electric(forward, FH, forward, -2, 2, third, totals)
    magnetic(forward, FH, -2, 1)
    totals = electric(forward, FH, forward, -1, 1, second, totals)
    magnetic(forward, FH, -1, 0)
    totals = electric(forward, FH, forward, 0, 0, first, totals)
    for t in range(own):
        values = gather(list(totals[t * blocks:(t + 1) * blocks]))
        for b, value in enumerate(values):
            grad_out[rows_at(b), t * LANES:(t + 1) * LANES] = value


def local(forward_e, forward_h, adjoint_e, adjoint_h, material, inv_permittivity, height):
    depth, rows, cols = material.shape
    tiles = cols // LANES
    gx, gy, gz = (lax.axis_index(a) for a in ("gx", "gy", "gz"))
    nx, ny, nz = (lax.axis_size(a) for a in ("gx", "gy", "gz"))
    assert nz == 2
    flags = jnp.stack([
        gx % 2, gz % 2, gy % 2,
        jnp.where(gy == 0, 1, 0), jnp.where(gx == 0, 1, 0),
        jnp.where(gz > 0, 1, 0), jnp.where(gz < nz - 1, 1, 0),
        gz * depth,
    ]).astype(jnp.int32)
    picker = [jnp.asarray(m, BF16) for m in row_picker(rows)]
    picker = jnp.where(gy % 2 == 0, picker[0], picker[1])
    placer = [jnp.asarray(m, BF16) for m in row_placer(rows)]
    placer = jnp.where(gy % 2 == 0, placer[0], placer[1])
    vmem = pl.BlockSpec(memory_space=pltpu.VMEM)
    smem = pl.BlockSpec(memory_space=pltpu.SMEM)
    params = pltpu.CompilerParams(vmem_limit_bytes=60 * 1024 * 1024)
    x_messages = 1 if nx == 2 else 2

    y_shape = jax.ShapeDtypeStruct((depth, LAYERS, cols), F32)
    packed = pl.pallas_call(
        functools.partial(pack_kernel, x_messages),
        out_shape=[jax.ShapeDtypeStruct((depth, rows, LANES), F32)] * x_messages
        + [jax.ShapeDtypeStruct((LAYERS, rows, cols), F32), y_shape, y_shape],
        in_specs=[smem] + [vmem] * 6,
        out_specs=[vmem] * (x_messages + 3),
        compiler_params=params,
        name="pack",
    )(flags, forward_e, forward_h, adjoint_e, adjoint_h, material, picker)
    z_message, ya, yb = packed[x_messages:]
    yb = swap(yb, "gy", 1)
    ya = swap(ya, "gy", 0)
    xp = swap(packed[0], "gx", 0)
    if x_messages == 2:
        xp = xp + swap(packed[1], "gx", 1)
    zr = swap(z_message, "gz", 0)
    xz = lax.dynamic_slice_in_dim(xp, jnp.where(gz % 2 == 0, depth - WIDE, 0), WIDE, axis=0)
    xz = swap(xz, "gz", 0)

    corner_shape = jax.ShapeDtypeStruct((LAYERS * tiles + depth + 2 * WIDE, TILE, LANES), F32)
    corner_a, corner_b = pl.pallas_call(
        corner_kernel,
        out_shape=[corner_shape, corner_shape],
        in_specs=[smem] + [vmem] * 3,
        out_specs=[vmem] * 2,
        compiler_params=params,
        name="corners",
    )(flags, xp, xz, zr)
    corner_b = swap(corner_b, "gy", 1)
    corner_a = swap(corner_a, "gy", 0)

    blocks = rows // TILE + 1
    planes = depth + 2 * WIDE
    block = (planes, tiles + 1, blocks * TILE, LANES)
    grad, dual = pl.pallas_call(
        window_kernel,
        out_shape=[
            jax.ShapeDtypeStruct((rows, cols), F32),
            jax.ShapeDtypeStruct((3, depth, rows, cols), F32),
        ],
        in_specs=[smem, smem] + [vmem] * 14,
        out_specs=[vmem] * 2,
        scratch_shapes=[
            pltpu.VMEM((COUNT,) + block, F32),
            pltpu.VMEM((6,) + block, F32),
            pltpu.VMEM((planes, blocks * TILE, LANES), F32),
        ],
        compiler_params=params,
        name="window",
    )(
        flags, inv_permittivity, forward_e, forward_h, adjoint_e, adjoint_h, material, height,
        xp, xz, zr, ya, yb, corner_a, corner_b, placer,
    )
    return grad + swap(grad, "gz", 0), dual


def solution(mesh):
    fields = P(None, "gz", "gy", "gx")
    return jax.shard_map(
        local,
        mesh=mesh,
        in_specs=(fields, fields, fields, fields, P("gz", "gy", "gx"), P(), P("gy", "gx")),
        out_specs=(P("gy", "gx"), fields),
        check_vma=False,
    )
```

time: 183 us -> 103 us (0.56)
  the two profiles are of different devices: /device:TPU:0 before, /device:TPU:1 now
where the time goes in v1:
time: 103 us; the launch traced here: 102 us
  Pallas kernels  63.7 us (62%)
  waiting for transfers between devices  16.2 us (16%)
  starting transfers between devices  14.4 us (14%)
  local copies, waits for them, and re-layouts  4.15 us (4%)
  other arithmetic  3.32 us (3%)
    pallas_call x1, Pallas kernels, local(): pl.pallas_call(window_kernel, out_shape=[jax.ShapeDtypeStruct((rows, cols...  51.7 us
    ppermute x8, waiting for transfers between devices, swap(): return lax.ppermute(array, axis, swap_pairs(lax.axis_size(axis), offset))  16.2 us
    ppermute x8, starting transfers between devices, swap(): return lax.ppermute(array, axis, swap_pairs(lax.axis_size(axis), offset))  14.4 us
    pallas_call x1, Pallas kernels, local(): pl.pallas_call(functools.partial(pack_kernel, x_messages), out_shape=[jax...  9.38 us
    unnamed x18, local copies, waits for them, and re-layouts  3.5 us
    pallas_call x1, Pallas kernels, local(): pl.pallas_call(corner_kernel, out_shape=[corner_shape, corner_shape], in_...  2.62 us
  transfers between devices with their start and end apart: 8, of which 4 were waited for; matrix products, arithmetic and copies ran while one was open for 1% of the time, Pallas kernels for 3%

profile of v1, /device:TPU:1, one launch (start us, length us, event | category | flops | bytes accessed | tf_op | source)
XLA Modules:
  0.0 102.5 jit_solution(13336550942650241539)
XLA Ops:
  0.7 1.4 %broadcast_select_fusion.picker = bf16[64,208]{1,0:T(8,128)(2,1)} fusion(bf16[64,208]{1,0:T(8,128)(2,1)} %constant.54.clone, bf16[64,208]{1,0:T(8,128)(2,1)} %constant.55.clone, pred[]{:T(512)S(6)} %eq.22), kind=kLoop, calls=%fused_computation | loop fusion | flops 13312 | bytes 79873 | tf_op jit(solution)/shard_map/jit(_where)/select_n | solution.py:477
  2.1 0.7 stack.35.flags
  2.7 9.4 %pack.1 = (f32[32,16,128]{2,1,0:T(8,128)}, f32[32,16,256]{2,1,0:T(8,128)}, f32[32,32,256]{2,1,0:T(8,128)}, f32[32,32,256]{2,1,0:T(8,128)}) custom-call(s32[8]{0:T(128)} %stack.35.flags, bf16[3,32,16,256]{3,2,1,0:T(8,128)(2,1)} %fe.3, bf16[3,32,16,256]{3,2,1,0:T(8,128)(2,1)} %fh.3, bf16[3,32,16,256]{3,2,1,0:T(8,128)(2,1)} %ae.3, bf16[3,32,16,256]{3,2,1,0:T(8,128)(2,1)} %ah.3, ...), custom_call_target="tpu_custom_call" | custom-call | tf_op jit(solution)/shard_map/pack/pallas_call | solution.py:486
  12.1 0.1 collective-permute-start.3
  12.2 4.5 %collective-permute-start.4 = (f32[32,32,256]{2,1,0:T(8,128)}, f32[32,32,256]{2,1,0:T(8,128)S(1)}, u32[]{:S(2)}, u32[]{:S(2)}) collective-permute-start(f32[32,32,256]{2,1,0:T(8,128)} %get-tuple-element.13), channel_id=1, source_target_pairs={{2,4},{4,2},{6,8},{8,6},{10,12},{12,10},{3,5},{5,3},{7,9},{9,7},{1... | collective-permute-start | bytes 3145736 | tf_op jit(solution)/shard_map/ppermute | solution.py:43
  16.7 1.3 %collective-permute-start.2 = (f32[32,16,256]{2,1,0:T(8,128)}, f32[32,16,256]{2,1,0:T(8,128)S(1)}, u32[]{:S(2)}, u32[]{:S(2)}) collective-permute-start(f32[32,16,256]{2,1,0:T(8,128)} %get-tuple-element.11), channel_id=1, source_target_pairs={{0,1},{1,0},{2,3},{3,2},{4,5},{5,4},{6,7},{7,6},{8,9},{9,8},{10,11... | collective-permute-start | bytes 1572872 | tf_op jit(solution)/shard_map/ppermute | solution.py:43
  18.0 1.2 %collective-permute-start = (f32[32,16,128]{2,1,0:T(8,128)}, f32[32,16,128]{2,1,0:T(8,128)S(1)}, u32[]{:S(2)}, u32[]{:S(2)}) collective-permute-start(f32[32,16,128]{2,1,0:T(8,128)} %get-tuple-element.10), channel_id=1, source_target_pairs={{0,16},{16,0},{1,17},{17,1},{2,18},{18,2},{3,19},{19,3},{4,20},{20... | collective-permute-start | bytes 786440 | tf_op jit(solution)/shard_map/ppermute | solution.py:43
  19.2 5.7 %collective-permute-done.xp = f32[32,16,128]{2,1,0:T(8,128)S(1)} collective-permute-done((f32[32,16,128]{2,1,0:T(8,128)}, f32[32,16,128]{2,1,0:T(8,128)S(1)}, u32[]{:S(2)}, u32[]{:S(2)}) %collective-permute-start) | collective-permute-done | bytes 262176 | tf_op jit(solution)/shard_map/ppermute | solution.py:43
  24.9 0.0 collective-permute-start.1
  24.9 3.8 %collective-permute-done.1.xz = f32[3,16,128]{2,1,0:T(8,128)S(1)} collective-permute-done((f32[3,16,128]{2,1,0:T(8,128)S(1)}, f32[3,16,128]{2,1,0:T(8,128)S(1)}, u32[]{:S(2)}, u32[]{:S(2)}) %collective-permute-start.1) | collective-permute-done | bytes 24608 | tf_op jit(solution)/shard_map/ppermute | solution.py:43
  28.8 0.0 collective-permute-done.2.zr
  28.8 0.6 copy-done.6
  29.4 0.8 copy-done
  30.2 2.6 %corners.1 = (f32[102,8,128]{2,1,0:T(8,128)}, f32[102,8,128]{2,1,0:T(8,128)}) custom-call(s32[8]{0:T(128)} %stack.35.flags, f32[32,16,128]{2,1,0:T(8,128)} %copy-done.1, f32[3,16,128]{2,1,0:T(8,128)} %copy-done.6, f32[32,16,256]{2,1,0:T(8,128)} %copy-done), custom_call_target="tpu_custom_call" | custom-call | tf_op jit(solution)/shard_map/corners/pallas_call | solution.py:506
  32.8 5.5 %collective-permute-start.6 = (f32[102,8,128]{2,1,0:T(8,128)}, f32[102,8,128]{2,1,0:T(8,128)S(1)}, u32[]{:S(2)}, u32[]{:S(2)}) collective-permute-start(f32[102,8,128]{2,1,0:T(8,128)} %get-tuple-element.15), channel_id=1, source_target_pairs={{2,4},{4,2},{6,8},{8,6},{10,12},{12,10},{3,5},{5,3},{7,9},{9,7},{1... | collective-permute-start | bytes 1253384 | tf_op jit(solution)/shard_map/ppermute | solution.py:43
  38.3 0.6 broadcast_select_fusion.1.placer
  38.9 5.3 %collective-permute-done.6.corner_b = f32[102,8,128]{2,1,0:T(8,128)S(1)} collective-permute-done((f32[102,8,128]{2,1,0:T(8,128)}, f32[102,8,128]{2,1,0:T(8,128)S(1)}, u32[]{:S(2)}, u32[]{:S(2)}) %collective-permute-start.6) | collective-permute-done | bytes 417824 | tf_op jit(solution)/shard_map/ppermute | solution.py:43
  44.2 0.7 copy-done.5
  45.0 0.4 copy-done.2
  45.4 1.0 copy-done.3
  46.3 51.7 %window.1 = (f32[16,256]{1,0:T(8,128)}, f32[3,32,16,256]{3,2,1,0:T(8,128)}) custom-call(s32[8]{0:T(128)} %stack.35.flags, f32[4]{0:T(128)} %inverse.1, bf16[3,32,16,256]{3,2,1,0:T(8,128)(2,1)} %fe.3, bf16[3,32,16,256]{3,2,1,0:T(8,128)(2,1)} %fh.3, bf16[3,32,16,256]{3,2,1,0:T(8,128)(2,1)} %ae.3, bf16[3,32,16,256]{3,2,1,0:T(8,128)(2,1)} %ah.3, ...), custom_call_target="tpu_custom_call" | custom-call | tf_op jit(solution)/shard_map/window/pallas_call | solution.py:520
  98.0 1.8 %collective-permute-start.7 = (f32[16,256]{1,0:T(8,128)}, f32[16,256]{1,0:T(8,128)S(1)}, u32[]{:S(2)}, u32[]{:S(2)}) collective-permute-start(f32[16,256]{1,0:T(8,128)} %get-tuple-element.16), channel_id=1, source_target_pairs={{0,1},{1,0},{2,3},{3,2},{4,5},{5,4},{6,7},{7,6},{8,9},{9,8},{10,11... | collective-permute-start | bytes 49160 | tf_op jit(solution)/shard_map/ppermute | solution.py:43
  99.8 1.3 %collective-permute-done.7 = f32[16,256]{1,0:T(8,128)S(1)} collective-permute-done((f32[16,256]{1,0:T(8,128)}, f32[16,256]{1,0:T(8,128)S(1)}, u32[]{:S(2)}, u32[]{:S(2)}) %collective-permute-start.7) | collective-permute-done | bytes 16416 | tf_op jit(solution)/shard_map/ppermute | solution.py:43
  101.1 1.3 %add.20 = f32[16,256]{1,0:T(8,128)} add(f32[16,256]{1,0:T(8,128)} %get-tuple-element.16, f32[16,256]{1,0:T(8,128)S(1)} %collective-permute-done.7) | non-fusion elementwise | flops 4096 | bytes 49152 | tf_op jit(solution)/shard_map/add | solution.py:539
  (18 shorter events, 0.0 us)
Async XLA Ops:
  2.7 35.6 %copy-start.7 = (bf16[104,64]{1,0:T(8,128)(2,1)S(1)}, bf16[104,64]{1,0:T(8,128)(2,1)}, u32[]{:S(2)}) copy-start(bf16[104,64]{1,0:T(8,128)(2,1)} %constant.57.clone) | copy-start | bytes 39940
  2.7 35.6 %copy-start.8 = (bf16[104,64]{1,0:T(8,128)(2,1)S(1)}, bf16[104,64]{1,0:T(8,128)(2,1)}, u32[]{:S(2)}) copy-start(bf16[104,64]{1,0:T(8,128)(2,1)} %constant.56.clone) | copy-start | bytes 39940
  12.1 32.1 %collective-permute-start.3 = (f32[32,32,256]{2,1,0:T(8,128)}, f32[32,32,256]{2,1,0:T(8,128)S(1)}, u32[]{:S(2)}, u32[]{:S(2)}) collective-permute-start(f32[32,32,256]{2,1,0:T(8,128)} %get-tuple-element.12), channel_id=1, source_target_pairs={{0,2},{2,0},{4,6},{6,4},{8,10},{10,8},{12,14},{14,12},{1,3},{3,1},... | collective-permute-start | bytes 3145736 | tf_op jit(solution)/shard_map/ppermute | solution.py:43
  12.2 32.1 %collective-permute-start.4 = (f32[32,32,256]{2,1,0:T(8,128)}, f32[32,32,256]{2,1,0:T(8,128)S(1)}, u32[]{:S(2)}, u32[]{:S(2)}) collective-permute-start(f32[32,32,256]{2,1,0:T(8,128)} %get-tuple-element.13), channel_id=1, source_target_pairs={{2,4},{4,2},{6,8},{8,6},{10,12},{12,10},{3,5},{5,3},{7,9},{9,7},{1... | collective-permute-start | bytes 3145736 | tf_op jit(solution)/shard_map/ppermute | solution.py:43
  16.7 12.1 %collective-permute-start.2 = (f32[32,16,256]{2,1,0:T(8,128)}, f32[32,16,256]{2,1,0:T(8,128)S(1)}, u32[]{:S(2)}, u32[]{:S(2)}) collective-permute-start(f32[32,16,256]{2,1,0:T(8,128)} %get-tuple-element.11), channel_id=1, source_target_pairs={{0,1},{1,0},{2,3},{3,2},{4,5},{5,4},{6,7},{7,6},{8,9},{9,8},{10,11... | collective-permute-start | bytes 1572872 | tf_op jit(solution)/shard_map/ppermute | solution.py:43
  18.0 6.9 %collective-permute-start = (f32[32,16,128]{2,1,0:T(8,128)}, f32[32,16,128]{2,1,0:T(8,128)S(1)}, u32[]{:S(2)}, u32[]{:S(2)}) collective-permute-start(f32[32,16,128]{2,1,0:T(8,128)} %get-tuple-element.10), channel_id=1, source_target_pairs={{0,16},{16,0},{1,17},{17,1},{2,18},{18,2},{3,19},{19,3},{4,20},{20... | collective-permute-start | bytes 786440 | tf_op jit(solution)/shard_map/ppermute | solution.py:43
  24.9 3.8 %copy-start.1 = (f32[32,16,128]{2,1,0:T(8,128)}, f32[32,16,128]{2,1,0:T(8,128)S(1)}, u32[]{:S(2)}) copy-start(f32[32,16,128]{2,1,0:T(8,128)S(1)} %collective-permute-done.xp) | copy-start | bytes 786436
  24.9 3.8 %collective-permute-start.1 = (f32[3,16,128]{2,1,0:T(8,128)S(1)}, f32[3,16,128]{2,1,0:T(8,128)S(1)}, u32[]{:S(2)}, u32[]{:S(2)}) collective-permute-start(f32[3,16,128]{2,1,0:T(8,128)S(1)} %constant_dynamic-slice_fusion), channel_id=1, source_target_pairs={{0,1},{1,0},{2,3},{3,2},{4,5},{5,4},{6,7},{7,6},{8,9},{9,8},{10,11... | collective-permute-start | bytes 73736 | tf_op jit(solution)/shard_map/ppermute | solution.py:43
  28.8 0.6 copy-start.6
  29.4 0.8 copy-start
  32.8 6.2 %collective-permute-start.5 = (f32[102,8,128]{2,1,0:T(8,128)}, f32[102,8,128]{2,1,0:T(8,128)S(1)}, u32[]{:S(2)}, u32[]{:S(2)}) collective-permute-start(f32[102,8,128]{2,1,0:T(8,128)} %get-tuple-element.14), channel_id=1, source_target_pairs={{0,2},{2,0},{4,6},{6,4},{8,10},{10,8},{12,14},{14,12},{1,3},{3,1},... | collective-permute-start | bytes 1253384 | tf_op jit(solution)/shard_map/ppermute | solution.py:43
  32.8 11.4 %collective-permute-start.6 = (f32[102,8,128]{2,1,0:T(8,128)}, f32[102,8,128]{2,1,0:T(8,128)S(1)}, u32[]{:S(2)}, u32[]{:S(2)}) collective-permute-start(f32[102,8,128]{2,1,0:T(8,128)} %get-tuple-element.15), channel_id=1, source_target_pairs={{2,4},{4,2},{6,8},{8,6},{10,12},{12,10},{3,5},{5,3},{7,9},{9,7},{1... | collective-permute-start | bytes 1253384 | tf_op jit(solution)/shard_map/ppermute | solution.py:43
  38.9 5.3 %copy-start.4 = (f32[102,8,128]{2,1,0:T(8,128)}, f32[102,8,128]{2,1,0:T(8,128)S(1)}, u32[]{:S(2)}) copy-start(f32[102,8,128]{2,1,0:T(8,128)S(1)} %collective-permute-done.5.corner_a) | copy-start | bytes 1253380
  44.2 0.8 copy-start.5
  44.2 1.1 %copy-start.2 = (f32[32,32,256]{2,1,0:T(8,128)}, f32[32,32,256]{2,1,0:T(8,128)S(1)}, u32[]{:S(2)}) copy-start(f32[32,32,256]{2,1,0:T(8,128)S(1)} %collective-permute-done.3.ya) | copy-start | bytes 3145732
  45.4 1.0 copy-start.3
  98.0 3.1 %collective-permute-start.7 = (f32[16,256]{1,0:T(8,128)}, f32[16,256]{1,0:T(8,128)S(1)}, u32[]{:S(2)}, u32[]{:S(2)}) collective-permute-start(f32[16,256]{1,0:T(8,128)} %get-tuple-element.16), channel_id=1, source_target_pairs={{0,1},{1,0},{2,3},{3,2},{4,5},{5,4},{6,7},{7,6},{8,9},{9,8},{10,11... | collective-permute-start | bytes 49160 | tf_op jit(solution)/shard_map/ppermute | solution.py:43

commit v2 on v1

--- a/solution.py
+++ b/solution.py
@@ -13,6 +13,9 @@
 LANES = 128
 TILE = 8
 WIDE = 3
+BEFORE = 4
+AFTER = 5
+UNROLL = 2
 SHIFT = 4
 COUNT = 13
 FE, FH, AE, AH, KAPPA = 0, 3, 6, 9, 12
@@ -194,7 +197,8 @@
 
 def window_kernel(
     flags, inverse, fe, fh, ae, ah, material, height, xp, xz, zr, ya, yb, corner_a, corner_b,
-    placer, grad_out, dual_out, field, stored, wide_x,
+    placer, grad_out, dual_out, forward_e, forward_g, dual_e, dual_g, second_e, third_e, factor,
+    wide_x,
 ):
     depth, rows, cols = material.shape
     own = cols // LANES
@@ -203,74 +207,99 @@
     planes = depth + 2 * WIDE
     refs = (fe, fh, ae, ah, material)
     odd_z = flags[1]
-    has_low, has_high = flags[5], flags[6]
     start_z = flags[7]
     row = row_of((TILE, LANES))
     lane = lane_of((TILE, LANES))
+    zero = jnp.zeros((TILE, LANES), F32)
+    squared = [inverse[m] * (COURANT * COURANT) for m in range(inverse.shape[0])]
+
+    def rows_at(b):
+        return pl.ds(b * TILE, TILE)
 
     def lane_tile(array, t):
         return array[:, t * LANES:(t + 1) * LANES]
 
-    zero = jnp.zeros((TILE, LANES), F32)
+    def row_tiles(array):
+        return [array[b * TILE:(b + 1) * TILE] for b in range(blocks - 1)]
+
+    def target(c):
+        if c == KAPPA:
+            return factor, 0
+        return (forward_e, forward_g, dual_e, dual_g)[c // 3], c % 3
+
+    def weight(number):
+        value = jnp.zeros(number.shape, F32)
+        for m, w in enumerate(squared):
+            value = jnp.where(number == m + 1, w, value)
+        return value
+
     for t in range(tiles):
         for b in range(blocks):
             for c in range(3):
-                field[FH + c, WIDE - 1, t, pl.ds(b * TILE, TILE)] = zero
-                field[AH + c, WIDE - 1, t, pl.ds(b * TILE, TILE)] = zero
-                field[FE + c, depth + WIDE, t, pl.ds(b * TILE, TILE)] = zero
-                field[AE + c, depth + WIDE, t, pl.ds(b * TILE, TILE)] = zero
-                stored[c, depth + WIDE, t, pl.ds(b * TILE, TILE)] = zero
-                stored[3 + c, depth + WIDE, t, pl.ds(b * TILE, TILE)] = zero
+                forward_g[c, BEFORE - 1, t, rows_at(b)] = zero
+                dual_g[c, BEFORE - 1, t, rows_at(b)] = zero
+                for ref in (forward_e, dual_e, second_e, third_e):
+                    ref[c, depth + BEFORE, t, rows_at(b)] = zero
 
     base = LAYERS * own
 
     def put_wide(slot, own_rows):
         halo = corner_a[base + slot] + corner_b[base + slot]
-        parts = spread([own_rows[b * TILE:(b + 1) * TILE] for b in range(blocks - 1)], halo)
-        for b, part in enumerate(parts):
-            wide_x[slot, pl.ds(b * TILE, TILE)] = part
-
-    def wide_plane(z, _):
-        put_wide(z + WIDE, xp[z])
+        return slot, spread(row_tiles(own_rows), halo)
+
+    def store_wide(items):
+        for slot, parts in items:
+            for b, part in enumerate(parts):
+                wide_x[slot, rows_at(b)] = part
+
+    def wide_planes(step, _):
+        store_wide([put_wide(step * 8 + k + WIDE, xp[step * 8 + k]) for k in range(8)])
         return 0
 
-    lax.fori_loop(0, depth, wide_plane, 0)
+    lax.fori_loop(0, depth // 8, wide_planes, 0)
     there = jnp.where(odd_z == 1, 0, depth + WIDE)
+    items = []
     for k in range(WIDE):
-        put_wide(there + k, xz[k])
-        put_wide(depth + WIDE - there + k, jnp.zeros((rows, LANES), F32))
-
-    def place_columns(c, _):
-        scale = jnp.where(
-            (c >= FH) & (c < FH + 3), SCALE[FH], jnp.where((c >= AH) & (c < AH + 3), SCALE[AH], 1.0)
-        )
-        source = row_of((LANES, LANES))
-        target = lane_of((LANES, LANES))
-        spot = source % TILE
-        lands = jnp.where(spot < TILE // 2, spot, LANES - TILE + spot)
-        placed = (target == lands) & (source // TILE == c)
-        matrix = jnp.where(placed, scale, 0.0).astype(BF16)
-        block = wide_x[...].reshape(planes * blocks * TILE, LANES).astype(BF16)
-        result = jnp.dot(block, matrix, preferred_element_type=F32)
-        field[c, :, own] = result.reshape(planes, blocks * TILE, LANES)
-        return 0
-
-    lax.fori_loop(0, COUNT, place_columns, 0)
-
-    def put(c, slot, t, own_tiles, halo):
-        for b, part in enumerate(spread(own_tiles, halo)):
-            field[c, slot, t, pl.ds(b * TILE, TILE)] = part
+        items.append(put_wide(there + k, xz[k]))
+        items.append(put_wide(depth + WIDE - there + k, jnp.zeros((rows, LANES), F32)))
+    store_wide(items)
+
+    source = row_of((LANES, LANES))
+    spot = source % TILE
+    lands = jnp.where(spot < TILE // 2, spot, LANES - TILE + spot) == lane_of((LANES, LANES))
+    wide = wide_x[...].reshape(planes * blocks * TILE, LANES).astype(BF16)
+    pairs = [(c, c + 1) if c + 1 < COUNT else (c,) for c in range(0, COUNT, 2)]
+    for pair in pairs:
+        matrix = [jnp.where(lands & (source // TILE == c), SCALE[c], 0.0).astype(BF16) for c in pair]
+        matrix = jnp.concatenate(matrix, axis=1) if len(pair) > 1 else matrix[0]
+        result = jnp.dot(wide, matrix, preferred_element_type=F32)
+        for n, c in enumerate(pair):
+            ref, at = target(c)
+            value = lane_tile(result, n).reshape(planes, blocks * TILE, LANES)
+            ref[at, pl.ds(BEFORE - WIDE, planes), own] = weight(value) if c == KAPPA else value
+
+    def store(items):
+        for c, slot, t, parts in items:
+            ref, at = target(c)
+            for b, part in enumerate(parts):
+                ref[at, slot, t, rows_at(b)] = part
+
+    def arrange(c, own_tiles, halo):
+        if c == KAPPA:
+            own_tiles = [weight(p) for p in own_tiles]
+            halo = weight(halo)
+        elif SCALE[c] != 1.0:
+            own_tiles = [p * SCALE[c] for p in own_tiles]
+        return spread(own_tiles, halo)
 
     def halo_planes(layers):
         for n, (c, _, position) in enumerate(layers):
+            items = []
             for t in range(own):
-                whole = lane_tile(zr[n], t)
-                halo = corner_a[n * own + t] + corner_b[n * own + t]
-                pieces = [whole[b * TILE:(b + 1) * TILE] for b in range(blocks - 1)]
-                if SCALE[c] != 1.0:
-                    pieces = [p * SCALE[c] for p in pieces]
-                    halo = halo * SCALE[c]
-                put(c, position + WIDE, t, pieces, halo)
+                halo = (corner_a[n * own + t] + corner_b[n * own + t]) * SCALE[c]
+                parts = arrange(c, row_tiles(lane_tile(zr[n], t)), halo)
+                items.append((c, position + BEFORE, t, parts))
+            store(items)
 
     @pl.when(odd_z == 0)
     def _():
@@ -280,36 +309,22 @@
     def _():
         halo_planes(layers_to_next(depth))
 
-    def own_plane(z, _):
-        arrived = jnp.concatenate([ya[z], yb[z]], axis=0).astype(BF16)
-        halos = jnp.dot(placer[...], arrived, preferred_element_type=F32)
-        for c in range(COUNT):
-            whole = own_field(refs, c, z).astype(F32)
-            for t in range(own):
-                halo = lane_tile(halos[c * TILE:(c + 1) * TILE], t)
-                part = lane_tile(whole, t)
-                pieces = [part[b * TILE:(b + 1) * TILE] for b in range(blocks - 1)]
-                if SCALE[c] != 1.0:
-                    pieces = [p * SCALE[c] for p in pieces]
-                put(c, z + WIDE, t, pieces, halo)
+    def own_planes(step, _):
+        items = []
+        for k in range(2):
+            z = step * 2 + k
+            arrived = jnp.concatenate([ya[z], yb[z]], axis=0).astype(BF16)
+            halos = jnp.dot(placer[...], arrived, preferred_element_type=F32)
+            for c in range(COUNT):
+                whole = own_field(refs, c, z).astype(F32)
+                for t in range(own):
+                    halo = lane_tile(halos[c * TILE:(c + 1) * TILE], t)
+                    parts = arrange(c, row_tiles(lane_tile(whole, t)), halo)
+                    items.append((c, z + BEFORE, t, parts))
+        store(items)
         return 0
 
-    lax.fori_loop(0, depth, own_plane, 0)
-
-    squared = [inverse[m] * (COURANT * COURANT) for m in range(inverse.shape[0])]
-
-    def factor_plane(slot, _):
-        for t in range(tiles):
-            for b in range(blocks):
-                at = (KAPPA, slot, t, pl.ds(b * TILE, TILE))
-                number = field[at]
-                value = jnp.zeros((TILE, LANES), F32)
-                for m, weight in enumerate(squared):
-                    value = jnp.where(number == m + 1, weight, value)
-                field[at] = value
-        return 0
-
-    lax.fori_loop(1, planes - 1, factor_plane, 0)
+    lax.fori_loop(0, depth // 2, own_planes, 0)
 
     keep_row = jnp.where((row < SHIFT) & (flags[3] == 1), 0.0, 1.0)
     keep_lane = jnp.where((lane >= LANES // 2) & (flags[4] == 1), 0.0, 1.0)
@@ -321,16 +336,6 @@
             value = value * keep_lane
         return value
 
-    def ahead_rows(ref, c, slot, t, b, tile):
-        if b == blocks - 1:
-            return pltpu.roll(tile, TILE - 1, 0)
-        return ref[c, slot, t, pl.ds(b * TILE + 1, TILE)]
-
-    def behind_rows(ref, c, slot, t, b, tile):
-        if b == 0:
-            return pltpu.roll(tile, 1, 0)
-        return ref[c, slot, t, pl.ds(b * TILE - 1, TILE)]
-
     def ahead_lanes(parts):
         turned = [pltpu.roll(p, LANES - 1, 1) for p in parts]
         return [jnp.where(lane == LANES - 1, turned[(t + 1) % tiles], turned[t]) for t in range(tiles)]
@@ -339,122 +344,132 @@
         turned = [pltpu.roll(p, 1, 1) for p in parts]
         return [jnp.where(lane == 0, turned[(t - 1) % tiles], turned[t]) for t in range(tiles)]
 
-    def span(low, high):
-        return WIDE + jnp.where(has_low == 1, low, 0), WIDE + depth + jnp.where(has_high == 1, high, 0)
-
-    def rows_at(b):
-        return pl.ds(b * TILE, TILE)
-
-    def magnetic(e, g, low, high, emit=None):
-        e_ref, e0 = e
-        g0 = g
+    def reader(ref, slot):
+        seen = {}
+
+        def read(c, ahead, t, b):
+            if (c, ahead, t, b) not in seen:
+                seen[c, ahead, t, b] = ref[c, slot + ahead, t, rows_at(b)]
+            return seen[c, ahead, t, b]
+
+        def ahead_rows(c, ahead, t, b):
+            if b == blocks - 1:
+                return pltpu.roll(read(c, ahead, t, b), TILE - 1, 0)
+            return ref[c, slot + ahead, t, pl.ds(b * TILE + 1, TILE)]
+
+        def behind_rows(c, ahead, t, b):
+            if b == 0:
+                return pltpu.roll(read(c, ahead, t, b), 1, 0)
+            return ref[c, slot + ahead, t, pl.ds(b * TILE - 1, TILE)]
+
+        return read, ahead_rows, behind_rows
+
+    def begin(count):
+        return BEFORE + jnp.where(odd_z == 1, depth - count, 0)
+
+    def magnetic(e, g, count, emit=None):
         width = own if emit is not None else tiles
-
-        def plane(slot, _):
+        first = begin(count)
+
+        def step(number, _):
+            slot = first + number * UNROLL
+            read, ahead_rows, _ = reader(e, slot)
+            old, _, _ = reader(g, slot)
             results = {}
-            for b in range(blocks):
-                at = rows_at(b)
-                here = [[e_ref[e0 + c, slot, t, at] for t in range(tiles)] for c in range(3)]
-                y_x = ahead_lanes(here[1])
-                z_x = ahead_lanes(here[2])
-                for t in range(width):
-                    ex, ey, ez = here[0][t], here[1][t], here[2][t]
-                    ex_y = ahead_rows(e_ref, e0, slot, t, b, ex)
-                    ez_y = ahead_rows(e_ref, e0 + 2, slot, t, b, ez)
-                    ex_z = e_ref[e0, slot + 1, t, at]
-                    ey_z = e_ref[e0 + 1, slot + 1, t, at]
-                    curl = (
-                        (ez_y - ez) - (ey_z - ey),
-                        (ex_z - ex) - (z_x[t] - ez),
-                        (y_x[t] - ey) - (ex_y - ex),
-                    )
-                    for c in range(3):
-                        value = field[g0 + c, slot, t, at] + curl[c]
-                        if emit is None:
-                            field[g0 + c, slot, t, at] = mask(value, t, b)
-                        else:
-                            results[c, t, b] = value
+            for k in range(UNROLL):
+                for b in range(blocks):
+                    y_x = ahead_lanes([read(1, k, t, b) for t in range(tiles)])
+                    z_x = ahead_lanes([read(2, k, t, b) for t in range(tiles)])
+                    for t in range(width):
+                        ex, ey, ez = (read(c, k, t, b) for c in range(3))
+                        curl = (
+                            (ahead_rows(2, k, t, b) - ez) - (read(1, k + 1, t, b) - ey),
+                            (read(0, k + 1, t, b) - ex) - (z_x[t] - ez),
+                            (y_x[t] - ey) - (ahead_rows(0, k, t, b) - ex),
+                        )
+                        for c in range(3):
+                            value = old(c, k, t, b) + curl[c]
+                            results[c, k, t, b] = value if emit is not None else mask(value, t, b)
             if emit is not None:
                 emit(slot, results)
+            else:
+                for (c, k, t, b), value in results.items():
+                    g[c, slot + k, t, rows_at(b)] = value
             return 0
 
-        begin, end = span(low, high)
-        lax.fori_loop(begin, end, plane, 0)
-
-    def electric(e, g, to, low, high, partner=None, totals=None):
-        e_ref, e0 = e
-        to_ref, to0 = to
-        g0 = g
-
-        def plane(slot, carry):
+        lax.fori_loop(0, count // UNROLL, step, 0)
+
+    def electric(e, g, to, count, partner=None, totals=()):
+        first = begin(count)
+
+        def step(number, carry):
             carry = list(carry)
-            if partner is not None:
-                p_ref, p0 = partner
-                position = slot - WIDE
-                inside = (position >= 0) & (position < depth)
-                position = jnp.where(inside, position + start_z, jnp.int32(2**30))
-            for b in range(blocks):
-                at = rows_at(b)
-                here = [[field[g0 + c, slot, t, at] for t in range(tiles)] for c in range(3)]
-                y_x = behind_lanes(here[1])
-                z_x = behind_lanes(here[2])
-                for t in range(tiles):
-                    gx, gy, gz = here[0][t], here[1][t], here[2][t]
-                    gx_y = behind_rows(field, g0, slot, t, b, gx)
-                    gz_y = behind_rows(field, g0 + 2, slot, t, b, gz)
-                    gx_z = field[g0, slot - 1, t, at]
-                    gy_z = field[g0 + 1, slot - 1, t, at]
-                    curl = (
-                        (gz - gz_y) - (gy - gy_z),
-                        (gx - gx_z) - (gz - z_x[t]),
-                        (gy - y_x[t]) - (gx - gx_y),
-                    )
-                    factor = field[KAPPA, slot, t, at]
-                    product = None
-                    for c in range(3):
-                        value = e_ref[e0 + c, slot, t, at] - factor * curl[c]
-                        to_ref[to0 + c, slot, t, at] = value
-                        if partner is not None and t < own:
-                            term = value * p_ref[p0 + c, slot, t, at]
-                            product = term if product is None else product + term
-                    if product is not None:
-                        inside = position < limits[t * blocks + b]
-                        carry[t * blocks + b] += jnp.where(inside, product, 0.0)
+            slot = first + number * UNROLL
+            read, _, behind_rows = reader(g, slot)
+            old, _, _ = reader(e, slot)
+            weights, _, _ = reader(factor, slot)
+            results = {}
+            for k in range(UNROLL):
+                if partner is not None:
+                    position = slot + k - BEFORE
+                    inside = (position >= 0) & (position < depth)
+                    position = jnp.where(inside, position + start_z, jnp.int32(2**30))
+                for b in range(blocks):
+                    y_x = behind_lanes([read(1, k, t, b) for t in range(tiles)])
+                    z_x = behind_lanes([read(2, k, t, b) for t in range(tiles)])
+                    for t in range(tiles):
+                        gx, gy, gz = (read(c, k, t, b) for c in range(3))
+                        curl = (
+                            (gz - behind_rows(2, k, t, b)) - (gy - read(1, k - 1, t, b)),
+                            (gx - read(0, k - 1, t, b)) - (gz - z_x[t]),
+                            (gy - y_x[t]) - (gx - behind_rows(0, k, t, b)),
+                        )
+                        scale = weights(0, k, t, b)
+                        product = None
+                        for c in range(3):
+                            value = old(c, k, t, b) - scale * curl[c]
+                            results[c, k, t, b] = value
+                            if partner is not None and t < own:
+                                term = value * partner[c, slot + k, t, rows_at(b)]
+                                product = term if product is None else product + term
+                        if product is not None:
+                            chosen = position < limits[t * blocks + b]
+                            carry[t * blocks + b] += jnp.where(chosen, product, 0.0)
+            for (c, k, t, b), value in results.items():
+                to[c, slot + k, t, rows_at(b)] = value
             return tuple(carry)
 
-        begin, end = span(low, high)
-        return lax.fori_loop(begin, end, plane, totals if totals is not None else ())
-
-    first = (field, AE)
-    second = (stored, 0)
-    third = (stored, 3)
-    forward = (field, FE)
+        return lax.fori_loop(0, count // UNROLL, step, totals)
 
     def emit_dual(slot, results):
-        for c in range(3):
-            for t in range(own):
-                values = gather([results[c, t, b] for b in range(blocks)])
-                for b, value in enumerate(values):
-                    dual_out[c, slot - WIDE, rows_at(b), t * LANES:(t + 1) * LANES] = value * COURANT
-
-    magnetic(first, AH, -2, 2)
-    electric(first, AH, second, -1, 2)
-    magnetic(second, AH, -1, 1)
-    electric(second, AH, third, 0, 1)
-    magnetic(third, AH, 0, 0, emit_dual)
+        for k in range(UNROLL):
+            for c in range(3):
+                for t in range(own):
+                    values = gather([results[c, k, t, b] for b in range(blocks)])
+                    for b, value in enumerate(values):
+                        where = (c, slot + k - BEFORE, rows_at(b), pl.ds(t * LANES, LANES))
+                        dual_out[where] = value * COURANT
+
+    def count(low, high):
+        return -(-(depth + max(low, high)) // UNROLL) * UNROLL
+
+    magnetic(dual_e, dual_g, count(2, 2))
+    electric(dual_e, dual_g, second_e, count(1, 2))
+    magnetic(second_e, dual_g, count(1, 1))
+    electric(second_e, dual_g, third_e, count(0, 1))
+    magnetic(third_e, dual_g, depth, emit_dual)
 
     none = jnp.zeros((TILE, LANES), jnp.int32)
     limits = []
     for t in range(own):
-        part = lane_tile(height[...], t)
-        limits += spread([part[b * TILE:(b + 1) * TILE] for b in range(blocks - 1)], none)
+        limits += spread(row_tiles(lane_tile(height[...], t)), none)
     totals = (zero,) * (own * blocks)
-    magnetic(forward, FH, -3, 2)
-    totals = electric(forward, FH, forward, -2, 2, third, totals)
-    magnetic(forward, FH, -2, 1)
-    totals = electric(forward, FH, forward, -1, 1, second, totals)
-    magnetic(forward, FH, -1, 0)
-    totals = electric(forward, FH, forward, 0, 0, first, totals)
+    magnetic(forward_e, forward_g, count(3, 2))
+    totals = electric(forward_e, forward_g, forward_e, count(2, 2), third_e, totals)
+    magnetic(forward_e, forward_g, count(2, 1))
+    totals = electric(forward_e, forward_g, forward_e, count(1, 1), second_e, totals)
+    magnetic(forward_e, forward_g, count(1, 0))
+    totals = electric(forward_e, forward_g, forward_e, depth, dual_e, totals)
     for t in range(own):
         values = gather(list(totals[t * blocks:(t + 1) * blocks]))
         for b, value in enumerate(values):
@@ -516,7 +531,7 @@
 
     blocks = rows // TILE + 1
     planes = depth + 2 * WIDE
-    block = (planes, tiles + 1, blocks * TILE, LANES)
+    block = (BEFORE + depth + AFTER, tiles + 1, blocks * TILE, LANES)
     grad, dual = pl.pallas_call(
         window_kernel,
         out_shape=[
@@ -526,8 +541,8 @@
         in_specs=[smem, smem] + [vmem] * 14,
         out_specs=[vmem] * 2,
         scratch_shapes=[
-            pltpu.VMEM((COUNT,) + block, F32),
-            pltpu.VMEM((6,) + block, F32),
+            *[pltpu.VMEM((3,) + block, F32)] * 6,
+            pltpu.VMEM((1,) + block, F32),
             pltpu.VMEM((planes, blocks * TILE, LANES), F32),
         ],
         compiler_params=params,

time: 103 us -> 81.7 us (0.79)
  Pallas kernels: 63.7 us -> 42.3 us
    pallas_call x1, Pallas kernels: 51.7 us -> 30.3 us  [local(): pl.pallas_call(window_kernel, out_shape=[jax.ShapeDtypeStruct((rows, cols...]
where the time goes in v2:
time: 81.7 us; the launch traced here: 81 us
  Pallas kernels  42.3 us (52%)
  waiting for transfers between devices  16.2 us (20%)
  starting transfers between devices  14.3 us (18%)
  local copies, waits for them, and re-layouts  4.15 us (5%)
  other arithmetic  3.32 us (4%)
    pallas_call x1, Pallas kernels, local(): pl.pallas_call(window_kernel, out_shape=[jax.ShapeDtypeStruct((rows, cols...  30.3 us
    ppermute x8, waiting for transfers between devices, swap(): return lax.ppermute(array, axis, swap_pairs(lax.axis_size(axis), offset))  16.2 us
    ppermute x8, starting transfers between devices, swap(): return lax.ppermute(array, axis, swap_pairs(lax.axis_size(axis), offset))  14.3 us
    pallas_call x1, Pallas kernels, local(): pl.pallas_call(functools.partial(pack_kernel, x_messages), out_shape=[jax...  9.38 us
    unnamed x18, local copies, waits for them, and re-layouts  3.5 us
    pallas_call x1, Pallas kernels, local(): pl.pallas_call(corner_kernel, out_shape=[corner_shape, corner_shape], in_...  2.62 us
  transfers between devices with their start and end apart: 8, of which 4 were waited for; matrix products, arithmetic and copies ran while one was open for 1% of the time, Pallas kernels for 3%

profile of v2, /device:TPU:1, one launch (start us, length us, event | category | flops | bytes accessed | tf_op | source)
XLA Modules:
  0.0 81.0 jit_solution(13765422855519844864)
XLA Ops:
  0.7 1.4 %broadcast_select_fusion.picker = bf16[64,208]{1,0:T(8,128)(2,1)} fusion(bf16[64,208]{1,0:T(8,128)(2,1)} %constant.54.clone, bf16[64,208]{1,0:T(8,128)(2,1)} %constant.55.clone, pred[]{:T(512)S(6)} %eq.22), kind=kLoop, calls=%fused_computation | loop fusion | flops 13312 | bytes 79873 | tf_op jit(solution)/shard_map/jit(_where)/select_n | solution.py:492
  2.1 0.7 stack.35.flags
  2.7 9.4 %pack.1 = (f32[32,16,128]{2,1,0:T(8,128)}, f32[32,16,256]{2,1,0:T(8,128)}, f32[32,32,256]{2,1,0:T(8,128)}, f32[32,32,256]{2,1,0:T(8,128)}) custom-call(s32[8]{0:T(128)} %stack.35.flags, bf16[3,32,16,256]{3,2,1,0:T(8,128)(2,1)} %fe.3, bf16[3,32,16,256]{3,2,1,0:T(8,128)(2,1)} %fh.3, bf16[3,32,16,256]{3,2,1,0:T(8,128)(2,1)} %ae.3, bf16[3,32,16,256]{3,2,1,0:T(8,128)(2,1)} %ah.3, ...), custom_call_target="tpu_custom_call" | custom-call | tf_op jit(solution)/shard_map/pack/pallas_call | solution.py:501
  12.1 0.1 collective-permute-start.3
  12.2 4.5 %collective-permute-start.4 = (f32[32,32,256]{2,1,0:T(8,128)}, f32[32,32,256]{2,1,0:T(8,128)S(1)}, u32[]{:S(2)}, u32[]{:S(2)}) collective-permute-start(f32[32,32,256]{2,1,0:T(8,128)} %get-tuple-element.13), channel_id=1, source_target_pairs={{2,4},{4,2},{6,8},{8,6},{10,12},{12,10},{3,5},{5,3},{7,9},{9,7},{1... | collective-permute-start | bytes 3145736 | tf_op jit(solution)/shard_map/ppermute | solution.py:46
  16.7 1.3 %collective-permute-start.2 = (f32[32,16,256]{2,1,0:T(8,128)}, f32[32,16,256]{2,1,0:T(8,128)S(1)}, u32[]{:S(2)}, u32[]{:S(2)}) collective-permute-start(f32[32,16,256]{2,1,0:T(8,128)} %get-tuple-element.11), channel_id=1, source_target_pairs={{0,1},{1,0},{2,3},{3,2},{4,5},{5,4},{6,7},{7,6},{8,9},{9,8},{10,11... | collective-permute-start | bytes 1572872 | tf_op jit(solution)/shard_map/ppermute | solution.py:46
  18.0 1.2 %collective-permute-start = (f32[32,16,128]{2,1,0:T(8,128)}, f32[32,16,128]{2,1,0:T(8,128)S(1)}, u32[]{:S(2)}, u32[]{:S(2)}) collective-permute-start(f32[32,16,128]{2,1,0:T(8,128)} %get-tuple-element.10), channel_id=1, source_target_pairs={{0,16},{16,0},{1,17},{17,1},{2,18},{18,2},{3,19},{19,3},{4,20},{20... | collective-permute-start | bytes 786440 | tf_op jit(solution)/shard_map/ppermute | solution.py:46
  19.2 5.7 %collective-permute-done.xp = f32[32,16,128]{2,1,0:T(8,128)S(1)} collective-permute-done((f32[32,16,128]{2,1,0:T(8,128)}, f32[32,16,128]{2,1,0:T(8,128)S(1)}, u32[]{:S(2)}, u32[]{:S(2)}) %collective-permute-start) | collective-permute-done | bytes 262176 | tf_op jit(solution)/shard_map/ppermute | solution.py:46
  24.9 0.0 collective-permute-start.1
  24.9 3.8 %collective-permute-done.1.xz = f32[3,16,128]{2,1,0:T(8,128)S(1)} collective-permute-done((f32[3,16,128]{2,1,0:T(8,128)S(1)}, f32[3,16,128]{2,1,0:T(8,128)S(1)}, u32[]{:S(2)}, u32[]{:S(2)}) %collective-permute-start.1) | collective-permute-done | bytes 24608 | tf_op jit(solution)/shard_map/ppermute | solution.py:46
  28.8 0.0 collective-permute-done.2.zr
  28.8 0.6 copy-done.6
  29.4 0.8 copy-done
  30.2 2.6 %corners.1 = (f32[102,8,128]{2,1,0:T(8,128)}, f32[102,8,128]{2,1,0:T(8,128)}) custom-call(s32[8]{0:T(128)} %stack.35.flags, f32[32,16,128]{2,1,0:T(8,128)} %copy-done.1, f32[3,16,128]{2,1,0:T(8,128)} %copy-done.6, f32[32,16,256]{2,1,0:T(8,128)} %copy-done), custom_call_target="tpu_custom_call" | custom-call | tf_op jit(solution)/shard_map/corners/pallas_call | solution.py:521
  32.8 5.5 %collective-permute-start.6 = (f32[102,8,128]{2,1,0:T(8,128)}, f32[102,8,128]{2,1,0:T(8,128)S(1)}, u32[]{:S(2)}, u32[]{:S(2)}) collective-permute-start(f32[102,8,128]{2,1,0:T(8,128)} %get-tuple-element.15), channel_id=1, source_target_pairs={{2,4},{4,2},{6,8},{8,6},{10,12},{12,10},{3,5},{5,3},{7,9},{9,7},{1... | collective-permute-start | bytes 1253384 | tf_op jit(solution)/shard_map/ppermute | solution.py:46
  38.3 0.6 broadcast_select_fusion.1.placer
  38.9 5.3 %collective-permute-done.6.corner_b = f32[102,8,128]{2,1,0:T(8,128)S(1)} collective-permute-done((f32[102,8,128]{2,1,0:T(8,128)}, f32[102,8,128]{2,1,0:T(8,128)S(1)}, u32[]{:S(2)}, u32[]{:S(2)}) %collective-permute-start.6) | collective-permute-done | bytes 417824 | tf_op jit(solution)/shard_map/ppermute | solution.py:46
  44.2 0.7 copy-done.5
  45.0 0.4 copy-done.2
  45.4 1.0 %copy-done.3 = f32[32,32,256]{2,1,0:T(8,128)} copy-done((f32[32,32,256]{2,1,0:T(8,128)}, f32[32,32,256]{2,1,0:T(8,128)S(1)}, u32[]{:S(2)}) %copy-start.3) | copy-done | bytes 1048600
  46.3 30.3 %window.1 = (f32[16,256]{1,0:T(8,128)}, f32[3,32,16,256]{3,2,1,0:T(8,128)}) custom-call(s32[8]{0:T(128)} %stack.35.flags, f32[4]{0:T(128)} %inverse.1, bf16[3,32,16,256]{3,2,1,0:T(8,128)(2,1)} %fe.3, bf16[3,32,16,256]{3,2,1,0:T(8,128)(2,1)} %fh.3, bf16[3,32,16,256]{3,2,1,0:T(8,128)(2,1)} %ae.3, bf16[3,32,16,256]{3,2,1,0:T(8,128)(2,1)} %ah.3, ...), custom_call_target="tpu_custom_call" | custom-call | tf_op jit(solution)/shard_map/window/pallas_call | solution.py:535
  76.6 1.7 %collective-permute-start.7 = (f32[16,256]{1,0:T(8,128)}, f32[16,256]{1,0:T(8,128)S(1)}, u32[]{:S(2)}, u32[]{:S(2)}) collective-permute-start(f32[16,256]{1,0:T(8,128)} %get-tuple-element.16), channel_id=1, source_target_pairs={{0,1},{1,0},{2,3},{3,2},{4,5},{5,4},{6,7},{7,6},{8,9},{9,8},{10,11... | collective-permute-start | bytes 49160 | tf_op jit(solution)/shard_map/ppermute | solution.py:46
  78.3 1.3 %collective-permute-done.7 = f32[16,256]{1,0:T(8,128)S(1)} collective-permute-done((f32[16,256]{1,0:T(8,128)}, f32[16,256]{1,0:T(8,128)S(1)}, u32[]{:S(2)}, u32[]{:S(2)}) %collective-permute-start.7) | collective-permute-done | bytes 16416 | tf_op jit(solution)/shard_map/ppermute | solution.py:46
  79.6 1.3 %add.20 = f32[16,256]{1,0:T(8,128)} add(f32[16,256]{1,0:T(8,128)} %get-tuple-element.16, f32[16,256]{1,0:T(8,128)S(1)} %collective-permute-done.7) | non-fusion elementwise | flops 4096 | bytes 49152 | tf_op jit(solution)/shard_map/add | solution.py:554
  (18 shorter events, 0.0 us)
Async XLA Ops:
  2.7 35.6 %copy-start.7 = (bf16[104,64]{1,0:T(8,128)(2,1)S(1)}, bf16[104,64]{1,0:T(8,128)(2,1)}, u32[]{:S(2)}) copy-start(bf16[104,64]{1,0:T(8,128)(2,1)} %constant.57.clone) | copy-start | bytes 39940
  2.7 35.6 %copy-start.8 = (bf16[104,64]{1,0:T(8,128)(2,1)S(1)}, bf16[104,64]{1,0:T(8,128)(2,1)}, u32[]{:S(2)}) copy-start(bf16[104,64]{1,0:T(8,128)(2,1)} %constant.56.clone) | copy-start | bytes 39940
  12.1 32.1 %collective-permute-start.3 = (f32[32,32,256]{2,1,0:T(8,128)}, f32[32,32,256]{2,1,0:T(8,128)S(1)}, u32[]{:S(2)}, u32[]{:S(2)}) collective-permute-start(f32[32,32,256]{2,1,0:T(8,128)} %get-tuple-element.12), channel_id=1, source_target_pairs={{0,2},{2,0},{4,6},{6,4},{8,10},{10,8},{12,14},{14,12},{1,3},{3,1},... | collective-permute-start | bytes 3145736 | tf_op jit(solution)/shard_map/ppermute | solution.py:46
  12.2 32.1 %collective-permute-start.4 = (f32[32,32,256]{2,1,0:T(8,128)}, f32[32,32,256]{2,1,0:T(8,128)S(1)}, u32[]{:S(2)}, u32[]{:S(2)}) collective-permute-start(f32[32,32,256]{2,1,0:T(8,128)} %get-tuple-element.13), channel_id=1, source_target_pairs={{2,4},{4,2},{6,8},{8,6},{10,12},{12,10},{3,5},{5,3},{7,9},{9,7},{1... | collective-permute-start | bytes 3145736 | tf_op jit(solution)/shard_map/ppermute | solution.py:46
  16.7 12.1 %collective-permute-start.2 = (f32[32,16,256]{2,1,0:T(8,128)}, f32[32,16,256]{2,1,0:T(8,128)S(1)}, u32[]{:S(2)}, u32[]{:S(2)}) collective-permute-start(f32[32,16,256]{2,1,0:T(8,128)} %get-tuple-element.11), channel_id=1, source_target_pairs={{0,1},{1,0},{2,3},{3,2},{4,5},{5,4},{6,7},{7,6},{8,9},{9,8},{10,11... | collective-permute-start | bytes 1572872 | tf_op jit(solution)/shard_map/ppermute | solution.py:46
  18.0 6.9 %collective-permute-start = (f32[32,16,128]{2,1,0:T(8,128)}, f32[32,16,128]{2,1,0:T(8,128)S(1)}, u32[]{:S(2)}, u32[]{:S(2)}) collective-permute-start(f32[32,16,128]{2,1,0:T(8,128)} %get-tuple-element.10), channel_id=1, source_target_pairs={{0,16},{16,0},{1,17},{17,1},{2,18},{18,2},{3,19},{19,3},{4,20},{20... | collective-permute-start | bytes 786440 | tf_op jit(solution)/shard_map/ppermute | solution.py:46
  24.9 3.8 %copy-start.1 = (f32[32,16,128]{2,1,0:T(8,128)}, f32[32,16,128]{2,1,0:T(8,128)S(1)}, u32[]{:S(2)}) copy-start(f32[32,16,128]{2,1,0:T(8,128)S(1)} %collective-permute-done.xp) | copy-start | bytes 786436
  24.9 3.8 %collective-permute-start.1 = (f32[3,16,128]{2,1,0:T(8,128)S(1)}, f32[3,16,128]{2,1,0:T(8,128)S(1)}, u32[]{:S(2)}, u32[]{:S(2)}) collective-permute-start(f32[3,16,128]{2,1,0:T(8,128)S(1)} %constant_dynamic-slice_fusion), channel_id=1, source_target_pairs={{0,1},{1,0},{2,3},{3,2},{4,5},{5,4},{6,7},{7,6},{8,9},{9,8},{10,11... | collective-permute-start | bytes 73736 | tf_op jit(solution)/shard_map/ppermute | solution.py:46
  28.8 0.6 copy-start.6
  29.4 0.8 copy-start
  32.8 6.2 %collective-permute-start.5 = (f32[102,8,128]{2,1,0:T(8,128)}, f32[102,8,128]{2,1,0:T(8,128)S(1)}, u32[]{:S(2)}, u32[]{:S(2)}) collective-permute-start(f32[102,8,128]{2,1,0:T(8,128)} %get-tuple-element.14), channel_id=1, source_target_pairs={{0,2},{2,0},{4,6},{6,4},{8,10},{10,8},{12,14},{14,12},{1,3},{3,1},... | collective-permute-start | bytes 1253384 | tf_op jit(solution)/shard_map/ppermute | solution.py:46
  32.8 11.4 %collective-permute-start.6 = (f32[102,8,128]{2,1,0:T(8,128)}, f32[102,8,128]{2,1,0:T(8,128)S(1)}, u32[]{:S(2)}, u32[]{:S(2)}) collective-permute-start(f32[102,8,128]{2,1,0:T(8,128)} %get-tuple-element.15), channel_id=1, source_target_pairs={{2,4},{4,2},{6,8},{8,6},{10,12},{12,10},{3,5},{5,3},{7,9},{9,7},{1... | collective-permute-start | bytes 1253384 | tf_op jit(solution)/shard_map/ppermute | solution.py:46
  38.9 5.3 %copy-start.4 = (f32[102,8,128]{2,1,0:T(8,128)}, f32[102,8,128]{2,1,0:T(8,128)S(1)}, u32[]{:S(2)}) copy-start(f32[102,8,128]{2,1,0:T(8,128)S(1)} %collective-permute-done.5.corner_a) | copy-start | bytes 1253380
  44.2 0.8 copy-start.5
  44.2 1.1 %copy-start.2 = (f32[32,32,256]{2,1,0:T(8,128)}, f32[32,32,256]{2,1,0:T(8,128)S(1)}, u32[]{:S(2)}) copy-start(f32[32,32,256]{2,1,0:T(8,128)S(1)} %collective-permute-done.3.ya) | copy-start | bytes 3145732
  45.4 1.0 %copy-start.3 = (f32[32,32,256]{2,1,0:T(8,128)}, f32[32,32,256]{2,1,0:T(8,128)S(1)}, u32[]{:S(2)}) copy-start(f32[32,32,256]{2,1,0:T(8,128)S(1)} %collective-permute-done.4.yb) | copy-start | bytes 3145732
  76.6 3.0 %collective-permute-start.7 = (f32[16,256]{1,0:T(8,128)}, f32[16,256]{1,0:T(8,128)S(1)}, u32[]{:S(2)}, u32[]{:S(2)}) collective-permute-start(f32[16,256]{1,0:T(8,128)} %get-tuple-element.16), channel_id=1, source_target_pairs={{0,1},{1,0},{2,3},{3,2},{4,5},{5,4},{6,7},{7,6},{8,9},{9,8},{10,11... | collective-permute-start | bytes 49160 | tf_op jit(solution)/shard_map/ppermute | solution.py:46

commit v3 on v2

--- a/solution.py
+++ b/solution.py
@@ -13,9 +13,9 @@
 LANES = 128
 TILE = 8
 WIDE = 3
-BEFORE = 4
+BEFORE = 5
 AFTER = 5
-UNROLL = 2
+UNROLL = 4
 SHIFT = 4
 COUNT = 13
 FE, FH, AE, AH, KAPPA = 0, 3, 6, 9, 12
@@ -46,28 +46,63 @@
     return lax.ppermute(array, axis, swap_pairs(lax.axis_size(axis), offset))
 
 
+def two_ways(rows_in, to_next, to_previous):
+    first, second = np.zeros((2, len(to_next), rows_in), np.float32)
+    for n, index in enumerate(to_next):
+        first[n, index] = 1
+    for n, index in enumerate(to_previous):
+        second[n, index] = 1
+    return np.stack([np.concatenate([first, second]), np.concatenate([second, first])])
+
+
 def row_picker(rows):
-    to_next = np.zeros((LAYERS, COUNT * rows), np.float32)
-    to_previous = np.zeros((LAYERS, COUNT * rows), np.float32)
-    for n, (c, own, _) in enumerate(layers_to_next(rows)):
-        to_next[n, c * rows + own] = 1
-    for n, (c, own, _) in enumerate(layers_to_previous(rows)):
-        to_previous[n, c * rows + own] = 1
-    even = np.concatenate([to_next, to_previous])
-    odd = np.concatenate([to_previous, to_next])
-    return even, odd
+    return two_ways(
+        COUNT * rows,
+        [c * rows + own for c, own, _ in layers_to_next(rows)],
+        [c * rows + own for c, own, _ in layers_to_previous(rows)],
+    )
+
+
+def corner_picker(rows):
+    return two_ways(
+        LAYERS * rows,
+        [n * rows + rows - WIDE + k for n in range(LAYERS) for k in range(WIDE)],
+        [n * rows + k for n in range(LAYERS) for k in range(WIDE)],
+    )
+
+
+def ways_back(rows_out, low, high):
+    first = np.zeros((rows_out, len(low)), np.float32)
+    second = np.zeros((rows_out, len(high)), np.float32)
+    for n, (index, value) in enumerate(low):
+        first[index, n] = value
+    for n, (index, value) in enumerate(high):
+        second[index, n] = value
+    return np.stack([np.concatenate([second, first], 1), np.concatenate([first, second], 1)])
 
 
 def row_placer(rows):
-    low = np.zeros((COUNT * TILE, LAYERS), np.float32)
-    high = np.zeros((COUNT * TILE, LAYERS), np.float32)
-    for n, (c, _, there) in enumerate(layers_to_next(rows)):
-        low[c * TILE + there + SHIFT, n] = SCALE[c]
-    for n, (c, _, there) in enumerate(layers_to_previous(rows)):
-        high[c * TILE + there - rows + SHIFT, n] = SCALE[c]
-    even = np.concatenate([high, low], axis=1)
-    odd = np.concatenate([low, high], axis=1)
-    return even, odd
+    low = [(c * TILE + there + SHIFT, SCALE[c]) for c, _, there in layers_to_next(rows)]
+    high = [(c * TILE + there - rows + SHIFT, SCALE[c]) for c, _, there in layers_to_previous(rows)]
+    return ways_back(COUNT * TILE, low, high)
+
+
+def corner_placer():
+    low = [(n * TILE + SHIFT - WIDE + k, 1) for n in range(LAYERS) for k in range(WIDE)]
+    high = [(n * TILE + SHIFT + k, 1) for n in range(LAYERS) for k in range(WIDE)]
+    return ways_back(LAYERS * TILE, low, high)
+
+
+def column_table(depth):
+    groups = depth // TILE
+    assert groups * LAYERS <= LANES
+    table = np.full((2, TILE, LANES), -1, np.int32)
+    for way, layers in enumerate((layers_to_next(LANES), layers_to_previous(0))):
+        for g in range(groups):
+            for n, (c, own, there) in enumerate(layers):
+                lane = g * LAYERS + n
+                table[way, :4, lane] = c, own, there % LANES, g
+    return table
 
 
 def lane_of(shape):
@@ -85,98 +120,98 @@
     return (fe, fh, ae, ah)[c // 3][c % 3, z]
 
 
-def pack_kernel(x_messages, flags, fe, fh, ae, ah, material, picker, *outs):
-    depth, rows, cols = material.shape
+def place_on(axis):
+    return lax.axis_index(axis), lax.rem(lax.axis_index(axis), 2)
+
+
+def pack_kernel(x_messages, fe, fh, ae, ah, material, picker, table, *outs):
+    chunk, rows, cols = material.shape
     refs = (fe, fh, ae, ah, material)
     x_out = outs[:x_messages]
     z_out, ya_out, yb_out = outs[x_messages:]
-    chunk = 8
-    odd_x, odd_z = flags[0], flags[1]
-
-    for number in range(x_messages):
-        first = jnp.where(odd_x == number, 1, 0)
-        offset = pl.multiple_of(first * (cols - LANES), LANES)
-        row = row_of((LANES, LANES))
-        lane = lane_of((LANES, LANES))
-        spot = lane % TILE
-        top = jnp.where(spot >= TILE - WIDE, LANES - TILE + spot, -1)
-        bottom = jnp.where(spot < WIDE, spot, -1)
-        picked = row == jnp.where(first == 1, top, bottom)
-        pickers = [
-            jnp.where(picked & (lane // TILE == c), 1.0, 0.0).astype(BF16) for c in range(COUNT)
-        ]
-
-        def columns(step, _):
-            start = step * chunk
-            total = jnp.zeros((chunk * rows, LANES), F32)
-            for c in range(COUNT):
-                if c == KAPPA:
-                    part = material[pl.ds(start, chunk), :, pl.ds(offset, LANES)]
-                    part = (part + 1).astype(F32).astype(BF16)
-                else:
-                    part = (fe, fh, ae, ah)[c // 3][
-                        c % 3, pl.ds(start, chunk), :, pl.ds(offset, LANES)
-                    ]
-                total += jnp.dot(
-                    part.reshape(chunk * rows, LANES), pickers[c], preferred_element_type=F32
-                )
-            x_out[number][pl.ds(start, chunk)] = total.reshape(chunk, rows, LANES)
-            return 0
-
-        lax.fori_loop(0, depth // chunk, columns, 0)
-
-    @pl.when(odd_z == 0)
+    odd_x, odd_y, odd_z = (place_on(axis)[1] for axis in ("gx", "gy", "gz"))
+    step = pl.program_id(0)
+
+    picked = [
+        jnp.dot(
+            picker[odd_y],
+            jnp.concatenate([own_field(refs, c, z) for c in range(COUNT)], axis=0),
+            preferred_element_type=F32,
+        )
+        for z in range(chunk)
+    ]
+    for z in range(chunk):
+        ya_out[z] = picked[z][:LAYERS]
+        yb_out[z] = picked[z][LAYERS:]
+
+    for number, out in enumerate(x_out):
+        way = odd_x ^ number
+        offset = pl.multiple_of((1 - way) * (cols - LANES), LANES)
+        total = jnp.zeros((chunk * rows, LANES), F32)
+        of_field, of_lane, of_group = (table[way, k:k + 1, :] for k in (0, 1, 3))
+        chosen = (row_of((LANES, LANES)) == of_lane) & (of_group == step)
+        for c in range(COUNT):
+            if c == KAPPA:
+                part = material[:, :, pl.ds(offset, LANES)]
+                part = (part + 1).astype(F32).astype(BF16)
+            else:
+                part = (fe, fh, ae, ah)[c // 3][c % 3, :, :, pl.ds(offset, LANES)]
+            matrix = jnp.where(chosen & (of_field == c), 1.0, 0.0).astype(BF16)
+            total += jnp.dot(
+                part.reshape(chunk * rows, LANES), matrix, preferred_element_type=F32
+            )
+        total = total.reshape(chunk, rows, LANES)
+
+        @pl.when(step == 0)
+        def _():
+            out[...] = total
+
+        @pl.when(step > 0)
+        def _():
+            out[...] += total
+
+    depth = chunk * pl.num_programs(0)
+
+    @pl.when((odd_z == 0) & (step == pl.num_programs(0) - 1))
     def _():
-        for n, (c, own, _) in enumerate(layers_to_next(depth)):
+        for n, (c, own, _) in enumerate(layers_to_next(chunk)):
             z_out[n] = own_field(refs, c, own).astype(F32)
 
-    @pl.when(odd_z == 1)
+    @pl.when((odd_z == 1) & (step == 0))
     def _():
-        for n, (c, own, _) in enumerate(layers_to_previous(depth)):
+        for n, (c, own, _) in enumerate(layers_to_previous(chunk)):
             z_out[n] = own_field(refs, c, own).astype(F32)
 
-    def plane(z, _):
-        stacked = jnp.concatenate([own_field(refs, c, z) for c in range(COUNT)], axis=0)
-        picked = jnp.dot(picker[...], stacked, preferred_element_type=F32)
-        ya_out[z] = picked[:LAYERS]
-        yb_out[z] = picked[LAYERS:]
-        return 0
-
-    lax.fori_loop(0, depth, plane, 0)
-
-
-def edge_rows(array, odd, message):
+
+def edge_rows(array, to_next):
     rows = array.shape[0]
     row = row_of((TILE, LANES))
-    last = pltpu.roll(array[rows - TILE:], 4, 0)
-    first = pltpu.roll(array[:TILE], 4, 0)
-    last = jnp.where((row >= 1) & (row < 4), last, 0.0)
-    first = jnp.where((row >= 4) & (row < 7), first, 0.0)
-    return jnp.where(odd == message, last, first)
-
-
-def corner_kernel(flags, xp, xz, zr, a_out, b_out):
-    depth, rows, _ = xp.shape
-    cols = zr.shape[2]
-    tiles = cols // LANES
-    odd_y, odd_z = flags[2], flags[1]
-    base = LAYERS * tiles
+    last = pltpu.roll(array[rows - TILE:], SHIFT, 0)
+    first = pltpu.roll(array[:TILE], SHIFT, 0)
+    last = jnp.where((row >= SHIFT - WIDE) & (row < SHIFT), last, 0.0)
+    first = jnp.where((row >= SHIFT) & (row < SHIFT + WIDE), first, 0.0)
+    return jnp.where(to_next == 1, last, first)
+
+
+def corner_kernel(x_messages, *refs):
+    xp, xz = refs[:x_messages], refs[x_messages:2 * x_messages]
+    zr, picker, a_out, b_out = refs[2 * x_messages:]
+    _, rows, cols = zr.shape
+    odd_y = place_on("gy")[1]
+    arrived = zr[...].reshape(LAYERS * rows, cols).astype(BF16)
+    picked = jnp.dot(picker[odd_y], arrived, preferred_element_type=F32)
+    count = LAYERS * WIDE
     for message, out in ((0, a_out), (1, b_out)):
-        for n in range(LAYERS):
-            for t in range(tiles):
-                out[n * tiles + t] = edge_rows(
-                    zr[n, :, t * LANES:(t + 1) * LANES], odd_y, message
-                )
-
-        def plane(z, _):
-            out[base + WIDE + z] = edge_rows(xp[z], odd_y, message)
-            return 0
-
-        lax.fori_loop(0, depth, plane, 0)
-        there = jnp.where(odd_z == 1, 0, depth + WIDE)
-        for k in range(WIDE):
-            out[base + there + k] = edge_rows(xz[k], odd_y, message)
-            out[base + depth + WIDE - there + k] = jnp.zeros((TILE, LANES), F32)
+        at = 0
+        for t in range(cols // LANES):
+            for n in range(0, count, TILE):
+                begin = message * count + n
+                out[at] = picked[begin:begin + TILE, t * LANES:(t + 1) * LANES]
+                at += 1
+        for array in (*xp, *xz):
+            for k in range(array.shape[0]):
+                out[at + k] = edge_rows(array[k], 1 - (odd_y ^ message))
+            at += array.shape[0]
 
 
 def spread(tiles, halo):
@@ -195,19 +230,17 @@
     return [jnp.where(low, before, after) for before, after in zip(turned, turned[1:])]
 
 
-def window_kernel(
-    flags, inverse, fe, fh, ae, ah, material, height, xp, xz, zr, ya, yb, corner_a, corner_b,
-    placer, grad_out, dual_out, forward_e, forward_g, dual_e, dual_g, second_e, third_e, factor,
-    wide_x,
-):
+def window_kernel(x_messages, inverse, fe, fh, ae, ah, material, height, *others):
+    xp, xz = others[:x_messages], others[x_messages:2 * x_messages]
+    (zr, ya, yb, corner_a, corner_b, placer, corner_placing, table, grad_out, dual_out, forward_e,
+     forward_g, dual_e, dual_g, second_e, third_e, factor) = others[2 * x_messages:]
     depth, rows, cols = material.shape
     own = cols // LANES
     tiles = own + 1
     blocks = rows // TILE + 1
-    planes = depth + 2 * WIDE
     refs = (fe, fh, ae, ah, material)
-    odd_z = flags[1]
-    start_z = flags[7]
+    (at_x, odd_x), (at_y, odd_y), (at_z, odd_z) = (place_on(axis) for axis in ("gx", "gy", "gz"))
+    start_z = at_z * depth
     row = row_of((TILE, LANES))
     lane = lane_of((TILE, LANES))
     zero = jnp.zeros((TILE, LANES), F32)
@@ -241,42 +274,39 @@
                 for ref in (forward_e, dual_e, second_e, third_e):
                     ref[c, depth + BEFORE, t, rows_at(b)] = zero
 
-    base = LAYERS * own
-
-    def put_wide(slot, own_rows):
-        halo = corner_a[base + slot] + corner_b[base + slot]
-        return slot, spread(row_tiles(own_rows), halo)
-
-    def store_wide(items):
-        for slot, parts in items:
-            for b, part in enumerate(parts):
-                wide_x[slot, rows_at(b)] = part
-
-    def wide_planes(step, _):
-        store_wide([put_wide(step * 8 + k + WIDE, xp[step * 8 + k]) for k in range(8)])
-        return 0
-
-    lax.fori_loop(0, depth // 8, wide_planes, 0)
-    there = jnp.where(odd_z == 1, 0, depth + WIDE)
-    items = []
-    for k in range(WIDE):
-        items.append(put_wide(there + k, xz[k]))
-        items.append(put_wide(depth + WIDE - there + k, jnp.zeros((rows, LANES), F32)))
-    store_wide(items)
-
-    source = row_of((LANES, LANES))
-    spot = source % TILE
-    lands = jnp.where(spot < TILE // 2, spot, LANES - TILE + spot) == lane_of((LANES, LANES))
-    wide = wide_x[...].reshape(planes * blocks * TILE, LANES).astype(BF16)
-    pairs = [(c, c + 1) if c + 1 < COUNT else (c,) for c in range(0, COUNT, 2)]
-    for pair in pairs:
-        matrix = [jnp.where(lands & (source // TILE == c), SCALE[c], 0.0).astype(BF16) for c in pair]
-        matrix = jnp.concatenate(matrix, axis=1) if len(pair) > 1 else matrix[0]
-        result = jnp.dot(wide, matrix, preferred_element_type=F32)
-        for n, c in enumerate(pair):
-            ref, at = target(c)
-            value = lane_tile(result, n).reshape(planes, blocks * TILE, LANES)
-            ref[at, pl.ds(BEFORE - WIDE, planes), own] = weight(value) if c == KAPPA else value
+    corner_tiles = LAYERS * WIDE // TILE
+    at = own * corner_tiles
+    groups = depth // TILE
+    begin_halo = jnp.where(odd_z == 1, BEFORE - WIDE, BEFORE + depth)
+    halo_group = jnp.where(odd_z == 1, groups - 1, 0)
+    wides = []
+    for array in (*xp, *xz):
+        blocks_in = []
+        for k in range(array.shape[0]):
+            blocks_in += spread(row_tiles(array[k]), corner_a[at + k] + corner_b[at + k])
+        at += array.shape[0]
+        wides.append(jnp.concatenate(blocks_in, axis=0).astype(BF16))
+
+    def columns_of(c, group, arrays):
+        total = None
+        for number, array in enumerate(arrays):
+            way = 1 - (odd_x ^ number)
+            of_field, of_target, of_group = (table[way, k:k + 1, :] for k in (0, 2, 3))
+            chosen = (of_field == c) & (of_group == group) & (of_target == row_of((LANES, LANES)))
+            matrix = jnp.where(chosen, SCALE[c], 0.0).astype(BF16)
+            part = lax.dot_general(
+                array, matrix, (((1,), (1,)), ((), ())), preferred_element_type=F32
+            )
+            total = part if total is None else total + part
+        total = total.reshape(-1, blocks * TILE, LANES)
+        return weight(total) if c == KAPPA else total
+
+    for c in range(COUNT):
+        ref, to = target(c)
+        for group in range(groups):
+            found = columns_of(c, group, wides[:x_messages])
+            ref[to, pl.ds(BEFORE + group * TILE, TILE), own] = found
+        ref[to, pl.ds(begin_halo, WIDE), own] = columns_of(c, halo_group, wides[x_messages:])
 
     def store(items):
         for c, slot, t, parts in items:
@@ -292,11 +322,17 @@
             own_tiles = [p * SCALE[c] for p in own_tiles]
         return spread(own_tiles, halo)
 
+    arrived = jnp.concatenate([
+        jnp.concatenate([ref[t * corner_tiles + k] for t in range(own)], axis=1)
+        for ref in (corner_a, corner_b) for k in range(corner_tiles)
+    ], axis=0).astype(BF16)
+    plane_halos = jnp.dot(corner_placing[odd_y], arrived, preferred_element_type=F32)
+
     def halo_planes(layers):
         for n, (c, _, position) in enumerate(layers):
             items = []
             for t in range(own):
-                halo = (corner_a[n * own + t] + corner_b[n * own + t]) * SCALE[c]
+                halo = lane_tile(plane_halos[n * TILE:(n + 1) * TILE], t) * SCALE[c]
                 parts = arrange(c, row_tiles(lane_tile(zr[n], t)), halo)
                 items.append((c, position + BEFORE, t, parts))
             store(items)
@@ -314,7 +350,7 @@
         for k in range(2):
             z = step * 2 + k
             arrived = jnp.concatenate([ya[z], yb[z]], axis=0).astype(BF16)
-            halos = jnp.dot(placer[...], arrived, preferred_element_type=F32)
+            halos = jnp.dot(placer[odd_y], arrived, preferred_element_type=F32)
             for c in range(COUNT):
                 whole = own_field(refs, c, z).astype(F32)
                 for t in range(own):
@@ -326,8 +362,8 @@
 
     lax.fori_loop(0, depth // 2, own_planes, 0)
 
-    keep_row = jnp.where((row < SHIFT) & (flags[3] == 1), 0.0, 1.0)
-    keep_lane = jnp.where((lane >= LANES // 2) & (flags[4] == 1), 0.0, 1.0)
+    keep_row = jnp.where((row < SHIFT) & (at_y == 0), 0.0, 1.0)
+    keep_lane = jnp.where((lane >= LANES // 2) & (at_x == 0), 0.0, 1.0)
 
     def mask(value, t, b):
         if b == 0:
@@ -479,77 +515,74 @@
 def local(forward_e, forward_h, adjoint_e, adjoint_h, material, inv_permittivity, height):
     depth, rows, cols = material.shape
     tiles = cols // LANES
-    gx, gy, gz = (lax.axis_index(a) for a in ("gx", "gy", "gz"))
-    nx, ny, nz = (lax.axis_size(a) for a in ("gx", "gy", "gz"))
+    nx, nz = lax.axis_size("gx"), lax.axis_size("gz")
     assert nz == 2
-    flags = jnp.stack([
-        gx % 2, gz % 2, gy % 2,
-        jnp.where(gy == 0, 1, 0), jnp.where(gx == 0, 1, 0),
-        jnp.where(gz > 0, 1, 0), jnp.where(gz < nz - 1, 1, 0),
-        gz * depth,
-    ]).astype(jnp.int32)
-    picker = [jnp.asarray(m, BF16) for m in row_picker(rows)]
-    picker = jnp.where(gy % 2 == 0, picker[0], picker[1])
-    placer = [jnp.asarray(m, BF16) for m in row_placer(rows)]
-    placer = jnp.where(gy % 2 == 0, placer[0], placer[1])
+    odd_z = lax.rem(lax.axis_index("gz"), 2)
+    picker = jnp.asarray(row_picker(rows), BF16)
+    placer = jnp.asarray(row_placer(rows), BF16)
+    corner_picking = jnp.asarray(corner_picker(rows), BF16)
+    corner_placing = jnp.asarray(corner_placer(), BF16)
+    table = jnp.asarray(column_table(depth))
     vmem = pl.BlockSpec(memory_space=pltpu.VMEM)
     smem = pl.BlockSpec(memory_space=pltpu.SMEM)
     params = pltpu.CompilerParams(vmem_limit_bytes=60 * 1024 * 1024)
     x_messages = 1 if nx == 2 else 2
 
+    chunk = TILE
+    field_block = pl.BlockSpec((3, chunk, rows, cols), lambda i: (0, i, 0, 0))
+    y_block = pl.BlockSpec((chunk, LAYERS, cols), lambda i: (i, 0, 0))
+    x_shape = jax.ShapeDtypeStruct((chunk, rows, LANES), F32)
     y_shape = jax.ShapeDtypeStruct((depth, LAYERS, cols), F32)
     packed = pl.pallas_call(
         functools.partial(pack_kernel, x_messages),
-        out_shape=[jax.ShapeDtypeStruct((depth, rows, LANES), F32)] * x_messages
+        grid=(depth // chunk,),
+        out_shape=[x_shape] * x_messages
         + [jax.ShapeDtypeStruct((LAYERS, rows, cols), F32), y_shape, y_shape],
-        in_specs=[smem] + [vmem] * 6,
-        out_specs=[vmem] * (x_messages + 3),
+        in_specs=[field_block] * 4
+        + [pl.BlockSpec((chunk, rows, cols), lambda i: (i, 0, 0)), vmem, vmem],
+        out_specs=[vmem] * (x_messages + 1) + [y_block] * 2,
         compiler_params=params,
         name="pack",
-    )(flags, forward_e, forward_h, adjoint_e, adjoint_h, material, picker)
+    )(forward_e, forward_h, adjoint_e, adjoint_h, material, picker, table)
     z_message, ya, yb = packed[x_messages:]
+    xp = [swap(packed[n], "gx", n) for n in range(x_messages)]
     yb = swap(yb, "gy", 1)
     ya = swap(ya, "gy", 0)
-    xp = swap(packed[0], "gx", 0)
-    if x_messages == 2:
-        xp = xp + swap(packed[1], "gx", 1)
     zr = swap(z_message, "gz", 0)
-    xz = lax.dynamic_slice_in_dim(xp, jnp.where(gz % 2 == 0, depth - WIDE, 0), WIDE, axis=0)
-    xz = swap(xz, "gz", 0)
-
-    corner_shape = jax.ShapeDtypeStruct((LAYERS * tiles + depth + 2 * WIDE, TILE, LANES), F32)
+    edge = jnp.where(odd_z == 0, chunk - WIDE, 0)
+    xz = [swap(lax.dynamic_slice_in_dim(x, edge, WIDE, axis=0), "gz", 0) for x in xp]
+
+    corner_tiles = LAYERS * WIDE // TILE * tiles + x_messages * (chunk + WIDE)
+    corner_shape = jax.ShapeDtypeStruct((corner_tiles, TILE, LANES), F32)
     corner_a, corner_b = pl.pallas_call(
-        corner_kernel,
+        functools.partial(corner_kernel, x_messages),
         out_shape=[corner_shape, corner_shape],
-        in_specs=[smem] + [vmem] * 3,
+        in_specs=[vmem] * (2 * x_messages + 2),
         out_specs=[vmem] * 2,
         compiler_params=params,
         name="corners",
-    )(flags, xp, xz, zr)
+    )(*xp, *xz, zr, corner_picking)
     corner_b = swap(corner_b, "gy", 1)
     corner_a = swap(corner_a, "gy", 0)
 
-    blocks = rows // TILE + 1
-    planes = depth + 2 * WIDE
-    block = (BEFORE + depth + AFTER, tiles + 1, blocks * TILE, LANES)
+    block = (BEFORE + depth + AFTER, tiles + 1, (rows // TILE + 1) * TILE, LANES)
     grad, dual = pl.pallas_call(
-        window_kernel,
+        functools.partial(window_kernel, x_messages),
         out_shape=[
             jax.ShapeDtypeStruct((rows, cols), F32),
             jax.ShapeDtypeStruct((3, depth, rows, cols), F32),
         ],
-        in_specs=[smem, smem] + [vmem] * 14,
+        in_specs=[smem] + [vmem] * (14 + 2 * x_messages),
         out_specs=[vmem] * 2,
         scratch_shapes=[
             *[pltpu.VMEM((3,) + block, F32)] * 6,
             pltpu.VMEM((1,) + block, F32),
-            pltpu.VMEM((planes, blocks * TILE, LANES), F32),
         ],
         compiler_params=params,
         name="window",
     )(
-        flags, inv_permittivity, forward_e, forward_h, adjoint_e, adjoint_h, material, height,
-        xp, xz, zr, ya, yb, corner_a, corner_b, placer,
+        inv_permittivity, forward_e, forward_h, adjoint_e, adjoint_h, material, height,
+        *xp, *xz, zr, ya, yb, corner_a, corner_b, placer, corner_placing, table,
     )
     return grad + swap(grad, "gz", 0), dual
 

time: 81.7 us -> 67 us (0.82)
  Pallas kernels: 42.3 us -> 32.8 us
  waiting for transfers between devices: 16.2 us -> 13.6 us
  other arithmetic: 3.32 us -> 1.33 us
    pallas_call x3, Pallas kernels: 42.3 us -> 32.8 us  [the longest x1 25.3 us: local(): pl.pallas_call(functools.partial(window_kernel, x_messages), out_shape=[j...]
    ppermute x8, waiting for transfers between devices: 16.2 us -> 13.6 us  [swap(): return lax.ppermute(array, axis, swap_pairs(lax.axis_size(axis), offset))]
    select_n x2 -> x0, other arithmetic: 1.99 us -> none  [the longest x1 1.38 us: local(): picker = jnp.where(gy % 2 == 0, picker[0], picker[1])]
    unnamed x18 -> x14, local copies, waits for them, and re-layouts: 3.5 us -> 3.42 us
  transfers between devices with their start and end apart: 8 -> 8, of which waited for: 4 -> 4; matrix products, arithmetic and copies ran while one was open for 1% -> 0% of each run, Pallas kernels for 3% -> 3%
where the time goes in v3:
time: 67 us; the launch traced here: 66.3 us
  Pallas kernels  32.8 us (49%)
  starting transfers between devices  14.5 us (22%)
  waiting for transfers between devices  13.6 us (20%)
  local copies, waits for them, and re-layouts  3.42 us (5%)
  other arithmetic  1.33 us (2%)
  between operations  0.7 us (1%)
    pallas_call x1, Pallas kernels, local(): pl.pallas_call(functools.partial(window_kernel, x_messages), out_shape=[j...  25.3 us
    ppermute x8, starting transfers between devices, swap(): return lax.ppermute(array, axis, swap_pairs(lax.axis_size(axis), offset))  14.5 us
    ppermute x8, waiting for transfers between devices, swap(): return lax.ppermute(array, axis, swap_pairs(lax.axis_size(axis), offset))  13.6 us
    pallas_call x1, Pallas kernels, local(): pl.pallas_call(functools.partial(pack_kernel, x_messages), grid=(depth //...  5.32 us
    unnamed x14, local copies, waits for them, and re-layouts  3.42 us
    pallas_call x1, Pallas kernels, local(): pl.pallas_call(functools.partial(corner_kernel, x_messages), out_shape=[c...  2.12 us
  transfers between devices with their start and end apart: 8, of which 4 were waited for; matrix products, arithmetic and copies ran while one was open for 0% of the time, Pallas kernels for 3%

profile of v3, /device:TPU:1, one launch (start us, length us, event | category | flops | bytes accessed | tf_op | source)
XLA Modules:
  0.0 66.3 jit_solution(17221363048162213573)
XLA Ops:
  0.6 5.3 %pack.1 = (f32[8,16,128]{2,1,0:T(8,128)}, f32[32,16,256]{2,1,0:T(8,128)}, f32[32,32,256]{2,1,0:T(8,128)}, f32[32,32,256]{2,1,0:T(8,128)}) custom-call(bf16[3,32,16,256]{3,2,1,0:T(8,128)(2,1)} %fe.3, bf16[3,32,16,256]{3,2,1,0:T(8,128)(2,1)} %fh.3, bf16[3,32,16,256]{3,2,1,0:T(8,128)(2,1)} %ae.3, bf16[3,32,16,256]{3,2,1,0:T(8,128)(2,1)} %ah.3, ...), custom_call_target="tpu_custom_call" | custom-call | tf_op jit(solution)/shard_map/pack/pallas_call | solution.py:536
  5.9 0.0 collective-permute-start.3
  6.0 4.5 %collective-permute-start.4 = (f32[32,32,256]{2,1,0:T(8,128)}, f32[32,32,256]{2,1,0:T(8,128)S(1)}, u32[]{:S(2)}, u32[]{:S(2)}) collective-permute-start(f32[32,32,256]{2,1,0:T(8,128)} %get-tuple-element.13), channel_id=1, source_target_pairs={{2,4},{4,2},{6,8},{8,6},{10,12},{12,10},{3,5},{5,3},{7,9},{9,7},{1... | collective-permute-start | bytes 3145736 | tf_op jit(solution)/shard_map/ppermute | solution.py:46
  10.5 1.3 %collective-permute-start.2 = (f32[32,16,256]{2,1,0:T(8,128)}, f32[32,16,256]{2,1,0:T(8,128)S(1)}, u32[]{:S(2)}, u32[]{:S(2)}) collective-permute-start(f32[32,16,256]{2,1,0:T(8,128)} %get-tuple-element.11), channel_id=1, source_target_pairs={{0,1},{1,0},{2,3},{3,2},{4,5},{5,4},{6,7},{7,6},{8,9},{9,8},{10,11... | collective-permute-start | bytes 1572872 | tf_op jit(solution)/shard_map/ppermute | solution.py:46
  11.8 1.2 %collective-permute-start = (f32[8,16,128]{2,1,0:T(8,128)}, f32[8,16,128]{2,1,0:T(8,128)S(1)}, u32[]{:S(2)}, u32[]{:S(2)}) collective-permute-start(f32[8,16,128]{2,1,0:T(8,128)} %get-tuple-element.10), channel_id=1, source_target_pairs={{0,16},{16,0},{1,17},{17,1},{2,18},{18,2},{3,19},{19,3},{4,20},{20... | collective-permute-start | bytes 196616 | tf_op jit(solution)/shard_map/ppermute | solution.py:46
  13.1 2.4 %collective-permute-done.refs_0_.others_0_ = f32[8,16,128]{2,1,0:T(8,128)S(1)} collective-permute-done((f32[8,16,128]{2,1,0:T(8,128)}, f32[8,16,128]{2,1,0:T(8,128)S(1)}, u32[]{:S(2)}, u32[]{:S(2)}) %collective-permute-start) | collective-permute-done | bytes 65568 | tf_op jit(solution)/shard_map/ppermute | solution.py:46
  15.5 0.2 collective-permute-start.1
  15.7 6.9 %collective-permute-done.1.refs_1_.others_1_ = f32[3,16,128]{2,1,0:T(8,128)S(1)} collective-permute-done((f32[3,16,128]{2,1,0:T(8,128)S(1)}, f32[3,16,128]{2,1,0:T(8,128)S(1)}, u32[]{:S(2)}, u32[]{:S(2)}) %collective-permute-start.1) | collective-permute-done | bytes 24608 | tf_op jit(solution)/shard_map/ppermute | solution.py:46
  22.6 0.0 collective-permute-done.2.refs_2_.others_2_
  22.6 0.6 copy-done.6
  23.2 0.8 %copy-done = f32[32,16,256]{2,1,0:T(8,128)} copy-done((f32[32,16,256]{2,1,0:T(8,128)}, f32[32,16,256]{2,1,0:T(8,128)S(1)}, u32[]{:S(2)}) %copy-start) | copy-done | bytes 524312
  24.0 2.1 %corners.1 = (f32[35,8,128]{2,1,0:T(8,128)}, f32[35,8,128]{2,1,0:T(8,128)}) custom-call(f32[8,16,128]{2,1,0:T(8,128)} %copy-done.3, f32[3,16,128]{2,1,0:T(8,128)} %copy-done.6, f32[32,16,256]{2,1,0:T(8,128)} %copy-done, bf16[2,192,512]{2,1,0:T(8,128)(2,1)} %constant.26.clone.refs_3_), custom_call_target="tpu_custom_call" | custom-call | tf_op jit(solution)/shard_map/corners/pallas_call | solution.py:557
  26.1 0.0 collective-permute-start.5
  26.1 5.3 %collective-permute-start.6 = (f32[35,8,128]{2,1,0:T(8,128)}, f32[35,8,128]{2,1,0:T(8,128)S(1)}, u32[]{:S(2)}, u32[]{:S(2)}) collective-permute-start(f32[35,8,128]{2,1,0:T(8,128)} %get-tuple-element.15), channel_id=1, source_target_pairs={{2,4},{4,2},{6,8},{8,6},{10,12},{12,10},{3,5},{5,3},{7,9},{9,7},{1... | collective-permute-start | bytes 430088 | tf_op jit(solution)/shard_map/ppermute | solution.py:46
  31.4 0.0 collective-permute-done.5.others_5_
  31.4 3.0 %collective-permute-done.6.others_6_ = f32[35,8,128]{2,1,0:T(8,128)S(1)} collective-permute-done((f32[35,8,128]{2,1,0:T(8,128)}, f32[35,8,128]{2,1,0:T(8,128)S(1)}, u32[]{:S(2)}, u32[]{:S(2)}) %collective-permute-start.6) | collective-permute-done | bytes 143392 | tf_op jit(solution)/shard_map/ppermute | solution.py:46
  34.4 0.0 collective-permute-done.3.others_3_
  34.4 0.6 copy-done.5
  35.1 0.4 copy-done.1
  35.4 1.0 %copy-done.2 = f32[32,32,256]{2,1,0:T(8,128)} copy-done((f32[32,32,256]{2,1,0:T(8,128)}, f32[32,32,256]{2,1,0:T(8,128)S(1)}, u32[]{:S(2)}) %copy-start.2) | copy-done | bytes 1048600
  36.4 25.3 %window.1 = (f32[16,256]{1,0:T(8,128)}, f32[3,32,16,256]{3,2,1,0:T(8,128)}) custom-call(f32[4]{0:T(128)} %inverse.1, bf16[3,32,16,256]{3,2,1,0:T(8,128)(2,1)} %fe.3, bf16[3,32,16,256]{3,2,1,0:T(8,128)(2,1)} %fh.3, bf16[3,32,16,256]{3,2,1,0:T(8,128)(2,1)} %ae.3, bf16[3,32,16,256]{3,2,1,0:T(8,128)(2,1)} %ah.3, s32[32,16,256]{2,1,0:T(8,128)} %material.3, ...), custom_call_target="tpu_custom_call" | custom-call | tf_op jit(solution)/shard_map/window/pallas_call | solution.py:569
  61.8 1.9 %collective-permute-start.7 = (f32[16,256]{1,0:T(8,128)}, f32[16,256]{1,0:T(8,128)S(1)}, u32[]{:S(2)}, u32[]{:S(2)}) collective-permute-start(f32[16,256]{1,0:T(8,128)} %get-tuple-element.16), channel_id=1, source_target_pairs={{0,1},{1,0},{2,3},{3,2},{4,5},{5,4},{6,7},{7,6},{8,9},{9,8},{10,11... | collective-permute-start | bytes 49160 | tf_op jit(solution)/shard_map/ppermute | solution.py:46
  63.6 1.3 %collective-permute-done.7 = f32[16,256]{1,0:T(8,128)S(1)} collective-permute-done((f32[16,256]{1,0:T(8,128)}, f32[16,256]{1,0:T(8,128)S(1)}, u32[]{:S(2)}, u32[]{:S(2)}) %collective-permute-start.7) | collective-permute-done | bytes 16416 | tf_op jit(solution)/shard_map/ppermute | solution.py:46
  65.0 1.3 %add.4 = f32[16,256]{1,0:T(8,128)} add(f32[16,256]{1,0:T(8,128)} %get-tuple-element.16, f32[16,256]{1,0:T(8,128)S(1)} %collective-permute-done.7) | non-fusion elementwise | flops 4096 | bytes 49152 | tf_op jit(solution)/shard_map/add | solution.py:587
  (11 shorter events, 0.0 us)
Async XLA Ops:
  5.9 28.5 %collective-permute-start.3 = (f32[32,32,256]{2,1,0:T(8,128)}, f32[32,32,256]{2,1,0:T(8,128)S(1)}, u32[]{:S(2)}, u32[]{:S(2)}) collective-permute-start(f32[32,32,256]{2,1,0:T(8,128)} %get-tuple-element.12), channel_id=1, source_target_pairs={{0,2},{2,0},{4,6},{6,4},{8,10},{10,8},{12,14},{14,12},{1,3},{3,1},... | collective-permute-start | bytes 3145736 | tf_op jit(solution)/shard_map/ppermute | solution.py:46
  6.0 28.4 %collective-permute-start.4 = (f32[32,32,256]{2,1,0:T(8,128)}, f32[32,32,256]{2,1,0:T(8,128)S(1)}, u32[]{:S(2)}, u32[]{:S(2)}) collective-permute-start(f32[32,32,256]{2,1,0:T(8,128)} %get-tuple-element.13), channel_id=1, source_target_pairs={{2,4},{4,2},{6,8},{8,6},{10,12},{12,10},{3,5},{5,3},{7,9},{9,7},{1... | collective-permute-start | bytes 3145736 | tf_op jit(solution)/shard_map/ppermute | solution.py:46
  10.5 12.1 %collective-permute-start.2 = (f32[32,16,256]{2,1,0:T(8,128)}, f32[32,16,256]{2,1,0:T(8,128)S(1)}, u32[]{:S(2)}, u32[]{:S(2)}) collective-permute-start(f32[32,16,256]{2,1,0:T(8,128)} %get-tuple-element.11), channel_id=1, source_target_pairs={{0,1},{1,0},{2,3},{3,2},{4,5},{5,4},{6,7},{7,6},{8,9},{9,8},{10,11... | collective-permute-start | bytes 1572872 | tf_op jit(solution)/shard_map/ppermute | solution.py:46
  11.8 3.6 %collective-permute-start = (f32[8,16,128]{2,1,0:T(8,128)}, f32[8,16,128]{2,1,0:T(8,128)S(1)}, u32[]{:S(2)}, u32[]{:S(2)}) collective-permute-start(f32[8,16,128]{2,1,0:T(8,128)} %get-tuple-element.10), channel_id=1, source_target_pairs={{0,16},{16,0},{1,17},{17,1},{2,18},{18,2},{3,19},{19,3},{4,20},{20... | collective-permute-start | bytes 196616 | tf_op jit(solution)/shard_map/ppermute | solution.py:46
  15.5 7.1 %copy-start.3 = (f32[8,16,128]{2,1,0:T(8,128)}, f32[8,16,128]{2,1,0:T(8,128)S(1)}, u32[]{:S(2)}) copy-start(f32[8,16,128]{2,1,0:T(8,128)S(1)} %collective-permute-done.refs_0_.others_0_) | copy-start | bytes 196612
  15.5 7.1 %collective-permute-start.1 = (f32[3,16,128]{2,1,0:T(8,128)S(1)}, f32[3,16,128]{2,1,0:T(8,128)S(1)}, u32[]{:S(2)}, u32[]{:S(2)}) collective-permute-start(f32[3,16,128]{2,1,0:T(8,128)S(1)} %constant_dynamic-slice_fusion), channel_id=1, source_target_pairs={{0,1},{1,0},{2,3},{3,2},{4,5},{5,4},{6,7},{7,6},{8,9},{9,8},{10,11... | collective-permute-start | bytes 73736 | tf_op jit(solution)/shard_map/ppermute | solution.py:46
  22.6 0.6 copy-start.6
  23.2 0.8 %copy-start = (f32[32,16,256]{2,1,0:T(8,128)}, f32[32,16,256]{2,1,0:T(8,128)S(1)}, u32[]{:S(2)}) copy-start(f32[32,16,256]{2,1,0:T(8,128)S(1)} %collective-permute-done.2.refs_2_.others_2_) | copy-start | bytes 1572868
  26.1 5.3 %collective-permute-start.5 = (f32[35,8,128]{2,1,0:T(8,128)}, f32[35,8,128]{2,1,0:T(8,128)S(1)}, u32[]{:S(2)}, u32[]{:S(2)}) collective-permute-start(f32[35,8,128]{2,1,0:T(8,128)} %get-tuple-element.14), channel_id=1, source_target_pairs={{0,2},{2,0},{4,6},{6,4},{8,10},{10,8},{12,14},{14,12},{1,3},{3,1},... | collective-permute-start | bytes 430088 | tf_op jit(solution)/shard_map/ppermute | solution.py:46
  26.1 8.3 %collective-permute-start.6 = (f32[35,8,128]{2,1,0:T(8,128)}, f32[35,8,128]{2,1,0:T(8,128)S(1)}, u32[]{:S(2)}, u32[]{:S(2)}) collective-permute-start(f32[35,8,128]{2,1,0:T(8,128)} %get-tuple-element.15), channel_id=1, source_target_pairs={{2,4},{4,2},{6,8},{8,6},{10,12},{12,10},{3,5},{5,3},{7,9},{9,7},{1... | collective-permute-start | bytes 430088 | tf_op jit(solution)/shard_map/ppermute | solution.py:46
  31.4 3.0 %copy-start.4 = (f32[35,8,128]{2,1,0:T(8,128)}, f32[35,8,128]{2,1,0:T(8,128)S(1)}, u32[]{:S(2)}) copy-start(f32[35,8,128]{2,1,0:T(8,128)S(1)} %collective-permute-done.5.others_5_) | copy-start | bytes 430084
  34.4 0.7 %copy-start.5 = (f32[35,8,128]{2,1,0:T(8,128)}, f32[35,8,128]{2,1,0:T(8,128)S(1)}, u32[]{:S(2)}) copy-start(f32[35,8,128]{2,1,0:T(8,128)S(1)} %collective-permute-done.6.others_6_) | copy-start | bytes 430084
  34.4 1.0 %copy-start.1 = (f32[32,32,256]{2,1,0:T(8,128)}, f32[32,32,256]{2,1,0:T(8,128)S(1)}, u32[]{:S(2)}) copy-start(f32[32,32,256]{2,1,0:T(8,128)S(1)} %collective-permute-done.3.others_3_) | copy-start | bytes 3145732
  35.4 1.0 %copy-start.2 = (f32[32,32,256]{2,1,0:T(8,128)}, f32[32,32,256]{2,1,0:T(8,128)S(1)}, u32[]{:S(2)}) copy-start(f32[32,32,256]{2,1,0:T(8,128)S(1)} %collective-permute-done.4.others_4_) | copy-start | bytes 3145732
  61.8 3.2 %collective-permute-start.7 = (f32[16,256]{1,0:T(8,128)}, f32[16,256]{1,0:T(8,128)S(1)}, u32[]{:S(2)}, u32[]{:S(2)}) collective-permute-start(f32[16,256]{1,0:T(8,128)} %get-tuple-element.16), channel_id=1, source_target_pairs={{0,1},{1,0},{2,3},{3,2},{4,5},{5,4},{6,7},{7,6},{8,9},{9,8},{10,11... | collective-permute-start | bytes 49160 | tf_op jit(solution)/shard_map/ppermute | solution.py:46

commit v4 on v3

--- a/solution.py
+++ b/solution.py
@@ -127,8 +127,8 @@
 def pack_kernel(x_messages, fe, fh, ae, ah, material, picker, table, *outs):
     chunk, rows, cols = material.shape
     refs = (fe, fh, ae, ah, material)
-    x_out = outs[:x_messages]
-    z_out, ya_out, yb_out = outs[x_messages:]
+    x_out, xz_out = outs[:x_messages], outs[x_messages:2 * x_messages]
+    z_out, ya_out, yb_out = outs[2 * x_messages:]
     odd_x, odd_y, odd_z = (place_on(axis)[1] for axis in ("gx", "gy", "gz"))
     step = pl.program_id(0)
 
@@ -170,17 +170,23 @@
         def _():
             out[...] += total
 
-    depth = chunk * pl.num_programs(0)
+    def edges(layers):
+        for n, (c, own, _) in enumerate(layers):
+            z_out[n] = own_field(refs, c, own).astype(F32)
 
     @pl.when((odd_z == 0) & (step == pl.num_programs(0) - 1))
     def _():
-        for n, (c, own, _) in enumerate(layers_to_next(chunk)):
-            z_out[n] = own_field(refs, c, own).astype(F32)
+        edges(layers_to_next(chunk))
 
     @pl.when((odd_z == 1) & (step == 0))
     def _():
-        for n, (c, own, _) in enumerate(layers_to_previous(chunk)):
-            z_out[n] = own_field(refs, c, own).astype(F32)
+        edges(layers_to_previous(chunk))
+
+    @pl.when(step == pl.num_programs(0) - 1)
+    def _():
+        edge = jnp.where(odd_z == 0, chunk - WIDE, 0)
+        for whole, part in zip(x_out, xz_out):
+            part[...] = whole[pl.ds(edge, WIDE)]
 
 
 def edge_rows(array, to_next):
@@ -194,7 +200,7 @@
 
 
 def corner_kernel(x_messages, *refs):
-    xp, xz = refs[:x_messages], refs[x_messages:2 * x_messages]
+    arrays = refs[:2 * x_messages]
     zr, picker, a_out, b_out = refs[2 * x_messages:]
     _, rows, cols = zr.shape
     odd_y = place_on("gy")[1]
@@ -204,11 +210,10 @@
     for message, out in ((0, a_out), (1, b_out)):
         at = 0
         for t in range(cols // LANES):
-            for n in range(0, count, TILE):
-                begin = message * count + n
-                out[at] = picked[begin:begin + TILE, t * LANES:(t + 1) * LANES]
+            for n in range(message * count, (message + 1) * count, TILE):
+                out[at] = lane_tile(picked[n:n + TILE], t)
                 at += 1
-        for array in (*xp, *xz):
+        for array in arrays:
             for k in range(array.shape[0]):
                 out[at + k] = edge_rows(array[k], 1 - (odd_y ^ message))
             at += array.shape[0]
@@ -230,41 +235,68 @@
     return [jnp.where(low, before, after) for before, after in zip(turned, turned[1:])]
 
 
-def window_kernel(x_messages, inverse, fe, fh, ae, ah, material, height, *others):
+def lane_tile(array, t):
+    return array[:, t * LANES:(t + 1) * LANES]
+
+
+def row_tiles(array):
+    return [array[b:b + TILE] for b in range(0, array.shape[0], TILE)]
+
+
+def rows_at(b):
+    return pl.ds(b * TILE, TILE)
+
+
+def weight(number, inverse):
+    value = jnp.zeros(number.shape, F32)
+    for m in range(inverse.shape[0]):
+        value = jnp.where(number == m + 1, inverse[m] * (COURANT * COURANT), value)
+    return value
+
+
+def arrange(c, own_tiles, halo, inverse):
+    if c == KAPPA:
+        own_tiles = [weight(p, inverse) for p in own_tiles]
+        halo = weight(halo, inverse)
+    elif SCALE[c] != 1.0:
+        own_tiles = [p * SCALE[c] for p in own_tiles]
+        halo = halo * SCALE[c]
+    return spread(own_tiles, halo)
+
+
+def prepare_kernel(inverse, fe, fh, ae, ah, material, *state):
+    chunk, rows, cols = material.shape
+    refs = (fe, fh, ae, ah, material)
+    first = BEFORE + pl.program_id(0) * chunk
+    zero = jnp.zeros((TILE, LANES), F32)
+    for z in range(chunk):
+        items = []
+        for c in range(COUNT):
+            whole = own_field(refs, c, z).astype(F32)
+            for t in range(cols // LANES):
+                items.append((c, t, arrange(c, row_tiles(lane_tile(whole, t)), zero, inverse)))
+        for c, t, parts in items:
+            for b, part in enumerate(parts):
+                state[c // 3][c % 3, first + z, t, rows_at(b)] = part
+
+
+def window_kernel(x_messages, inverse, height, *others):
     xp, xz = others[:x_messages], others[x_messages:2 * x_messages]
-    (zr, ya, yb, corner_a, corner_b, placer, corner_placing, table, grad_out, dual_out, forward_e,
-     forward_g, dual_e, dual_g, second_e, third_e, factor) = others[2 * x_messages:]
-    depth, rows, cols = material.shape
+    (zr, ya, yb, corner_a, corner_b, placer, corner_placing, table) = others[
+        2 * x_messages:2 * x_messages + 8]
+    (grad_out, dual_out, forward_e, forward_g, dual_e, dual_g, factor, second_e, third_e) = others[
+        2 * x_messages + 13:]
+    rows, cols = height.shape
+    depth = ya.shape[0]
     own = cols // LANES
     tiles = own + 1
     blocks = rows // TILE + 1
-    refs = (fe, fh, ae, ah, material)
     (at_x, odd_x), (at_y, odd_y), (at_z, odd_z) = (place_on(axis) for axis in ("gx", "gy", "gz"))
     start_z = at_z * depth
     row = row_of((TILE, LANES))
     lane = lane_of((TILE, LANES))
     zero = jnp.zeros((TILE, LANES), F32)
-    squared = [inverse[m] * (COURANT * COURANT) for m in range(inverse.shape[0])]
-
-    def rows_at(b):
-        return pl.ds(b * TILE, TILE)
-
-    def lane_tile(array, t):
-        return array[:, t * LANES:(t + 1) * LANES]
-
-    def row_tiles(array):
-        return [array[b * TILE:(b + 1) * TILE] for b in range(blocks - 1)]
-
-    def target(c):
-        if c == KAPPA:
-            return factor, 0
-        return (forward_e, forward_g, dual_e, dual_g)[c // 3], c % 3
-
-    def weight(number):
-        value = jnp.zeros(number.shape, F32)
-        for m, w in enumerate(squared):
-            value = jnp.where(number == m + 1, w, value)
-        return value
+    state = (forward_e, forward_g, dual_e, dual_g, factor)
 
     for t in range(tiles):
         for b in range(blocks):
@@ -299,28 +331,14 @@
             )
             total = part if total is None else total + part
         total = total.reshape(-1, blocks * TILE, LANES)
-        return weight(total) if c == KAPPA else total
+        return weight(total, inverse) if c == KAPPA else total
 
     for c in range(COUNT):
-        ref, to = target(c)
+        ref, to = state[c // 3], c % 3
         for group in range(groups):
             found = columns_of(c, group, wides[:x_messages])
             ref[to, pl.ds(BEFORE + group * TILE, TILE), own] = found
         ref[to, pl.ds(begin_halo, WIDE), own] = columns_of(c, halo_group, wides[x_messages:])
-
-    def store(items):
-        for c, slot, t, parts in items:
-            ref, at = target(c)
-            for b, part in enumerate(parts):
-                ref[at, slot, t, rows_at(b)] = part
-
-    def arrange(c, own_tiles, halo):
-        if c == KAPPA:
-            own_tiles = [weight(p) for p in own_tiles]
-            halo = weight(halo)
-        elif SCALE[c] != 1.0:
-            own_tiles = [p * SCALE[c] for p in own_tiles]
-        return spread(own_tiles, halo)
 
     arrived = jnp.concatenate([
         jnp.concatenate([ref[t * corner_tiles + k] for t in range(own)], axis=1)
@@ -330,12 +348,11 @@
 
     def halo_planes(layers):
         for n, (c, _, position) in enumerate(layers):
-            items = []
             for t in range(own):
-                halo = lane_tile(plane_halos[n * TILE:(n + 1) * TILE], t) * SCALE[c]
-                parts = arrange(c, row_tiles(lane_tile(zr[n], t)), halo)
-                items.append((c, position + BEFORE, t, parts))
-            store(items)
+                halo = lane_tile(plane_halos[n * TILE:(n + 1) * TILE], t)
+                parts = arrange(c, row_tiles(lane_tile(zr[n], t)), halo, inverse)
+                for b, part in enumerate(parts):
+                    state[c // 3][c % 3, position + BEFORE, t, rows_at(b)] = part
 
     @pl.when(odd_z == 0)
     def _():
@@ -345,22 +362,22 @@
     def _():
         halo_planes(layers_to_next(depth))
 
-    def own_planes(step, _):
-        items = []
-        for k in range(2):
-            z = step * 2 + k
+    def row_halos(step, _):
+        for k in range(4):
+            z = step * 4 + k
             arrived = jnp.concatenate([ya[z], yb[z]], axis=0).astype(BF16)
             halos = jnp.dot(placer[odd_y], arrived, preferred_element_type=F32)
             for c in range(COUNT):
-                whole = own_field(refs, c, z).astype(F32)
                 for t in range(own):
                     halo = lane_tile(halos[c * TILE:(c + 1) * TILE], t)
-                    parts = arrange(c, row_tiles(lane_tile(whole, t)), halo)
-                    items.append((c, z + BEFORE, t, parts))
-        store(items)
+                    if c == KAPPA:
+                        halo = weight(halo, inverse)
+                    ref, at = state[c // 3], (c % 3, z + BEFORE, t)
+                    ref[(*at, pl.ds(0, SHIFT))] = halo[:SHIFT]
+                    ref[(*at, pl.ds(blocks * TILE - SHIFT, SHIFT))] = halo[SHIFT:]
         return 0
 
-    lax.fori_loop(0, depth // 2, own_planes, 0)
+    lax.fori_loop(0, depth // 4, row_halos, 0)
 
     keep_row = jnp.where((row < SHIFT) & (at_y == 0), 0.0, 1.0)
     keep_lane = jnp.where((lane >= LANES // 2) & (at_x == 0), 0.0, 1.0)
@@ -512,12 +529,21 @@
             grad_out[rows_at(b), t * LANES:(t + 1) * LANES] = value
 
 
+def corner_swap(array, axes, offsets):
+    lengths = [lax.axis_size(a) for a in axes]
+    pairs = [
+        (i * lengths[1] + j, k * lengths[1] + l)
+        for i, k in swap_pairs(lengths[0], offsets[0])
+        for j, l in swap_pairs(lengths[1], offsets[1])
+    ]
+    return lax.ppermute(array, axes, pairs)
+
+
 def local(forward_e, forward_h, adjoint_e, adjoint_h, material, inv_permittivity, height):
     depth, rows, cols = material.shape
     tiles = cols // LANES
     nx, nz = lax.axis_size("gx"), lax.axis_size("gz")
     assert nz == 2
-    odd_z = lax.rem(lax.axis_index("gz"), 2)
     picker = jnp.asarray(row_picker(rows), BF16)
     placer = jnp.asarray(row_placer(rows), BF16)
     corner_picking = jnp.asarray(corner_picker(rows), BF16)
@@ -525,32 +551,45 @@
     table = jnp.asarray(column_table(depth))
     vmem = pl.BlockSpec(memory_space=pltpu.VMEM)
     smem = pl.BlockSpec(memory_space=pltpu.SMEM)
-    params = pltpu.CompilerParams(vmem_limit_bytes=60 * 1024 * 1024)
+    params = pltpu.CompilerParams(vmem_limit_bytes=24 * 1024 * 1024)
     x_messages = 1 if nx == 2 else 2
 
     chunk = TILE
     field_block = pl.BlockSpec((3, chunk, rows, cols), lambda i: (0, i, 0, 0))
+    material_block = pl.BlockSpec((chunk, rows, cols), lambda i: (i, 0, 0))
     y_block = pl.BlockSpec((chunk, LAYERS, cols), lambda i: (i, 0, 0))
     x_shape = jax.ShapeDtypeStruct((chunk, rows, LANES), F32)
+    xz_shape = jax.ShapeDtypeStruct((WIDE, rows, LANES), F32)
     y_shape = jax.ShapeDtypeStruct((depth, LAYERS, cols), F32)
+    fields = (forward_e, forward_h, adjoint_e, adjoint_h, material)
     packed = pl.pallas_call(
         functools.partial(pack_kernel, x_messages),
         grid=(depth // chunk,),
-        out_shape=[x_shape] * x_messages
+        out_shape=[x_shape] * x_messages + [xz_shape] * x_messages
         + [jax.ShapeDtypeStruct((LAYERS, rows, cols), F32), y_shape, y_shape],
-        in_specs=[field_block] * 4
-        + [pl.BlockSpec((chunk, rows, cols), lambda i: (i, 0, 0)), vmem, vmem],
-        out_specs=[vmem] * (x_messages + 1) + [y_block] * 2,
-        compiler_params=params,
+        in_specs=[field_block] * 4 + [material_block] + [vmem] * 2,
+        out_specs=[vmem] * (2 * x_messages + 1) + [y_block] * 2,
+        compiler_params=pltpu.CompilerParams(vmem_limit_bytes=60 * 1024 * 1024),
         name="pack",
-    )(forward_e, forward_h, adjoint_e, adjoint_h, material, picker, table)
-    z_message, ya, yb = packed[x_messages:]
+    )(*fields, picker, table)
+    z_message, ya, yb = packed[2 * x_messages:]
     xp = [swap(packed[n], "gx", n) for n in range(x_messages)]
+    xz = [corner_swap(packed[x_messages + n], ("gx", "gz"), (n, 0)) for n in range(x_messages)]
     yb = swap(yb, "gy", 1)
     ya = swap(ya, "gy", 0)
     zr = swap(z_message, "gz", 0)
-    edge = jnp.where(odd_z == 0, chunk - WIDE, 0)
-    xz = [swap(lax.dynamic_slice_in_dim(x, edge, WIDE, axis=0), "gz", 0) for x in xp]
+
+    block = (BEFORE + depth + AFTER, tiles + 1, (rows // TILE + 1) * TILE, LANES)
+    state_shapes = [pltpu.VMEM((3,) + block, F32)] * 4 + [pltpu.VMEM((1,) + block, F32)]
+    state = pl.pallas_call(
+        prepare_kernel,
+        grid=(depth // chunk,),
+        out_shape=state_shapes,
+        in_specs=[smem] + [field_block] * 4 + [material_block],
+        out_specs=[vmem] * 5,
+        compiler_params=params,
+        name="prepare",
+    )(inv_permittivity, *fields)
 
     corner_tiles = LAYERS * WIDE // TILE * tiles + x_messages * (chunk + WIDE)
     corner_shape = jax.ShapeDtypeStruct((corner_tiles, TILE, LANES), F32)
@@ -565,25 +604,24 @@
     corner_b = swap(corner_b, "gy", 1)
     corner_a = swap(corner_a, "gy", 0)
 
-    block = (BEFORE + depth + AFTER, tiles + 1, (rows // TILE + 1) * TILE, LANES)
+    operands = (
+        inv_permittivity, height, *xp, *xz, zr, ya, yb, corner_a, corner_b, placer,
+        corner_placing, table,
+    )
     grad, dual = pl.pallas_call(
         functools.partial(window_kernel, x_messages),
         out_shape=[
             jax.ShapeDtypeStruct((rows, cols), F32),
             jax.ShapeDtypeStruct((3, depth, rows, cols), F32),
+            *state_shapes,
         ],
-        in_specs=[smem] + [vmem] * (14 + 2 * x_messages),
-        out_specs=[vmem] * 2,
-        scratch_shapes=[
-            *[pltpu.VMEM((3,) + block, F32)] * 6,
-            pltpu.VMEM((1,) + block, F32),
-        ],
+        in_specs=[smem] + [vmem] * (len(operands) + 4),
+        out_specs=[vmem] * 7,
+        input_output_aliases={len(operands) + n: 2 + n for n in range(5)},
+        scratch_shapes=[pltpu.VMEM((3,) + block, F32)] * 2,
         compiler_params=params,
         name="window",
-    )(
-        inv_permittivity, forward_e, forward_h, adjoint_e, adjoint_h, material, height,
-        *xp, *xz, zr, ya, yb, corner_a, corner_b, placer, corner_placing, table,
-    )
+    )(*operands, *state)[:2]
     return grad + swap(grad, "gz", 0), dual
 
 

time: 67 us -> 58.6 us (0.87)
  Pallas kernels: 32.8 us -> 29.7 us
  waiting for transfers between devices: 13.6 us -> 11.2 us
  local copies, waits for them, and re-layouts: 3.42 us -> 1.04 us
  other arithmetic: 1.33 us -> 0.61 us
    ppermute x8 -> x7, waiting for transfers between devices: 13.6 us -> 7.55 us  [swap(): return lax.ppermute(array, axis, swap_pairs(lax.axis_size(axis), offset))]
    ppermute x0 -> x1, waiting for transfers between devices: none -> 3.69 us  [corner_swap(): return lax.ppermute(array, axes, pairs)]
    pallas_call x1, Pallas kernels: 25.3 us -> 22.1 us  [local(): pl.pallas_call(functools.partial(window_kernel, x_messages), out_shape=[j...]
    unnamed x14 -> x22, local copies, waits for them, and re-layouts: 3.42 us -> 1.04 us
    pallas_call x0 -> x1, Pallas kernels: none -> 1.91 us  [local(): pl.pallas_call(prepare_kernel, grid=(depth // chunk,), out_shape=state_sh...]
    pallas_call x1, Pallas kernels: 2.12 us -> 0.21 us  [local(): pl.pallas_call(functools.partial(corner_kernel, x_messages), out_shape=[c...]
    add x1, other arithmetic: 1.33 us -> 0.61 us  [local(): return (grad + swap(grad, 'gz', 0), dual)]
    ppermute x8 -> x7, starting transfers between devices: 14.5 us -> 14.3 us  [swap(): return lax.ppermute(array, axis, swap_pairs(lax.axis_size(axis), offset))]
  transfers between devices with their start and end apart: 8 -> 8, of which waited for: 4 -> 4; matrix products, arithmetic and copies ran while one was open for 0% -> 0% of each run, Pallas kernels for 3% -> 4%
where the time goes in v4:
time: 58.6 us; the launch traced here: 57.9 us
  Pallas kernels  29.7 us (51%)
  starting transfers between devices  14.5 us (25%)
  waiting for transfers between devices  11.2 us (19%)
  local copies, waits for them, and re-layouts  1.04 us (2%)
  between operations  0.83 us (1%)
  other arithmetic  0.61 us (1%)
    pallas_call x1, Pallas kernels, local(): pl.pallas_call(functools.partial(window_kernel, x_messages), out_shape=[j...  22.1 us
    ppermute x7, starting transfers between devices, swap(): return lax.ppermute(array, axis, swap_pairs(lax.axis_size(axis), offset))  14.3 us
    ppermute x7, waiting for transfers between devices, swap(): return lax.ppermute(array, axis, swap_pairs(lax.axis_size(axis), offset))  7.55 us
    pallas_call x1, Pallas kernels, local(): pl.pallas_call(functools.partial(pack_kernel, x_messages), grid=(depth //...  5.44 us
    ppermute x1, waiting for transfers between devices, corner_swap(): return lax.ppermute(array, axes, pairs)  3.69 us
    pallas_call x1, Pallas kernels, local(): pl.pallas_call(prepare_kernel, grid=(depth // chunk,), out_shape=state_sh...  1.91 us
  transfers between devices with their start and end apart: 8, of which 4 were waited for; matrix products, arithmetic and copies ran while one was open for 0% of the time, Pallas kernels for 4%

profile of v4, /device:TPU:1, one launch (start us, length us, event | category | flops | bytes accessed | tf_op | source)
XLA Modules:
  0.0 57.9 jit_solution(18272972357343369095)
XLA Ops:
  0.6 0.0 copy-start.8
  0.6 0.0 copy-start.7
  0.7 5.4 %pack.1 = (f32[8,16,128]{2,1,0:T(8,128)}, f32[3,16,128]{2,1,0:T(8,128)}, f32[32,16,256]{2,1,0:T(8,128)}, f32[32,32,256]{2,1,0:T(8,128)}, f32[32,32,256]{2,1,0:T(8,128)}) custom-call(bf16[3,32,16,256]{3,2,1,0:T(8,128)(2,1)} %fe.3, bf16[3,32,16,256]{3,2,1,0:T(8,128)(2,1)} %fh.3, bf16[3,32,16,256]{3,2,1,0:T(8,128)(2,1)} %ae.3, bf16[3,32,16,256]{3,2,1,0:T(8,128)(2,1)} %ah.3, ...), custom_call_target="tpu_custom_call" | custom-call | tf_op jit(solution)/shard_map/pack/pallas_call | solution.py:565
  6.2 0.1 collective-permute-start.3
  6.2 4.5 %collective-permute-start.4 = (f32[32,32,256]{2,1,0:T(8,128)}, f32[32,32,256]{2,1,0:T(8,128)S(1)}, u32[]{:S(2)}, u32[]{:S(2)}) collective-permute-start(f32[32,32,256]{2,1,0:T(8,128)} %get-tuple-element.20), channel_id=1, source_target_pairs={{2,4},{4,2},{6,8},{8,6},{10,12},{12,10},{3,5},{5,3},{7,9},{9,7},{1... | collective-permute-start | bytes 3145736 | tf_op jit(solution)/shard_map/ppermute | solution.py:46
  10.8 1.3 %collective-permute-start.2 = (f32[32,16,256]{2,1,0:T(8,128)}, f32[32,16,256]{2,1,0:T(8,128)S(1)}, u32[]{:S(2)}, u32[]{:S(2)}) collective-permute-start(f32[32,16,256]{2,1,0:T(8,128)} %get-tuple-element.18), channel_id=1, source_target_pairs={{0,1},{1,0},{2,3},{3,2},{4,5},{5,4},{6,7},{7,6},{8,9},{9,8},{10,11... | collective-permute-start | bytes 1572872 | tf_op jit(solution)/shard_map/ppermute | solution.py:46
  12.1 1.2 %collective-permute-start = (f32[8,16,128]{2,1,0:T(8,128)}, f32[8,16,128]{2,1,0:T(8,128)S(1)}, u32[]{:S(2)}, u32[]{:S(2)}) collective-permute-start(f32[8,16,128]{2,1,0:T(8,128)} %get-tuple-element.16), channel_id=1, source_target_pairs={{0,16},{16,0},{1,17},{17,1},{2,18},{18,2},{3,19},{19,3},{4,20},{20... | collective-permute-start | bytes 196616 | tf_op jit(solution)/shard_map/ppermute | solution.py:46
  13.3 0.2 collective-permute-start.1
  13.5 3.7 %collective-permute-done.1.refs_1_.others_1_ = f32[3,16,128]{2,1,0:T(8,128)S(1)} collective-permute-done((f32[3,16,128]{2,1,0:T(8,128)}, f32[3,16,128]{2,1,0:T(8,128)S(1)}, u32[]{:S(2)}, u32[]{:S(2)}) %collective-permute-start.1) | collective-permute-done | bytes 24608 | tf_op jit(solution)/shard_map/ppermute | solution.py:539
  17.2 0.0 collective-permute-done.refs_0_.others_0_
  17.2 5.6 %collective-permute-done.2.refs_2_.others_2_ = f32[32,16,256]{2,1,0:T(8,128)S(1)} collective-permute-done((f32[32,16,256]{2,1,0:T(8,128)}, f32[32,16,256]{2,1,0:T(8,128)S(1)}, u32[]{:S(2)}, u32[]{:S(2)}) %collective-permute-start.2) | collective-permute-done | bytes 524320 | tf_op jit(solution)/shard_map/ppermute | solution.py:46
  22.8 1.0 %copy-done.5 = bf16[2,192,512]{2,1,0:T(8,128)(2,1)S(1)} copy-done((bf16[2,192,512]{2,1,0:T(8,128)(2,1)S(1)}, bf16[2,192,512]{2,1,0:T(8,128)(2,1)}, u32[]{:S(2)}) %copy-start.5) | copy-done | bytes 393240
  23.8 0.2 corners.1
  24.0 0.1 collective-permute-start.5
  24.1 5.3 %collective-permute-start.6 = (f32[35,8,128]{2,1,0:T(8,128)S(1)}, f32[35,8,128]{2,1,0:T(8,128)S(1)}, u32[]{:S(2)}, u32[]{:S(2)}) collective-permute-start(f32[35,8,128]{2,1,0:T(8,128)S(1)} %get-tuple-element.22), channel_id=1, source_target_pairs={{2,4},{4,2},{6,8},{8,6},{10,12},{12,10},{3,5},{5,3},{7,9},{9,7},{1... | collective-permute-start | bytes 430088 | tf_op jit(solution)/shard_map/ppermute | solution.py:46
  29.5 1.9 %prepare.1 = (f32[3,42,3,24,128]{4,3,2,1,0:T(8,128)S(1)}, f32[3,42,3,24,128]{4,3,2,1,0:T(8,128)S(1)}, f32[3,42,3,24,128]{4,3,2,1,0:T(8,128)S(1)}, f32[3,42,3,24,...) custom-call(f32[4]{0:T(128)S(1)} %copy-done.10, bf16[3,32,16,256]{3,2,1,0:T(8,128)(2,1)S(1)} %copy-done, ...), custom_call_target="tpu_custom_call" | custom-call | tf_op jit(solution)/shard_map/prepare/pallas_call | solution.py:584
  31.4 0.0 collective-permute-done.5.others_5_
  31.4 0.8 %collective-permute-done.6.others_6_ = f32[35,8,128]{2,1,0:T(8,128)S(1)} collective-permute-done((f32[35,8,128]{2,1,0:T(8,128)S(1)}, f32[35,8,128]{2,1,0:T(8,128)S(1)}, u32[]{:S(2)}, u32[]{:S(2)}) %collective-permute-start.6) | collective-permute-done | bytes 143392 | tf_op jit(solution)/shard_map/ppermute | solution.py:46
  32.2 0.0 collective-permute-done.3.others_3_
  32.2 0.0 collective-permute-done.4.others_4_
  32.2 22.1 %window.1 = (f32[16,256]{1,0:T(8,128)S(1)}, f32[3,32,16,256]{3,2,1,0:T(8,128)}, f32[3,42,3,24,128]{4,3,2,1,0:T(8,128)S(1)}, f32[3,42,3,24,128]{4,3,2,1,0:T(8,128...) custom-call(f32[4]{0:T(128)S(1)} %copy-done.10, ...), custom_call_target="tpu_custom_call", output_to_operand_aliasing={{2}: (12, {}), {3}: (13, {}), {4}: (14, {}), {5}: (15, {}),... | custom-call | tf_op jit(solution)/shard_map/window/pallas_call | solution.py:611
  54.3 1.8 %collective-permute-start.7 = (f32[16,256]{1,0:T(8,128)S(1)}, f32[16,256]{1,0:T(8,128)S(1)}, u32[]{:S(2)}, u32[]{:S(2)}) collective-permute-start(f32[16,256]{1,0:T(8,128)S(1)} %get-tuple-element.28), channel_id=1, source_target_pairs={{0,1},{1,0},{2,3},{3,2},{4,5},{5,4},{6,7},{7,6},{8,9},{9,8},{10,11... | collective-permute-start | bytes 49160 | tf_op jit(solution)/shard_map/ppermute | solution.py:46
  56.1 1.1 %collective-permute-done.7 = f32[16,256]{1,0:T(8,128)S(1)} collective-permute-done((f32[16,256]{1,0:T(8,128)S(1)}, f32[16,256]{1,0:T(8,128)S(1)}, u32[]{:S(2)}, u32[]{:S(2)}) %collective-permute-start.7) | collective-permute-done | bytes 16416 | tf_op jit(solution)/shard_map/ppermute | solution.py:46
  57.2 0.6 %add.3 = f32[16,256]{1,0:T(8,128)} add(f32[16,256]{1,0:T(8,128)S(1)} %get-tuple-element.28, f32[16,256]{1,0:T(8,128)S(1)} %collective-permute-done.7) | non-fusion elementwise | flops 4096 | bytes 49152 | tf_op jit(solution)/shard_map/add | solution.py:625
  (19 shorter events, 0.0 us)
Async XLA Ops:
  0.6 31.6 %copy-start.8 = (s32[2,8,128]{2,1,0:T(8,128)S(1)}, s32[2,8,128]{2,1,0:T(8,128)}, u32[]{:S(2)}) copy-start(s32[2,8,128]{2,1,0:T(8,128)} %constant.14.clone.table.others_9_) | copy-start | bytes 24580
  0.6 31.6 %copy-start.7 = (bf16[2,104,64]{2,1,0:T(8,128)(2,1)S(1)}, bf16[2,104,64]{2,1,0:T(8,128)(2,1)}, u32[]{:S(2)}) copy-start(bf16[2,104,64]{2,1,0:T(8,128)(2,1)} %constant.11.clone.others_7_) | copy-start | bytes 79876
  0.7 28.8 %copy-start.4 = (s32[32,16,256]{2,1,0:T(8,128)S(1)}, s32[32,16,256]{2,1,0:T(8,128)}, u32[]{:S(2)}) copy-start(s32[32,16,256]{2,1,0:T(8,128)} %material.3) | copy-start | bytes 1572868
  0.7 28.8 %copy-start.3 = (bf16[3,32,16,256]{3,2,1,0:T(8,128)(2,1)S(1)}, bf16[3,32,16,256]{3,2,1,0:T(8,128)(2,1)}, u32[]{:S(2)}) copy-start(bf16[3,32,16,256]{3,2,1,0:T(8,128)(2,1)} %ah.3) | copy-start | bytes 2359300
  0.7 28.8 %copy-start.2 = (bf16[3,32,16,256]{3,2,1,0:T(8,128)(2,1)S(1)}, bf16[3,32,16,256]{3,2,1,0:T(8,128)(2,1)}, u32[]{:S(2)}) copy-start(bf16[3,32,16,256]{3,2,1,0:T(8,128)(2,1)} %ae.3) | copy-start | bytes 2359300
  0.7 28.8 %copy-start.1 = (bf16[3,32,16,256]{3,2,1,0:T(8,128)(2,1)S(1)}, bf16[3,32,16,256]{3,2,1,0:T(8,128)(2,1)}, u32[]{:S(2)}) copy-start(bf16[3,32,16,256]{3,2,1,0:T(8,128)(2,1)} %fh.3) | copy-start | bytes 2359300
  0.7 28.8 %copy-start = (bf16[3,32,16,256]{3,2,1,0:T(8,128)(2,1)S(1)}, bf16[3,32,16,256]{3,2,1,0:T(8,128)(2,1)}, u32[]{:S(2)}) copy-start(bf16[3,32,16,256]{3,2,1,0:T(8,128)(2,1)} %fe.3) | copy-start | bytes 2359300
  0.7 28.8 %copy-start.10 = (f32[4]{0:T(128)S(1)}, f32[4]{0:T(128)}, u32[]{:S(2)}) copy-start(f32[4]{0:T(128)} %inverse.3) | copy-start | bytes 52
  0.7 31.5 %copy-start.9 = (s32[16,256]{1,0:T(8,128)S(1)}, s32[16,256]{1,0:T(8,128)}, u32[]{:S(2)}) copy-start(s32[16,256]{1,0:T(8,128)} %height.1) | copy-start | bytes 49156
  6.2 26.0 %collective-permute-start.3 = (f32[32,32,256]{2,1,0:T(8,128)}, f32[32,32,256]{2,1,0:T(8,128)S(1)}, u32[]{:S(2)}, u32[]{:S(2)}) collective-permute-start(f32[32,32,256]{2,1,0:T(8,128)} %get-tuple-element.19), channel_id=1, source_target_pairs={{0,2},{2,0},{4,6},{6,4},{8,10},{10,8},{12,14},{14,12},{1,3},{3,1},... | collective-permute-start | bytes 3145736 | tf_op jit(solution)/shard_map/ppermute | solution.py:46
  6.2 25.9 %collective-permute-start.4 = (f32[32,32,256]{2,1,0:T(8,128)}, f32[32,32,256]{2,1,0:T(8,128)S(1)}, u32[]{:S(2)}, u32[]{:S(2)}) collective-permute-start(f32[32,32,256]{2,1,0:T(8,128)} %get-tuple-element.20), channel_id=1, source_target_pairs={{2,4},{4,2},{6,8},{8,6},{10,12},{12,10},{3,5},{5,3},{7,9},{9,7},{1... | collective-permute-start | bytes 3145736 | tf_op jit(solution)/shard_map/ppermute | solution.py:46
  10.8 12.0 %collective-permute-start.2 = (f32[32,16,256]{2,1,0:T(8,128)}, f32[32,16,256]{2,1,0:T(8,128)S(1)}, u32[]{:S(2)}, u32[]{:S(2)}) collective-permute-start(f32[32,16,256]{2,1,0:T(8,128)} %get-tuple-element.18), channel_id=1, source_target_pairs={{0,1},{1,0},{2,3},{3,2},{4,5},{5,4},{6,7},{7,6},{8,9},{9,8},{10,11... | collective-permute-start | bytes 1572872 | tf_op jit(solution)/shard_map/ppermute | solution.py:46
  12.1 5.1 %collective-permute-start = (f32[8,16,128]{2,1,0:T(8,128)}, f32[8,16,128]{2,1,0:T(8,128)S(1)}, u32[]{:S(2)}, u32[]{:S(2)}) collective-permute-start(f32[8,16,128]{2,1,0:T(8,128)} %get-tuple-element.16), channel_id=1, source_target_pairs={{0,16},{16,0},{1,17},{17,1},{2,18},{18,2},{3,19},{19,3},{4,20},{20... | collective-permute-start | bytes 196616 | tf_op jit(solution)/shard_map/ppermute | solution.py:46
  13.3 3.9 %collective-permute-start.1 = (f32[3,16,128]{2,1,0:T(8,128)}, f32[3,16,128]{2,1,0:T(8,128)S(1)}, u32[]{:S(2)}, u32[]{:S(2)}) collective-permute-start(f32[3,16,128]{2,1,0:T(8,128)} %get-tuple-element.17), channel_id=1, source_target_pairs={{0,17},{1,16},{16,1},{17,0},{2,19},{3,18},{18,3},{19,2},{4,21},{5,... | collective-permute-start | bytes 73736 | tf_op jit(solution)/shard_map/ppermute | solution.py:539
  22.8 1.0 %copy-start.5 = (bf16[2,192,512]{2,1,0:T(8,128)(2,1)S(1)}, bf16[2,192,512]{2,1,0:T(8,128)(2,1)}, u32[]{:S(2)}) copy-start(bf16[2,192,512]{2,1,0:T(8,128)(2,1)} %constant.12.clone.refs_3_) | copy-start | bytes 1179652
  23.8 8.4 %copy-start.6 = (bf16[2,256,192]{2,1,0:T(8,128)(2,1)S(1)}, bf16[2,256,192]{2,1,0:T(8,128)(2,1)}, u32[]{:S(2)}) copy-start(bf16[2,256,192]{2,1,0:T(8,128)(2,1)} %constant.13.clone.others_8_) | copy-start | bytes 589828
  24.0 7.4 %collective-permute-start.5 = (f32[35,8,128]{2,1,0:T(8,128)S(1)}, f32[35,8,128]{2,1,0:T(8,128)S(1)}, u32[]{:S(2)}, u32[]{:S(2)}) collective-permute-start(f32[35,8,128]{2,1,0:T(8,128)S(1)} %get-tuple-element.21), channel_id=1, source_target_pairs={{0,2},{2,0},{4,6},{6,4},{8,10},{10,8},{12,14},{14,12},{1,3},{3,1},... | collective-permute-start | bytes 430088 | tf_op jit(solution)/shard_map/ppermute | solution.py:46
  24.1 8.1 %collective-permute-start.6 = (f32[35,8,128]{2,1,0:T(8,128)S(1)}, f32[35,8,128]{2,1,0:T(8,128)S(1)}, u32[]{:S(2)}, u32[]{:S(2)}) collective-permute-start(f32[35,8,128]{2,1,0:T(8,128)S(1)} %get-tuple-element.22), channel_id=1, source_target_pairs={{2,4},{4,2},{6,8},{8,6},{10,12},{12,10},{3,5},{5,3},{7,9},{9,7},{1... | collective-permute-start | bytes 430088 | tf_op jit(solution)/shard_map/ppermute | solution.py:46
  54.3 2.9 %collective-permute-start.7 = (f32[16,256]{1,0:T(8,128)S(1)}, f32[16,256]{1,0:T(8,128)S(1)}, u32[]{:S(2)}, u32[]{:S(2)}) collective-permute-start(f32[16,256]{1,0:T(8,128)S(1)} %get-tuple-element.28), channel_id=1, source_target_pairs={{0,1},{1,0},{2,3},{3,2},{4,5},{5,4},{6,7},{7,6},{8,9},{9,8},{10,11... | collective-permute-start | bytes 49160 | tf_op jit(solution)/shard_map/ppermute | solution.py:46

commit v5 on v4

v5 whole, which is shorter than its diff:
```python
import functools

import jax
import jax.numpy as jnp
import numpy as np
from jax import lax
from jax.experimental import pallas as pl
from jax.experimental.pallas import tpu as pltpu
from jax.sharding import PartitionSpec as P

STEPS = 3
COURANT = 0.5
LANES = 128
TILE = 8
WIDE = 3
BEFORE = 5
AFTER = 5
SHIFT = 4
COUNT = 13
FE, FH, AE, AH, KAPPA = 0, 3, 6, 9, 12
LOW_DEPTH = [3] * 3 + [3] * 3 + [2] * 3 + [2] * 3 + [2]
HIGH_DEPTH = [3] * 3 + [2] * 3 + [3] * 3 + [2] * 3 + [2]
LAYERS = sum(LOW_DEPTH)
SCALE = [1.0] * 3 + [-1.0 / COURANT] * 3 + [1.0] * 3 + [1.0 / COURANT] * 3 + [1.0]
F32 = jnp.float32
BF16 = jnp.bfloat16


def layers_to_next(length):
    return [(c, length - d + k, k - d) for c, d in enumerate(LOW_DEPTH) for k in range(d)]


def layers_to_previous(length):
    return [(c, k, length + k) for c, d in enumerate(HIGH_DEPTH) for k in range(d)]


def swap_pairs(length, offset):
    pairs = []
    for i in range(offset, length - 1, 2):
        pairs += [(i, i + 1), (i + 1, i)]
    return pairs


def swap(array, axis, offset):
    return lax.ppermute(array, axis, swap_pairs(lax.axis_size(axis), offset))


def two_ways(rows_in, to_next, to_previous):
    first, second = np.zeros((2, len(to_next), rows_in), np.float32)
    for n, index in enumerate(to_next):
        first[n, index] = 1
    for n, index in enumerate(to_previous):
        second[n, index] = 1
    return np.stack([np.concatenate([first, second]), np.concatenate([second, first])])


def row_picker(rows):
    return two_ways(
        COUNT * rows,
        [c * rows + own for c, own, _ in layers_to_next(rows)],
        [c * rows + own for c, own, _ in layers_to_previous(rows)],
    )


def corner_picker(rows):
    group = LANES // rows
    return two_ways(
        LANES,
        [n * rows + rows - WIDE + k for n in range(group) for k in range(WIDE)],
        [n * rows + k for n in range(group) for k in range(WIDE)],
    )


def ways_back(rows_out, low, high):
    first = np.zeros((rows_out, len(low)), np.float32)
    second = np.zeros((rows_out, len(high)), np.float32)
    for n, (index, value) in enumerate(low):
        first[index, n] = value
    for n, (index, value) in enumerate(high):
        second[index, n] = value
    return np.stack([np.concatenate([second, first], 1), np.concatenate([first, second], 1)])


def row_placer(rows):
    low = [(c * TILE + there + SHIFT, SCALE[c]) for c, _, there in layers_to_next(rows)]
    high = [(c * TILE + there - rows + SHIFT, SCALE[c]) for c, _, there in layers_to_previous(rows)]
    return ways_back(COUNT * TILE, low, high)


def corner_placer(rows):
    group = LANES // rows
    low = [(n * TILE + SHIFT - WIDE + k, 1) for n in range(group) for k in range(WIDE)]
    high = [(n * TILE + SHIFT + k, 1) for n in range(group) for k in range(WIDE)]
    return ways_back(group * TILE, low, high)


def column_table(depth):
    groups = depth // TILE
    assert groups * LAYERS <= LANES
    table = np.full((2, TILE, LANES), -1, np.int32)
    for way, layers in enumerate((layers_to_next(LANES), layers_to_previous(0))):
        for g in range(groups):
            for n, (c, own, there) in enumerate(layers):
                lane = g * LAYERS + n
                table[way, :4, lane] = c, own, there % LANES, g
    return table


def lane_of(shape):
    return lax.broadcasted_iota(jnp.int32, shape, len(shape) - 1)


def row_of(shape):
    return lax.broadcasted_iota(jnp.int32, shape, len(shape) - 2)


def own_field(refs, c, z):
    fe, fh, ae, ah, material = refs
    if c == KAPPA:
        return (material[z] + 1).astype(F32).astype(BF16)
    return (fe, fh, ae, ah)[c // 3][c % 3, z]


def place_on(axis):
    return lax.axis_index(axis), lax.rem(lax.axis_index(axis), 2)


def pack_kernel(x_messages, *refs):
    whole, (picker, table), refs = refs[:5], refs[5:7], refs[7:]
    fields, refs = refs[:5], refs[5:]
    x_out, xz_out = refs[:x_messages], refs[x_messages:2 * x_messages]
    z_out, ya_out, yb_low_out, yb_high_out, arrived = refs[2 * x_messages:]
    depth, rows, cols = fields[4].shape
    odd_x, odd_y, odd_z = (place_on(axis)[1] for axis in ("gx", "gy", "gz"))
    groups = depth // TILE

    copies = []
    for group in range(groups):
        planes = pl.ds(group * TILE, TILE)
        parts = [(n, c, planes) for n in range(4) for c in range(3)] + [(4, planes)]
        copies.append([
            pltpu.make_async_copy(
                whole[n].at[at], fields[n].at[at], arrived.at[group, number]
            )
            for number, (n, *at) in enumerate((p[0], *p[1:]) for p in parts)
            for at in [tuple(at)]
        ])
    for group in copies:
        for copy in group:
            copy.start()

    totals = [jnp.zeros((TILE * rows, LANES), F32)] * x_messages
    for group in range(groups):
        for copy in copies[group]:
            copy.wait()
        for z in range(group * TILE, (group + 1) * TILE):
            stacked = jnp.concatenate([own_field(fields, c, z) for c in range(COUNT)], axis=0)
            picked = jnp.dot(picker[odd_y], stacked, preferred_element_type=F32)
            ya_out[z] = picked[:LAYERS]
            half = yb_low_out.shape[0]
            if z < half:
                yb_low_out[z] = picked[LAYERS:]
            else:
                yb_high_out[z - half] = picked[LAYERS:]

        for number in range(x_messages):
            way = odd_x ^ number
            offset = pl.multiple_of((1 - way) * (cols - LANES), LANES)
            of_field, of_lane, of_group = (table[way, k:k + 1, :] for k in (0, 1, 3))
            chosen = (row_of((LANES, LANES)) == of_lane) & (of_group == group)
            planes = pl.ds(group * TILE, TILE)
            for c in range(COUNT):
                if c == KAPPA:
                    part = fields[4][planes, :, pl.ds(offset, LANES)]
                    part = (part + 1).astype(F32).astype(BF16)
                else:
                    part = fields[c // 3][c % 3, planes, :, pl.ds(offset, LANES)]
                matrix = jnp.where(chosen & (of_field == c), 1.0, 0.0).astype(BF16)
                totals[number] += jnp.dot(
                    part.reshape(TILE * rows, LANES), matrix, preferred_element_type=F32
                )

    edge = jnp.where(odd_z == 0, TILE - WIDE, 0)
    for total, out, part in zip(totals, x_out, xz_out):
        out[...] = total.reshape(TILE, rows, LANES)
        part[...] = out[pl.ds(edge, WIDE)]

    def edges(layers):
        for n, (c, own, _) in enumerate(layers):
            z_out[n] = own_field(fields, c, own).astype(F32)

    @pl.when(odd_z == 0)
    def _():
        edges(layers_to_next(depth))

    @pl.when(odd_z == 1)
    def _():
        edges(layers_to_previous(depth))


def edge_rows(array, to_next):
    rows = array.shape[0]
    row = row_of((TILE, LANES))
    last = pltpu.roll(array[rows - TILE:], SHIFT, 0)
    first = pltpu.roll(array[:TILE], SHIFT, 0)
    last = jnp.where((row >= SHIFT - WIDE) & (row < SHIFT), last, 0.0)
    first = jnp.where((row >= SHIFT) & (row < SHIFT + WIDE), first, 0.0)
    return jnp.where(to_next == 1, last, first)


def corner_kernel(x_messages, *refs):
    arrays = refs[:2 * x_messages]
    zr, picker, _, a_out, b_out = refs[2 * x_messages:]
    _, rows, cols = zr.shape
    odd_y = place_on("gy")[1]
    arrived = zr[...].reshape(LAYERS * rows, cols).astype(BF16)
    picked = [
        jnp.dot(picker[odd_y], arrived[n:n + LANES], preferred_element_type=F32)
        for n in range(0, LAYERS * rows, LANES)
    ]
    count = picker.shape[1] // 2
    for message, out in ((0, a_out), (1, b_out)):
        at = 0
        for t in range(cols // LANES):
            for group in picked:
                for n in range(message * count, (message + 1) * count, TILE):
                    out[at] = lane_tile(group[n:n + TILE], t)
                    at += 1
        for array in arrays:
            for k in range(array.shape[0]):
                out[at + k] = edge_rows(array[k], 1 - (odd_y ^ message))
            at += array.shape[0]


def spread(tiles, halo):
    low = row_of((TILE, LANES)) < SHIFT
    turned = [pltpu.roll(t, SHIFT, 0) for t in tiles]
    out = [jnp.where(low, halo, turned[0])]
    for before, after in zip(turned, turned[1:]):
        out.append(jnp.where(low, before, after))
    out.append(jnp.where(low, turned[-1], halo))
    return out


def gather(tiles):
    low = row_of((TILE, LANES)) < SHIFT
    turned = [pltpu.roll(t, SHIFT, 0) for t in tiles]
    return [jnp.where(low, before, after) for before, after in zip(turned, turned[1:])]


def planes_at_once(count):
    return max(n for n in range(1, 18) if count % n == 0)


def lane_tile(array, t):
    return array[:, t * LANES:(t + 1) * LANES]


def row_tiles(array):
    return [array[b:b + TILE] for b in range(0, array.shape[0], TILE)]


def rows_at(b):
    return pl.ds(b * TILE, TILE)


def weight(number, inverse):
    value = jnp.zeros(number.shape, F32)
    for m in range(inverse.shape[0]):
        value = jnp.where(number == m + 1, inverse[m] * (COURANT * COURANT), value)
    return value


def arrange(c, own_tiles, halo, inverse):
    if c == KAPPA:
        own_tiles = [weight(p, inverse) for p in own_tiles]
        halo = weight(halo, inverse)
    elif SCALE[c] != 1.0:
        own_tiles = [p * SCALE[c] for p in own_tiles]
        halo = halo * SCALE[c]
    return spread(own_tiles, halo)


def prepare_kernel(inverse, fe, fh, ae, ah, material, *state):
    depth, _, cols = material.shape
    refs = (fe, fh, ae, ah, material)
    zero = jnp.zeros((TILE, LANES), F32)

    def planes(step, _):
        for k in range(4):
            z = step * 4 + k
            for c in range(COUNT):
                whole = own_field(refs, c, z).astype(F32)
                for t in range(cols // LANES):
                    parts = arrange(c, row_tiles(lane_tile(whole, t)), zero, inverse)
                    for b, part in enumerate(parts):
                        state[c // 3][c % 3, BEFORE + z, t, rows_at(b)] = part
        return 0

    lax.fori_loop(0, depth // 4, planes, 0)


def column_matrix(table, odd_x, number, c, group):
    way = 1 - (odd_x ^ number)
    of_field, of_target, of_group = (table[way, k:k + 1, :] for k in (0, 2, 3))
    chosen = (of_field == c) & (of_group == group) & (of_target == row_of((LANES, LANES)))
    return jnp.where(chosen, SCALE[c], 0.0).astype(BF16)


def columns_of(table, odd_x, c, group, arrays, inverse):
    total = None
    for number, array in enumerate(arrays):
        part = lax.dot_general(
            array, column_matrix(table, odd_x, number, c, group), (((1,), (1,)), ((), ())),
            preferred_element_type=F32,
        )
        total = part if total is None else total + part
    return weight(total, inverse) if c == KAPPA else total


def plane_kernel(x_messages, inverse, *others):
    xp, xz = others[:x_messages], others[x_messages:2 * x_messages]
    zr, table = others[2 * x_messages:2 * x_messages + 2]
    state = others[2 * x_messages + 7:]
    _, rows, cols = zr.shape
    own = cols // LANES
    blocks = rows // TILE + 1
    depth = state[0].shape[1] - BEFORE - AFTER
    odd_x, odd_z = (place_on(axis)[1] for axis in ("gx", "gz"))
    zero = jnp.zeros((TILE, LANES), F32)

    for t in range(own + 1):
        for b in range(blocks):
            for c in range(3):
                for ref, slot in zip(state, (depth + BEFORE, BEFORE - 1) * 2):
                    ref[c, slot, t, rows_at(b)] = zero

    groups = depth // TILE
    begin_halo = jnp.where(odd_z == 1, BEFORE - WIDE, BEFORE + depth)
    halo_group = jnp.where(odd_z == 1, groups - 1, 0)
    wides = []
    for array in (*xp, *xz):
        parts = []
        for k in range(array.shape[0]):
            parts += spread(row_tiles(array[k]), zero)
        wides.append(jnp.concatenate(parts, axis=0).astype(BF16))
    for c in range(COUNT):
        ref, to = state[c // 3], c % 3
        for group in range(groups):
            found = columns_of(table, odd_x, c, group, wides[:x_messages], inverse)
            found = found.reshape(TILE, blocks * TILE, LANES)
            ref[to, pl.ds(BEFORE + group * TILE, TILE), own] = found
        found = columns_of(table, odd_x, c, halo_group, wides[x_messages:], inverse)
        ref[to, pl.ds(begin_halo, WIDE), own] = found.reshape(WIDE, blocks * TILE, LANES)

    def halo_planes(layers):
        for n, (c, _, position) in enumerate(layers):
            for t in range(own):
                parts = arrange(c, row_tiles(lane_tile(zr[n], t)), zero, inverse)
                for b, part in enumerate(parts):
                    state[c // 3][c % 3, position + BEFORE, t, rows_at(b)] = part

    @pl.when(odd_z == 0)
    def _():
        halo_planes(layers_to_previous(depth))

    @pl.when(odd_z == 1)
    def _():
        halo_planes(layers_to_next(depth))


def first_slot(count, depth, odd_z):
    return BEFORE + jnp.where(odd_z == 1, depth - count, 0)


def ahead_lanes(parts):
    lane = lane_of((TILE, LANES))
    turned = [pltpu.roll(p, LANES - 1, 1) for p in parts]
    after = turned[1:] + turned[:1]
    return [jnp.where(lane == LANES - 1, a, t) for a, t in zip(after, turned)]


def reader(ref, slot):
    blocks = ref.shape[3] // TILE
    seen = {}

    def read(c, ahead, t, b):
        if (c, ahead, t, b) not in seen:
            seen[c, ahead, t, b] = ref[c, slot + ahead, t, rows_at(b)]
        return seen[c, ahead, t, b]

    def ahead_rows(c, ahead, t, b):
        if b == blocks - 1:
            return pltpu.roll(read(c, ahead, t, b), TILE - 1, 0)
        return ref[c, slot + ahead, t, pl.ds(b * TILE + 1, TILE)]

    def behind_rows(c, ahead, t, b):
        if b == 0:
            return pltpu.roll(read(c, ahead, t, b), 1, 0)
        return ref[c, slot + ahead, t, pl.ds(b * TILE - 1, TILE)]

    return read, ahead_rows, behind_rows


def magnetic_step(e, g, first, count, width, store):
    tiles, blocks = e.shape[2], e.shape[3] // TILE
    unroll = planes_at_once(count)

    def step(number, _):
        slot = first + number * unroll
        read, ahead_rows, _ = reader(e, slot)
        old, _, _ = reader(g, slot)
        results = {}
        for k in range(unroll):
            for b in range(blocks):
                y_x = ahead_lanes([read(1, k, t, b) for t in range(tiles)])
                z_x = ahead_lanes([read(2, k, t, b) for t in range(tiles)])
                for t in range(width):
                    ex, ey, ez = (read(c, k, t, b) for c in range(3))
                    curl = (
                        (ahead_rows(2, k, t, b) - ez) - (read(1, k + 1, t, b) - ey),
                        (read(0, k + 1, t, b) - ex) - (z_x[t] - ez),
                        (y_x[t] - ey) - (ahead_rows(0, k, t, b) - ex),
                    )
                    for c in range(3):
                        results[c, k, t, b] = old(c, k, t, b) + curl[c]
        store(slot, results)
        return 0

    lax.fori_loop(0, count // unroll, step, 0)


def dual_kernel(third_e, dual_g, dual_out):
    _, depth, rows, cols = dual_out.shape
    own, blocks = cols // LANES, rows // TILE + 1

    def store(slot, results):
        for c, k, t, b in results:
            if b == 0:
                values = gather([results[c, k, t, n] for n in range(blocks)])
                for n, value in enumerate(values):
                    where = (c, slot + k - BEFORE, rows_at(n), pl.ds(t * LANES, LANES))
                    dual_out[where] = value * COURANT

    magnetic_step(third_e, dual_g, BEFORE, depth, own, store)


def row_kernel(inverse, ya, yb_low, yb_high, placer, *state):
    state = state[5:]
    odd_y = place_on("gy")[1]
    own = ya.shape[2] // LANES
    height = state[0].shape[3]
    below, above = pl.ds(0, SHIFT), pl.ds(height - SHIFT, SHIFT)
    at_once = 4

    def place(array, start):
        def step(number, _):
            results = []
            for k in range(at_once):
                z = number * at_once + k
                arrived = jnp.concatenate([ya[start + z], array[z]], axis=0).astype(BF16)
                results.append(jnp.dot(placer[odd_y], arrived, preferred_element_type=F32))
            for k, halos in enumerate(results):
                z = number * at_once + k + start
                for c in range(COUNT):
                    for t in range(own):
                        halo = lane_tile(halos[c * TILE:(c + 1) * TILE], t)
                        if c == KAPPA:
                            halo = weight(halo, inverse)
                        at = (c % 3, z + BEFORE, t)
                        state[c // 3][(*at, below)] = halo[:SHIFT]
                        state[c // 3][(*at, above)] = halo[SHIFT:]
            return 0

        lax.fori_loop(0, array.shape[0] // at_once, step, 0)

    place(yb_low, 0)
    place(yb_high, yb_low.shape[0])


def window_kernel(x_messages, inverse, height, *others):
    corner_a, corner_b, corner_placing, table = others[:4]
    grad_out, forward_e, forward_g, dual_e, dual_g, factor, third_e, second_e = others[9:]
    rows, cols = height.shape
    depth = factor.shape[1] - BEFORE - AFTER
    own = cols // LANES
    tiles = own + 1
    blocks = rows // TILE + 1
    (at_x, odd_x), (at_y, odd_y), (at_z, odd_z) = (place_on(axis) for axis in ("gx", "gy", "gz"))
    start_z = at_z * depth
    row = row_of((TILE, LANES))
    lane = lane_of((TILE, LANES))
    zero = jnp.zeros((TILE, LANES), F32)
    state = (forward_e, forward_g, dual_e, dual_g, factor)
    below, above = pl.ds(0, SHIFT), pl.ds(blocks * TILE - SHIFT, SHIFT)

    for t in range(tiles):
        for b in range(blocks):
            for c in range(3):
                second_e[c, depth + BEFORE, t, rows_at(b)] = zero
                third_e[c, depth + BEFORE, t, rows_at(b)] = zero

    corner_tiles = LAYERS * WIDE // TILE
    groups = depth // TILE
    begin_halo = jnp.where(odd_z == 1, BEFORE - WIDE, BEFORE + depth)
    halo_group = jnp.where(odd_z == 1, groups - 1, 0)
    at = own * corner_tiles
    wides = []
    for count in [TILE] * x_messages + [WIDE] * x_messages:
        parts = [corner_a[at + k] + corner_b[at + k] for k in range(count)]
        wides.append(jnp.concatenate(parts, axis=0).astype(BF16))
        at += count
    for c in range(COUNT):
        ref, to = state[c // 3], c % 3
        for group in range(groups + 1):
            if group < groups:
                found = columns_of(table, odd_x, c, group, wides[:x_messages], inverse)
                slots = pl.ds(BEFORE + group * TILE, TILE)
            else:
                found = columns_of(table, odd_x, c, halo_group, wides[x_messages:], inverse)
                slots = pl.ds(begin_halo, WIDE)
            found = found.reshape(-1, TILE, LANES)
            ref[to, slots, own, below] = found[:, :SHIFT]
            ref[to, slots, own, above] = found[:, SHIFT:]

    group = LANES // rows
    group_tiles = group * WIDE // TILE
    plane_halos = []
    for n in range(LAYERS // group):
        arrived = jnp.concatenate([
            jnp.concatenate([ref[t * corner_tiles + k] for t in range(own)], axis=1)
            for ref in (corner_a, corner_b) for k in range(n * group_tiles, (n + 1) * group_tiles)
        ], axis=0).astype(BF16)
        placed = jnp.dot(corner_placing[odd_y], arrived, preferred_element_type=F32)
        plane_halos += [placed[k * TILE:(k + 1) * TILE] for k in range(group)]

    def halo_planes(layers):
        for n, (c, _, position) in enumerate(layers):
            for t in range(own):
                halo = lane_tile(plane_halos[n], t) * SCALE[c]
                if c == KAPPA:
                    halo = weight(halo, inverse)
                at = (c % 3, position + BEFORE, t)
                state[c // 3][(*at, below)] = halo[:SHIFT]
                state[c // 3][(*at, above)] = halo[SHIFT:]

    @pl.when(odd_z == 0)
    def _():
        halo_planes(layers_to_previous(depth))

    @pl.when(odd_z == 1)
    def _():
        halo_planes(layers_to_next(depth))

    keep_row = jnp.where((row < SHIFT) & (at_y == 0), 0.0, 1.0)
    keep_lane = jnp.where((lane >= LANES // 2) & (at_x == 0), 0.0, 1.0)

    def mask(value, t, b):
        if b == 0:
            value = value * keep_row
        if t == own:
            value = value * keep_lane
        return value

    def behind_lanes(parts):
        turned = [pltpu.roll(p, 1, 1) for p in parts]
        return [jnp.where(lane == 0, turned[(t - 1) % tiles], turned[t]) for t in range(tiles)]

    def begin(count):
        return first_slot(count, depth, odd_z)

    def magnetic(e, g, count):
        def store(slot, results):
            for (c, k, t, b), value in results.items():
                g[c, slot + k, t, rows_at(b)] = mask(value, t, b)

        magnetic_step(e, g, begin(count), count, tiles, store)

    def electric(e, g, to, count, partner=None, totals=()):
        unroll = planes_at_once(count)
        first = begin(count)

        def step(number, carry):
            carry = list(carry)
            slot = first + number * unroll
            read, _, behind_rows = reader(g, slot)
            old, _, _ = reader(e, slot)
            weights, _, _ = reader(factor, slot)
            results = {}
            for k in range(unroll):
                if partner is not None:
                    position = slot + k - BEFORE
                    inside = (position >= 0) & (position < depth)
                    position = jnp.where(inside, position + start_z, jnp.int32(2**30))
                for b in range(blocks):
                    y_x = behind_lanes([read(1, k, t, b) for t in range(tiles)])
                    z_x = behind_lanes([read(2, k, t, b) for t in range(tiles)])
                    for t in range(tiles):
                        gx, gy, gz = (read(c, k, t, b) for c in range(3))
                        curl = (
                            (gz - behind_rows(2, k, t, b)) - (gy - read(1, k - 1, t, b)),
                            (gx - read(0, k - 1, t, b)) - (gz - z_x[t]),
                            (gy - y_x[t]) - (gx - behind_rows(0, k, t, b)),
                        )
                        scale = weights(0, k, t, b)
                        product = None
                        for c in range(3):
                            value = old(c, k, t, b) - scale * curl[c]
                            results[c, k, t, b] = value
                            if partner is not None and t < own:
                                term = value * partner[c, slot + k, t, rows_at(b)]
                                product = term if product is None else product + term
                        if product is not None:
                            chosen = position < limits[t * blocks + b]
                            carry[t * blocks + b] += jnp.where(chosen, product, 0.0)
            for (c, k, t, b), value in results.items():
                to[c, slot + k, t, rows_at(b)] = value
            return tuple(carry)

        return lax.fori_loop(0, count // unroll, step, totals)

    def count(low, high):
        planes = depth + max(low, high)
        return planes if planes_at_once(planes) > 8 else planes + 1

    magnetic(dual_e, dual_g, count(2, 2))
    electric(dual_e, dual_g, second_e, count(1, 2))
    magnetic(second_e, dual_g, count(1, 1))
    electric(second_e, dual_g, third_e, count(0, 1))

    none = jnp.zeros((TILE, LANES), jnp.int32)
    limits = []
    for t in range(own):
        limits += spread(row_tiles(lane_tile(height[...], t)), none)
    totals = (zero,) * (own * blocks)
    magnetic(forward_e, forward_g, count(3, 2))
    totals = electric(forward_e, forward_g, forward_e, count(2, 2), third_e, totals)
    magnetic(forward_e, forward_g, count(2, 1))
    totals = electric(forward_e, forward_g, forward_e, count(1, 1), second_e, totals)
    magnetic(forward_e, forward_g, count(1, 0))
    totals = electric(forward_e, forward_g, forward_e, depth, dual_e, totals)
    for t in range(own):
        values = gather(list(totals[t * blocks:(t + 1) * blocks]))
        for b, value in enumerate(values):
            grad_out[rows_at(b), t * LANES:(t + 1) * LANES] = value


def corner_swap(array, axes, offsets):
    lengths = [lax.axis_size(a) for a in axes]
    pairs = [
        (i * lengths[1] + j, k * lengths[1] + l)
        for i, k in swap_pairs(lengths[0], offsets[0])
        for j, l in swap_pairs(lengths[1], offsets[1])
    ]
    return lax.ppermute(array, axes, pairs)


def local(forward_e, forward_h, adjoint_e, adjoint_h, material, inv_permittivity, height):
    depth, rows, cols = material.shape
    tiles = cols // LANES
    nx, nz = lax.axis_size("gx"), lax.axis_size("gz")
    assert nz == 2
    picker = jnp.asarray(row_picker(rows), BF16)
    placer = jnp.asarray(row_placer(rows), BF16)
    corner_picking = jnp.asarray(corner_picker(rows), BF16)
    corner_placing = jnp.asarray(corner_placer(rows), BF16)
    table = jnp.asarray(column_table(depth))
    vmem = pl.BlockSpec(memory_space=pltpu.VMEM)
    smem = pl.BlockSpec(memory_space=pltpu.SMEM)
    params = pltpu.CompilerParams(vmem_limit_bytes=24 * 1024 * 1024)
    anywhere = pl.BlockSpec(memory_space=pl.ANY)
    x_messages = 1 if nx == 2 else 2

    chunk = TILE
    x_shape = jax.ShapeDtypeStruct((chunk, rows, LANES), F32)
    xz_shape = jax.ShapeDtypeStruct((WIDE, rows, LANES), F32)
    y_shape = jax.ShapeDtypeStruct((depth, LAYERS, cols), F32)
    fields = (forward_e, forward_h, adjoint_e, adjoint_h, material)
    in_hbm = pl.BlockSpec(memory_space=pltpu.HBM)
    half_shape = jax.ShapeDtypeStruct((depth // 2, LAYERS, cols), F32)
    packed = pl.pallas_call(
        functools.partial(pack_kernel, x_messages),
        out_shape=[pltpu.VMEM(f.shape, f.dtype) for f in fields]
        + [x_shape] * x_messages + [xz_shape] * x_messages
        + [jax.ShapeDtypeStruct((LAYERS, rows, cols), F32), y_shape, half_shape, half_shape],
        in_specs=[in_hbm] * 5 + [vmem] * 2,
        out_specs=[vmem] * (2 * x_messages + 9),
        scratch_shapes=[pltpu.SemaphoreType.DMA((depth // TILE, COUNT))],
        compiler_params=pltpu.CompilerParams(vmem_limit_bytes=60 * 1024 * 1024),
        name="pack",
    )(*fields, picker, table)
    fields, packed = packed[:5], packed[5:]
    z_message, ya, yb_low, yb_high = packed[2 * x_messages:]
    ya = swap(ya, "gy", 0)
    zr = swap(z_message, "gz", 0)
    yb_low = swap(yb_low, "gy", 1)
    yb_high = swap(yb_high, "gy", 1)
    xp = [swap(packed[n], "gx", n) for n in range(x_messages)]
    xz = [corner_swap(packed[x_messages + n], ("gx", "gz"), (n, 0)) for n in range(x_messages)]

    block = (BEFORE + depth + AFTER, tiles + 1, (rows // TILE + 1) * TILE, LANES)
    state_shapes = [pltpu.VMEM((3,) + block, F32)] * 4 + [pltpu.VMEM((1,) + block, F32)]
    state = pl.pallas_call(
        prepare_kernel,
        out_shape=state_shapes,
        in_specs=[smem] + [vmem] * 5,
        out_specs=[vmem] * 5,
        compiler_params=params,
        name="prepare",
    )(inv_permittivity, *fields)

    corner_tiles = LAYERS * WIDE // TILE * tiles + x_messages * (chunk + WIDE)
    corner_shape = jax.ShapeDtypeStruct((corner_tiles, TILE, LANES), F32)
    corner_a, corner_b = pl.pallas_call(
        functools.partial(corner_kernel, x_messages),
        out_shape=[corner_shape, corner_shape],
        in_specs=[vmem] * (2 * x_messages + 2) + [anywhere],
        out_specs=[vmem] * 2,
        compiler_params=params,
        name="corners",
    )(*xp, *xz, zr, corner_picking, state[4])
    corner_b = swap(corner_b, "gy", 1)
    corner_a = swap(corner_a, "gy", 0)

    operands = (inv_permittivity, *xp, *xz, zr, table)
    state = pl.pallas_call(
        functools.partial(plane_kernel, x_messages),
        out_shape=state_shapes,
        in_specs=[smem] + [vmem] * (len(operands) + 4),
        out_specs=[vmem] * 5,
        input_output_aliases={len(operands) + n: n for n in range(5)},
        compiler_params=params,
        name="planes",
    )(*operands, *state)

    operands = (inv_permittivity, ya, yb_low, yb_high, placer)
    state = pl.pallas_call(
        row_kernel,
        out_shape=state_shapes,
        in_specs=[smem] + [vmem] * (len(operands) + 4),
        out_specs=[vmem] * 5,
        input_output_aliases={len(operands) + n: n for n in range(5)},
        compiler_params=params,
        name="rows",
    )(*operands, *state)

    operands = (inv_permittivity, height, corner_a, corner_b, corner_placing, table)
    results = pl.pallas_call(
        functools.partial(window_kernel, x_messages),
        out_shape=[jax.ShapeDtypeStruct((rows, cols), F32), *state_shapes, state_shapes[0]],
        in_specs=[smem] + [vmem] * (len(operands) + 4),
        out_specs=[vmem] * 7,
        input_output_aliases={len(operands) + n: 1 + n for n in range(5)},
        scratch_shapes=[pltpu.VMEM((3,) + block, F32)],
        compiler_params=params,
        name="window",
    )(*operands, *state)
    grad, dual_g, third_e = results[0], results[4], results[6]
    dual = pl.pallas_call(
        dual_kernel,
        out_shape=jax.ShapeDtypeStruct((3, depth, rows, cols), F32),
        in_specs=[vmem] * 2,
        out_specs=vmem,
        compiler_params=params,
        name="dual",
    )(third_e, dual_g)
    return grad + swap(grad, "gz", 0), dual


def solution(mesh):
    fields = P(None, "gz", "gy", "gx")
    return jax.shard_map(
        local,
        mesh=mesh,
        in_specs=(fields, fields, fields, fields, P("gz", "gy", "gx"), P(), P("gy", "gx")),
        out_specs=(P("gy", "gx"), fields),
        check_vma=False,
    )
```

time: 58.6 us -> 53.8 us (0.918)
  waiting for transfers between devices: 11.2 us -> 3.22 us
  local copies, waits for them, and re-layouts: 1.04 us -> 4.74 us
  Pallas kernels: 29.7 us -> 28.4 us
  starting transfers between devices: 14.5 us -> 15.7 us
    pallas_call x1, Pallas kernels: 22.1 us -> 14.5 us  [local(): pl.pallas_call(functools.partial(window_kernel, x_messages), out_shape=[j...]
    ppermute x7 -> x8, waiting for transfers between devices: 7.55 us -> 0.46 us  [swap(): return lax.ppermute(array, axis, swap_pairs(lax.axis_size(axis), offset))]
    pallas_call x2 -> x5, Pallas kernels: 7.35 us -> 13.7 us  [the longest x1 5.71 us: local(): pl.pallas_call(functools.partial(pack_kernel, x_messages), out_shape=[plt...]
    unnamed x22 -> x20, local copies, waits for them, and re-layouts: 1.04 us -> 4.74 us
    ppermute x1, starting transfers between devices: 0.21 us -> 1.2 us  [corner_swap(): return lax.ppermute(array, axes, pairs)]
    ppermute x1, waiting for transfers between devices: 3.69 us -> 2.76 us  [corner_swap(): return lax.ppermute(array, axes, pairs)]
    ppermute x7 -> x8, starting transfers between devices: 14.3 us -> 14.5 us  [swap(): return lax.ppermute(array, axis, swap_pairs(lax.axis_size(axis), offset))]
  transfers between devices with their start and end apart: 8 -> 9, of which waited for: 4 -> 2; matrix products, arithmetic and copies ran while one was open for 0% -> 0% of each run, Pallas kernels for 4% -> 15%
where the time goes in v5:
time: 53.8 us; the launch traced here: 53.5 us
  Pallas kernels  28.4 us (53%)
  starting transfers between devices  15.7 us (29%)
  local copies, waits for them, and re-layouts  4.74 us (9%)
  waiting for transfers between devices  3.22 us (6%)
  between operations  0.86 us (2%)
  other arithmetic  0.61 us (1%)
    pallas_call x1, Pallas kernels, local(): pl.pallas_call(functools.partial(window_kernel, x_messages), out_shape=[j...  14.5 us
    ppermute x8, starting transfers between devices, swap(): return lax.ppermute(array, axis, swap_pairs(lax.axis_size(axis), offset))  14.5 us
    pallas_call x1, Pallas kernels, local(): pl.pallas_call(functools.partial(pack_kernel, x_messages), out_shape=[plt...  5.71 us
    unnamed x20, local copies, waits for them, and re-layouts  4.74 us
    ppermute x1, waiting for transfers between devices, corner_swap(): return lax.ppermute(array, axes, pairs)  2.76 us
    pallas_call x1, Pallas kernels, local(): pl.pallas_call(functools.partial(plane_kernel, x_messages), out_shape=sta...  2.19 us
    pallas_call x1, Pallas kernels, local(): pl.pallas_call(row_kernel, out_shape=state_shapes, in_specs=[smem] + [vme...  2.15 us
    pallas_call x1, Pallas kernels, local(): pl.pallas_call(dual_kernel, out_shape=jax.ShapeDtypeStruct((3, depth, row...  2.01 us
  transfers between devices with their start and end apart: 9, of which 2 were waited for; matrix products, arithmetic and copies ran while one was open for 0% of the time, Pallas kernels for 15%

profile of v5, /device:TPU:1, one launch (start us, length us, event | category | flops | bytes accessed | tf_op | source)
XLA Modules:
  0.0 53.5 jit_solution(16002975528660783115)
XLA Ops:
  0.7 5.7 %pack.1 = (bf16[3,32,16,256]{3,2,1,0:T(8,128)(2,1)S(1)}, bf16[3,32,16,256]{3,2,1,0:T(8,128)(2,1)S(1)}, bf16[3,32,16,256]{3,2,1,0:T(8,128)(2,1)S(1)}, bf16[3,32,1...) custom-call(bf16[3,32,16,256]{3,2,1,0:T(8,128)(2,1)} %refs_0_.1, ...), custom_call_target="tpu_custom_call" | custom-call | tf_op jit(solution)/shard_map/pack/pallas_call | solution.py:681
  6.4 0.9 %copy-done = bf16[3,32,16,256]{3,2,1,0:T(8,128)(2,1)} copy-done((bf16[3,32,16,256]{3,2,1,0:T(8,128)(2,1)}, bf16[3,32,16,256]{3,2,1,0:T(8,128)(2,1)S(1)}, u32[]{:S(2)}) %copy-start) | copy-done | bytes 786456
  7.3 0.9 %copy-done.2 = bf16[3,32,16,256]{3,2,1,0:T(8,128)(2,1)} copy-done((bf16[3,32,16,256]{3,2,1,0:T(8,128)(2,1)}, bf16[3,32,16,256]{3,2,1,0:T(8,128)(2,1)S(1)}, u32[]{:S(2)}) %copy-start.2) | copy-done | bytes 786456
  8.2 0.1 collective-permute-start.5
  8.2 2.7 %collective-permute-start.2 = (f32[32,16,256]{2,1,0:T(8,128)}, f32[32,16,256]{2,1,0:T(8,128)S(1)}, u32[]{:S(2)}, u32[]{:S(2)}) collective-permute-start(f32[32,16,256]{2,1,0:T(8,128)} %get-tuple-element.35), channel_id=1, source_target_pairs={{0,1},{1,0},{2,3},{3,2},{4,5},{5,4},{6,7},{7,6},{8,9},{9,8},{10,11... | collective-permute-start | bytes 1572872 | tf_op jit(solution)/shard_map/ppermute | solution.py:45
  10.9 3.4 %collective-permute-start.6 = (f32[16,32,256]{2,1,0:T(8,128)}, f32[16,32,256]{2,1,0:T(8,128)S(1)}, u32[]{:S(2)}, u32[]{:S(2)}) collective-permute-start(f32[16,32,256]{2,1,0:T(8,128)} %get-tuple-element.45), channel_id=1, source_target_pairs={{2,4},{4,2},{6,8},{8,6},{10,12},{12,10},{3,5},{5,3},{7,9},{9,7},{1... | collective-permute-start | bytes 1572872 | tf_op jit(solution)/shard_map/ppermute | solution.py:45
  14.3 2.2 %collective-permute-start.7 = (f32[16,32,256]{2,1,0:T(8,128)}, f32[16,32,256]{2,1,0:T(8,128)S(1)}, u32[]{:S(2)}, u32[]{:S(2)}) collective-permute-start(f32[16,32,256]{2,1,0:T(8,128)} %get-tuple-element.46), channel_id=1, source_target_pairs={{2,4},{4,2},{6,8},{8,6},{10,12},{12,10},{3,5},{5,3},{7,9},{9,7},{1... | collective-permute-start | bytes 1572872 | tf_op jit(solution)/shard_map/ppermute | solution.py:45
  16.5 1.2 %collective-permute-start.1 = (f32[3,16,128]{2,1,0:T(8,128)}, f32[3,16,128]{2,1,0:T(8,128)S(1)}, u32[]{:S(2)}, u32[]{:S(2)}) collective-permute-start(f32[3,16,128]{2,1,0:T(8,128)} %get-tuple-element.34), channel_id=1, source_target_pairs={{0,17},{1,16},{16,1},{17,0},{2,19},{3,18},{18,3},{19,2},{4,21},{5,... | collective-permute-start | bytes 73736 | tf_op jit(solution)/shard_map/ppermute | solution.py:655
  17.7 2.8 %collective-permute-done.1.refs_1_.others_1_ = f32[3,16,128]{2,1,0:T(8,128)S(1)} collective-permute-done((f32[3,16,128]{2,1,0:T(8,128)}, f32[3,16,128]{2,1,0:T(8,128)S(1)}, u32[]{:S(2)}, u32[]{:S(2)}) %collective-permute-start.1) | collective-permute-done | bytes 24608 | tf_op jit(solution)/shard_map/ppermute | solution.py:655
  20.5 1.2 %collective-permute-start = (f32[8,16,128]{2,1,0:T(8,128)}, f32[8,16,128]{2,1,0:T(8,128)S(1)}, u32[]{:S(2)}, u32[]{:S(2)}) collective-permute-start(f32[8,16,128]{2,1,0:T(8,128)} %get-tuple-element.33), channel_id=1, source_target_pairs={{0,16},{16,0},{1,17},{17,1},{2,18},{18,2},{3,19},{19,3},{4,20},{20... | collective-permute-start | bytes 196616 | tf_op jit(solution)/shard_map/ppermute | solution.py:45
  21.7 1.1 %copy-done.1 = bf16[3,32,16,256]{3,2,1,0:T(8,128)(2,1)S(1)} copy-done((bf16[3,32,16,256]{3,2,1,0:T(8,128)(2,1)S(1)}, bf16[3,32,16,256]{3,2,1,0:T(8,128)(2,1)}, u32[]{:S(2)}) %copy-start.1) | copy-done | bytes 786456
  22.8 1.1 %copy-done.3 = bf16[3,32,16,256]{3,2,1,0:T(8,128)(2,1)S(1)} copy-done((bf16[3,32,16,256]{3,2,1,0:T(8,128)(2,1)S(1)}, bf16[3,32,16,256]{3,2,1,0:T(8,128)(2,1)}, u32[]{:S(2)}) %copy-start.3) | copy-done | bytes 786456
  23.9 0.7 %copy-done.9 = f32[4]{0:T(128)S(1)} copy-done((f32[4]{0:T(128)S(1)}, f32[4]{0:T(128)}, u32[]{:S(2)}) %copy-start.9) | copy-done | bytes 40
  24.6 1.6 %prepare.1 = (f32[3,42,3,24,128]{4,3,2,1,0:T(8,128)S(1)}, f32[3,42,3,24,128]{4,3,2,1,0:T(8,128)S(1)}, f32[3,42,3,24,128]{4,3,2,1,0:T(8,128)S(1)}, f32[3,42,3,24,...) custom-call(f32[4]{0:T(128)S(1)} %copy-done.9, bf16[3,32,16,256]{3,2,1,0:T(8,128)(2,1)S(1)} %copy-done.1, ...), custom_call_target="tpu_custom_call" | custom-call | tf_op jit(solution)/shard_map/prepare/pallas_call | solution.py:703
  26.3 0.2 corners.1
  26.4 0.1 collective-permute-start.3
  26.5 4.7 %collective-permute-start.4 = (f32[35,8,128]{2,1,0:T(8,128)S(1)}, f32[35,8,128]{2,1,0:T(8,128)S(1)}, u32[]{:S(2)}, u32[]{:S(2)}) collective-permute-start(f32[35,8,128]{2,1,0:T(8,128)S(1)} %get-tuple-element.43), channel_id=1, source_target_pairs={{2,4},{4,2},{6,8},{8,6},{10,12},{12,10},{3,5},{5,3},{7,9},{9,7},{1... | collective-permute-start | bytes 430088 | tf_op jit(solution)/shard_map/ppermute | solution.py:45
  31.3 2.2 %planes.1 = (f32[3,42,3,24,128]{4,3,2,1,0:T(8,128)S(1)}, f32[3,42,3,24,128]{4,3,2,1,0:T(8,128)S(1)}, f32[3,42,3,24,128]{4,3,2,1,0:T(8,128)S(1)}, f32[3,42,3,24,1...) custom-call(f32[4]{0:T(128)S(1)} %copy-done.9, ...), custom_call_target="tpu_custom_call", output_to_operand_aliasing={{0}: (5, {}), {1}: (6, {}), {2}: (7, {}), {3}: (8, {}), {4}... | custom-call | tf_op jit(solution)/shard_map/planes/pallas_call | solution.py:726
  33.5 2.2 %rows.1 = (f32[3,42,3,24,128]{4,3,2,1,0:T(8,128)S(1)}, f32[3,42,3,24,128]{4,3,2,1,0:T(8,128)S(1)}, f32[3,42,3,24,128]{4,3,2,1,0:T(8,128)S(1)}, f32[3,42,3,24,128...) custom-call(f32[4]{0:T(128)S(1)} %copy-done.9, ...), custom_call_target="tpu_custom_call", output_to_operand_aliasing={{0}: (5, {}), {1}: (6, {}), {2}: (7, {}), {3}: (8, {}), {4}... | custom-call | tf_op jit(solution)/shard_map/rows/pallas_call | solution.py:737
  35.7 14.5 %window.1 = (f32[16,256]{1,0:T(8,128)S(1)}, f32[3,42,3,24,128]{4,3,2,1,0:T(8,128)S(1)}, f32[3,42,3,24,128]{4,3,2,1,0:T(8,128)S(1)}, f32[3,42,3,24,128]{4,3,2,1,0...) custom-call(f32[4]{0:T(128)S(1)} %copy-done.9, ...), custom_call_target="tpu_custom_call", output_to_operand_aliasing={{1}: (6, {}), {2}: (7, {}), {3}: (8, {}), {4}: (9, {}), {5}... | custom-call | tf_op jit(solution)/shard_map/window/pallas_call | solution.py:748
  50.3 0.2 collective-permute-start.8
  50.5 2.0 %dual.1 = f32[3,32,16,256]{3,2,1,0:T(8,128)} custom-call(f32[3,42,3,24,128]{4,3,2,1,0:T(8,128)S(1)} %get-tuple-element.62.third_e, f32[3,42,3,24,128]{4,3,2,1,0:T(8,128)S(1)} %get-tuple-element.63.dual_g), custom_call_target="tpu_custom_call" | custom-call | tf_op jit(solution)/shard_map/dual/pallas_call | solution.py:759
  52.5 0.4 collective-permute-done.8
  52.9 0.6 %add.3 = f32[16,256]{1,0:T(8,128)} add(f32[16,256]{1,0:T(8,128)S(1)} %get-tuple-element.61, f32[16,256]{1,0:T(8,128)S(1)} %collective-permute-done.8) | non-fusion elementwise | flops 4096 | bytes 49152 | tf_op jit(solution)/shard_map/add | solution.py:767
  (22 shorter events, 0.1 us)
Async XLA Ops:
  0.6 25.6 %copy-start.7 = (bf16[2,48,128]{2,1,0:T(8,128)(2,1)S(1)}, bf16[2,48,128]{2,1,0:T(8,128)(2,1)}, u32[]{:S(2)}) copy-start(bf16[2,48,128]{2,1,0:T(8,128)(2,1)} %constant.12.clone.refs_3_) | copy-start | bytes 73732
  0.6 30.6 %copy-start.4 = (s32[2,8,128]{2,1,0:T(8,128)S(1)}, s32[2,8,128]{2,1,0:T(8,128)}, u32[]{:S(2)}) copy-start(s32[2,8,128]{2,1,0:T(8,128)} %constant.14.clone.refs_6_.others_3_) | copy-start | bytes 24580
  6.4 0.9 %copy-start = (bf16[3,32,16,256]{3,2,1,0:T(8,128)(2,1)}, bf16[3,32,16,256]{3,2,1,0:T(8,128)(2,1)S(1)}, u32[]{:S(2)}) copy-start(bf16[3,32,16,256]{3,2,1,0:T(8,128)(2,1)S(1)} %get-tuple-element.36.fe) | copy-start | bytes 2359300
  7.3 0.9 %copy-start.2 = (bf16[3,32,16,256]{3,2,1,0:T(8,128)(2,1)}, bf16[3,32,16,256]{3,2,1,0:T(8,128)(2,1)S(1)}, u32[]{:S(2)}) copy-start(bf16[3,32,16,256]{3,2,1,0:T(8,128)(2,1)S(1)} %get-tuple-element.37.fh) | copy-start | bytes 2359300
  8.2 25.3 %collective-permute-start.5 = (f32[32,32,256]{2,1,0:T(8,128)}, f32[32,32,256]{2,1,0:T(8,128)S(1)}, u32[]{:S(2)}, u32[]{:S(2)}) collective-permute-start(f32[32,32,256]{2,1,0:T(8,128)} %get-tuple-element.44), channel_id=1, source_target_pairs={{0,2},{2,0},{4,6},{6,4},{8,10},{10,8},{12,14},{14,12},{1,3},{3,1},... | collective-permute-start | bytes 3145736 | tf_op jit(solution)/shard_map/ppermute | solution.py:45
  8.2 18.0 %collective-permute-start.2 = (f32[32,16,256]{2,1,0:T(8,128)}, f32[32,16,256]{2,1,0:T(8,128)S(1)}, u32[]{:S(2)}, u32[]{:S(2)}) collective-permute-start(f32[32,16,256]{2,1,0:T(8,128)} %get-tuple-element.35), channel_id=1, source_target_pairs={{0,1},{1,0},{2,3},{3,2},{4,5},{5,4},{6,7},{7,6},{8,9},{9,8},{10,11... | collective-permute-start | bytes 1572872 | tf_op jit(solution)/shard_map/ppermute | solution.py:45
  10.9 22.5 %collective-permute-start.6 = (f32[16,32,256]{2,1,0:T(8,128)}, f32[16,32,256]{2,1,0:T(8,128)S(1)}, u32[]{:S(2)}, u32[]{:S(2)}) collective-permute-start(f32[16,32,256]{2,1,0:T(8,128)} %get-tuple-element.45), channel_id=1, source_target_pairs={{2,4},{4,2},{6,8},{8,6},{10,12},{12,10},{3,5},{5,3},{7,9},{9,7},{1... | collective-permute-start | bytes 1572872 | tf_op jit(solution)/shard_map/ppermute | solution.py:45
  14.3 19.2 %collective-permute-start.7 = (f32[16,32,256]{2,1,0:T(8,128)}, f32[16,32,256]{2,1,0:T(8,128)S(1)}, u32[]{:S(2)}, u32[]{:S(2)}) collective-permute-start(f32[16,32,256]{2,1,0:T(8,128)} %get-tuple-element.46), channel_id=1, source_target_pairs={{2,4},{4,2},{6,8},{8,6},{10,12},{12,10},{3,5},{5,3},{7,9},{9,7},{1... | collective-permute-start | bytes 1572872 | tf_op jit(solution)/shard_map/ppermute | solution.py:45
  16.5 4.0 %collective-permute-start.1 = (f32[3,16,128]{2,1,0:T(8,128)}, f32[3,16,128]{2,1,0:T(8,128)S(1)}, u32[]{:S(2)}, u32[]{:S(2)}) collective-permute-start(f32[3,16,128]{2,1,0:T(8,128)} %get-tuple-element.34), channel_id=1, source_target_pairs={{0,17},{1,16},{16,1},{17,0},{2,19},{3,18},{18,3},{19,2},{4,21},{5,... | collective-permute-start | bytes 73736 | tf_op jit(solution)/shard_map/ppermute | solution.py:655
  20.5 5.8 %collective-permute-start = (f32[8,16,128]{2,1,0:T(8,128)}, f32[8,16,128]{2,1,0:T(8,128)S(1)}, u32[]{:S(2)}, u32[]{:S(2)}) collective-permute-start(f32[8,16,128]{2,1,0:T(8,128)} %get-tuple-element.33), channel_id=1, source_target_pairs={{0,16},{16,0},{1,17},{17,1},{2,18},{18,2},{3,19},{19,3},{4,20},{20... | collective-permute-start | bytes 196616 | tf_op jit(solution)/shard_map/ppermute | solution.py:45
  21.7 1.1 %copy-start.1 = (bf16[3,32,16,256]{3,2,1,0:T(8,128)(2,1)S(1)}, bf16[3,32,16,256]{3,2,1,0:T(8,128)(2,1)}, u32[]{:S(2)}) copy-start(bf16[3,32,16,256]{3,2,1,0:T(8,128)(2,1)} %copy-done) | copy-start | bytes 2359300
  22.8 1.1 %copy-start.3 = (bf16[3,32,16,256]{3,2,1,0:T(8,128)(2,1)S(1)}, bf16[3,32,16,256]{3,2,1,0:T(8,128)(2,1)}, u32[]{:S(2)}) copy-start(bf16[3,32,16,256]{3,2,1,0:T(8,128)(2,1)} %copy-done.2) | copy-start | bytes 2359300
  23.9 0.7 %copy-start.9 = (f32[4]{0:T(128)S(1)}, f32[4]{0:T(128)}, u32[]{:S(2)}) copy-start(f32[4]{0:T(128)} %inverse.7) | copy-start | bytes 52
  26.4 9.3 %collective-permute-start.3 = (f32[35,8,128]{2,1,0:T(8,128)S(1)}, f32[35,8,128]{2,1,0:T(8,128)S(1)}, u32[]{:S(2)}, u32[]{:S(2)}) collective-permute-start(f32[35,8,128]{2,1,0:T(8,128)S(1)} %get-tuple-element.42), channel_id=1, source_target_pairs={{0,2},{2,0},{4,6},{6,4},{8,10},{10,8},{12,14},{14,12},{1,3},{3,1},... | collective-permute-start | bytes 430088 | tf_op jit(solution)/shard_map/ppermute | solution.py:45
  26.5 9.2 %collective-permute-start.4 = (f32[35,8,128]{2,1,0:T(8,128)S(1)}, f32[35,8,128]{2,1,0:T(8,128)S(1)}, u32[]{:S(2)}, u32[]{:S(2)}) collective-permute-start(f32[35,8,128]{2,1,0:T(8,128)S(1)} %get-tuple-element.43), channel_id=1, source_target_pairs={{2,4},{4,2},{6,8},{8,6},{10,12},{12,10},{3,5},{5,3},{7,9},{9,7},{1... | collective-permute-start | bytes 430088 | tf_op jit(solution)/shard_map/ppermute | solution.py:45
  31.3 2.2 %copy-start.5 = (bf16[2,104,64]{2,1,0:T(8,128)(2,1)S(1)}, bf16[2,104,64]{2,1,0:T(8,128)(2,1)}, u32[]{:S(2)}) copy-start(bf16[2,104,64]{2,1,0:T(8,128)(2,1)} %constant.11.clone.placer) | copy-start | bytes 79876
  33.5 2.2 %copy-start.6 = (bf16[2,64,48]{2,1,0:T(8,128)(2,1)S(1)}, bf16[2,64,48]{2,1,0:T(8,128)(2,1)}, u32[]{:S(2)}) copy-start(bf16[2,64,48]{2,1,0:T(8,128)(2,1)} %constant.13.clone.others_2_) | copy-start | bytes 36868
  33.5 2.2 %copy-start.8 = (s32[16,256]{1,0:T(8,128)S(1)}, s32[16,256]{1,0:T(8,128)}, u32[]{:S(2)}) copy-start(s32[16,256]{1,0:T(8,128)} %height.1) | copy-start | bytes 49156
  50.3 2.7 %collective-permute-start.8 = (f32[16,256]{1,0:T(8,128)S(1)}, f32[16,256]{1,0:T(8,128)S(1)}, u32[]{:S(2)}, u32[]{:S(2)}) collective-permute-start(f32[16,256]{1,0:T(8,128)S(1)} %get-tuple-element.61), channel_id=1, source_target_pairs={{0,1},{1,0},{2,3},{3,2},{4,5},{5,4},{6,7},{7,6},{8,9},{9,8},{10,11... | collective-permute-start | bytes 49160 | tf_op jit(solution)/shard_map/ppermute | solution.py:45

commit v6 on v5

--- a/solution.py
+++ b/solution.py
@@ -281,7 +281,7 @@
     return spread(own_tiles, halo)
 
 
-def prepare_kernel(inverse, fe, fh, ae, ah, material, *state):
+def prepare_kernel(inverse, fe, fh, ae, ah, material, _, *state):
     depth, _, cols = material.shape
     refs = (fe, fh, ae, ah, material)
     zero = jnp.zeros((TILE, LANES), F32)
@@ -672,21 +672,21 @@
     x_messages = 1 if nx == 2 else 2
 
     chunk = TILE
-    x_shape = jax.ShapeDtypeStruct((chunk, rows, LANES), F32)
-    xz_shape = jax.ShapeDtypeStruct((WIDE, rows, LANES), F32)
-    y_shape = jax.ShapeDtypeStruct((depth, LAYERS, cols), F32)
+    x_shape = pltpu.VMEM((chunk, rows, LANES), F32)
+    xz_shape = pltpu.VMEM((WIDE, rows, LANES), F32)
+    y_shape = pltpu.VMEM((depth, LAYERS, cols), F32)
     fields = (forward_e, forward_h, adjoint_e, adjoint_h, material)
     in_hbm = pl.BlockSpec(memory_space=pltpu.HBM)
-    half_shape = jax.ShapeDtypeStruct((depth // 2, LAYERS, cols), F32)
+    half_shape = pltpu.VMEM((depth // 2, LAYERS, cols), F32)
     packed = pl.pallas_call(
         functools.partial(pack_kernel, x_messages),
         out_shape=[pltpu.VMEM(f.shape, f.dtype) for f in fields]
         + [x_shape] * x_messages + [xz_shape] * x_messages
-        + [jax.ShapeDtypeStruct((LAYERS, rows, cols), F32), y_shape, half_shape, half_shape],
+        + [pltpu.VMEM((LAYERS, rows, cols), F32), y_shape, half_shape, half_shape],
         in_specs=[in_hbm] * 5 + [vmem] * 2,
         out_specs=[vmem] * (2 * x_messages + 9),
         scratch_shapes=[pltpu.SemaphoreType.DMA((depth // TILE, COUNT))],
-        compiler_params=pltpu.CompilerParams(vmem_limit_bytes=60 * 1024 * 1024),
+        compiler_params=pltpu.CompilerParams(vmem_limit_bytes=56 * 1024 * 1024),
         name="pack",
     )(*fields, picker, table)
     fields, packed = packed[:5], packed[5:]
@@ -703,11 +703,11 @@
     state = pl.pallas_call(
         prepare_kernel,
         out_shape=state_shapes,
-        in_specs=[smem] + [vmem] * 5,
+        in_specs=[smem] + [vmem] * 5 + [anywhere],
         out_specs=[vmem] * 5,
-        compiler_params=params,
+        compiler_params=pltpu.CompilerParams(vmem_limit_bytes=8 * 1024 * 1024),
         name="prepare",
-    )(inv_permittivity, *fields)
+    )(inv_permittivity, *fields, ya)
 
     corner_tiles = LAYERS * WIDE // TILE * tiles + x_messages * (chunk + WIDE)
     corner_shape = jax.ShapeDtypeStruct((corner_tiles, TILE, LANES), F32)
@@ -716,7 +716,7 @@
         out_shape=[corner_shape, corner_shape],
         in_specs=[vmem] * (2 * x_messages + 2) + [anywhere],
         out_specs=[vmem] * 2,
-        compiler_params=params,
+        compiler_params=pltpu.CompilerParams(vmem_limit_bytes=8 * 1024 * 1024),
         name="corners",
     )(*xp, *xz, zr, corner_picking, state[4])
     corner_b = swap(corner_b, "gy", 1)
@@ -729,7 +729,7 @@
         in_specs=[smem] + [vmem] * (len(operands) + 4),
         out_specs=[vmem] * 5,
         input_output_aliases={len(operands) + n: n for n in range(5)},
-        compiler_params=params,
+        compiler_params=pltpu.CompilerParams(vmem_limit_bytes=8 * 1024 * 1024),
         name="planes",
     )(*operands, *state)
 
@@ -740,7 +740,7 @@
         in_specs=[smem] + [vmem] * (len(operands) + 4),
         out_specs=[vmem] * 5,
         input_output_aliases={len(operands) + n: n for n in range(5)},
-        compiler_params=params,
+        compiler_params=pltpu.CompilerParams(vmem_limit_bytes=8 * 1024 * 1024),
         name="rows",
     )(*operands, *state)
 
@@ -752,7 +752,7 @@
         out_specs=[vmem] * 7,
         input_output_aliases={len(operands) + n: 1 + n for n in range(5)},
         scratch_shapes=[pltpu.VMEM((3,) + block, F32)],
-        compiler_params=params,
+        compiler_params=pltpu.CompilerParams(vmem_limit_bytes=16 * 1024 * 1024),
         name="window",
     )(*operands, *state)
     grad, dual_g, third_e = results[0], results[4], results[6]
@@ -761,7 +761,7 @@
         out_shape=jax.ShapeDtypeStruct((3, depth, rows, cols), F32),
         in_specs=[vmem] * 2,
         out_specs=vmem,
-        compiler_params=params,
+        compiler_params=pltpu.CompilerParams(vmem_limit_bytes=8 * 1024 * 1024),
         name="dual",
     )(third_e, dual_g)
     return grad + swap(grad, "gz", 0), dual

time: 53.8 us -> 49.1 us (0.913)
  local copies, waits for them, and re-layouts: 4.74 us -> 2.7 us
  Pallas kernels: 28.4 us -> 27.3 us
  starting transfers between devices: 15.7 us -> 14.9 us
  waiting for transfers between devices: 3.22 us -> 2.54 us
    ppermute x1, waiting for transfers between devices: 2.76 us -> 0.24 us  [corner_swap(): return lax.ppermute(array, axes, pairs)]
    unnamed x20 -> x18, local copies, waits for them, and re-layouts: 4.74 us -> 2.7 us
    ppermute x8, waiting for transfers between devices: 0.46 us -> 2.31 us  [swap(): return lax.ppermute(array, axis, swap_pairs(lax.axis_size(axis), offset))]
    pallas_call x1, Pallas kernels: 5.71 us -> 4.23 us  [local(): pl.pallas_call(functools.partial(pack_kernel, x_messages), out_shape=[plt...]
    ppermute x1, starting transfers between devices: 1.2 us -> 0.01 us  [corner_swap(): return lax.ppermute(array, axes, pairs)]
  transfers between devices with their start and end apart: 9 -> 9, of which waited for: 2 -> 2; matrix products, arithmetic and copies ran while one was open for 0% -> 0% of each run, Pallas kernels for 15% -> 17%
where the time goes in v6:
time: 49.1 us; the launch traced here: 48.8 us
  Pallas kernels  27.3 us (56%)
  starting transfers between devices  14.9 us (30%)
  local copies, waits for them, and re-layouts  2.7 us (5%)
  waiting for transfers between devices  2.54 us (5%)
  between operations  0.83 us (2%)
  other arithmetic  0.61 us (1%)
    pallas_call x1, Pallas kernels, local(): pl.pallas_call(functools.partial(window_kernel, x_messages), out_shape=[j...  14.9 us
    ppermute x8, starting transfers between devices, swap(): return lax.ppermute(array, axis, swap_pairs(lax.axis_size(axis), offset))  14.9 us
    pallas_call x1, Pallas kernels, local(): pl.pallas_call(functools.partial(pack_kernel, x_messages), out_shape=[plt...  4.23 us
    unnamed x18, local copies, waits for them, and re-layouts  2.7 us
    ppermute x8, waiting for transfers between devices, swap(): return lax.ppermute(array, axis, swap_pairs(lax.axis_size(axis), offset))  2.31 us
    pallas_call x1, Pallas kernels, local(): pl.pallas_call(functools.partial(plane_kernel, x_messages), out_shape=sta...  2.19 us
    pallas_call x1, Pallas kernels, local(): pl.pallas_call(row_kernel, out_shape=state_shapes, in_specs=[smem] + [vme...  2.16 us
    pallas_call x1, Pallas kernels, local(): pl.pallas_call(dual_kernel, out_shape=jax.ShapeDtypeStruct((3, depth, row...  2.01 us
  transfers between devices with their start and end apart: 9, of which 2 were waited for; matrix products, arithmetic and copies ran while one was open for 0% of the time, Pallas kernels for 17%

profile of v6, /device:TPU:1, one launch (start us, length us, event | category | flops | bytes accessed | tf_op | source)
XLA Modules:
  0.0 48.8 jit_solution(477037283036465958)
XLA Ops:
  0.6 0.0 copy-start.5
  0.6 0.0 copy-start.2
  0.7 4.2 %pack.1 = (bf16[3,32,16,256]{3,2,1,0:T(8,128)(2,1)S(1)}, bf16[3,32,16,256]{3,2,1,0:T(8,128)(2,1)S(1)}, bf16[3,32,16,256]{3,2,1,0:T(8,128)(2,1)S(1)}, bf16[3,32,1...) custom-call(bf16[3,32,16,256]{3,2,1,0:T(8,128)(2,1)} %refs_0_.1, ...), custom_call_target="tpu_custom_call" | custom-call | tf_op jit(solution)/shard_map/pack/pallas_call | solution.py:681
  4.9 0.9 %copy-done = bf16[3,32,16,256]{3,2,1,0:T(8,128)(2,1)} copy-done((bf16[3,32,16,256]{3,2,1,0:T(8,128)(2,1)}, bf16[3,32,16,256]{3,2,1,0:T(8,128)(2,1)S(1)}, u32[]{:S(2)}) %copy-start) | copy-done | bytes 786456
  5.8 0.1 collective-permute-start.3
  5.8 2.7 %collective-permute-start.2 = (f32[32,16,256]{2,1,0:T(8,128)S(1)}, f32[32,16,256]{2,1,0:T(8,128)S(1)}, u32[]{:S(2)}, u32[]{:S(2)}) collective-permute-start(f32[32,16,256]{2,1,0:T(8,128)S(1)} %get-tuple-element.35), channel_id=1, source_target_pairs={{0,1},{1,0},{2,3},{3,2},{4,5},{5,4},{6,7},{7,6},{8,9},{9,8},{10,11... | collective-permute-start | bytes 1572872 | tf_op jit(solution)/shard_map/ppermute | solution.py:45
  8.5 3.4 %collective-permute-start.6 = (f32[16,32,256]{2,1,0:T(8,128)S(1)}, f32[16,32,256]{2,1,0:T(8,128)S(1)}, u32[]{:S(2)}, u32[]{:S(2)}) collective-permute-start(f32[16,32,256]{2,1,0:T(8,128)S(1)} %get-tuple-element.45), channel_id=1, source_target_pairs={{2,4},{4,2},{6,8},{8,6},{10,12},{12,10},{3,5},{5,3},{7,9},{9,7},{1... | collective-permute-start | bytes 1572872 | tf_op jit(solution)/shard_map/ppermute | solution.py:45
  11.9 2.2 %collective-permute-start.7 = (f32[16,32,256]{2,1,0:T(8,128)S(1)}, f32[16,32,256]{2,1,0:T(8,128)S(1)}, u32[]{:S(2)}, u32[]{:S(2)}) collective-permute-start(f32[16,32,256]{2,1,0:T(8,128)S(1)} %get-tuple-element.46), channel_id=1, source_target_pairs={{2,4},{4,2},{6,8},{8,6},{10,12},{12,10},{3,5},{5,3},{7,9},{9,7},{1... | collective-permute-start | bytes 1572872 | tf_op jit(solution)/shard_map/ppermute | solution.py:45
  14.1 1.3 %collective-permute-start = (f32[8,16,128]{2,1,0:T(8,128)S(1)}, f32[8,16,128]{2,1,0:T(8,128)S(1)}, u32[]{:S(2)}, u32[]{:S(2)}) collective-permute-start(f32[8,16,128]{2,1,0:T(8,128)S(1)} %get-tuple-element.33), channel_id=1, source_target_pairs={{0,16},{16,0},{1,17},{17,1},{2,18},{18,2},{3,19},{19,3},{4,20},{20... | collective-permute-start | bytes 196616 | tf_op jit(solution)/shard_map/ppermute | solution.py:45
  15.4 0.0 collective-permute-start.1
  15.4 1.1 %copy-done.1 = bf16[3,32,16,256]{3,2,1,0:T(8,128)(2,1)S(1)} copy-done((bf16[3,32,16,256]{3,2,1,0:T(8,128)(2,1)S(1)}, bf16[3,32,16,256]{3,2,1,0:T(8,128)(2,1)}, u32[]{:S(2)}) %copy-start.1) | copy-done | bytes 786456
  16.5 0.7 %copy-done.7 = f32[4]{0:T(128)S(1)} copy-done((f32[4]{0:T(128)S(1)}, f32[4]{0:T(128)}, u32[]{:S(2)}) %copy-start.7) | copy-done | bytes 40
  17.2 1.6 %prepare.1 = (f32[3,42,3,24,128]{4,3,2,1,0:T(8,128)S(1)}, f32[3,42,3,24,128]{4,3,2,1,0:T(8,128)S(1)}, f32[3,42,3,24,128]{4,3,2,1,0:T(8,128)S(1)}, f32[3,42,3,24,...) custom-call(f32[4]{0:T(128)S(1)} %copy-done.7, bf16[3,32,16,256]{3,2,1,0:T(8,128)(2,1)S(1)} %get-tuple-element.36.fe, ...), custom_call_target="tpu_custom_call" | custom-call | tf_op jit(solution)/shard_map/prepare/pallas_call | solution.py:703
  18.8 0.2 collective-permute-done.1.refs_1_.others_1_
  19.1 2.3 %collective-permute-done.2.refs_2_.others_2_ = f32[32,16,256]{2,1,0:T(8,128)S(1)} collective-permute-done((f32[32,16,256]{2,1,0:T(8,128)S(1)}, f32[32,16,256]{2,1,0:T(8,128)S(1)}, u32[]{:S(2)}, u32[]{:S(2)}) %collective-permute-start.2) | collective-permute-done | bytes 524320 | tf_op jit(solution)/shard_map/ppermute | solution.py:45
  21.4 0.2 corners.1
  21.5 0.6 %collective-permute-start.4 = (f32[35,8,128]{2,1,0:T(8,128)S(1)}, f32[35,8,128]{2,1,0:T(8,128)S(1)}, u32[]{:S(2)}, u32[]{:S(2)}) collective-permute-start(f32[35,8,128]{2,1,0:T(8,128)S(1)} %get-tuple-element.43), channel_id=1, source_target_pairs={{0,2},{2,0},{4,6},{6,4},{8,10},{10,8},{12,14},{14,12},{1,3},{3,1},... | collective-permute-start | bytes 430088 | tf_op jit(solution)/shard_map/ppermute | solution.py:45
  22.2 3.3 %collective-permute-start.5 = (f32[35,8,128]{2,1,0:T(8,128)S(1)}, f32[35,8,128]{2,1,0:T(8,128)S(1)}, u32[]{:S(2)}, u32[]{:S(2)}) collective-permute-start(f32[35,8,128]{2,1,0:T(8,128)S(1)} %get-tuple-element.44), channel_id=1, source_target_pairs={{2,4},{4,2},{6,8},{8,6},{10,12},{12,10},{3,5},{5,3},{7,9},{9,7},{1... | collective-permute-start | bytes 430088 | tf_op jit(solution)/shard_map/ppermute | solution.py:45
  25.5 2.2 %planes.1 = (f32[3,42,3,24,128]{4,3,2,1,0:T(8,128)S(1)}, f32[3,42,3,24,128]{4,3,2,1,0:T(8,128)S(1)}, f32[3,42,3,24,128]{4,3,2,1,0:T(8,128)S(1)}, f32[3,42,3,24,1...) custom-call(f32[4]{0:T(128)S(1)} %copy-done.8, ...), custom_call_target="tpu_custom_call", output_to_operand_aliasing={{0}: (5, {}), {1}: (6, {}), {2}: (7, {}), {3}: (8, {}), {4}... | custom-call | tf_op jit(solution)/shard_map/planes/pallas_call | solution.py:726
  27.8 2.2 %rows.1 = (f32[3,42,3,24,128]{4,3,2,1,0:T(8,128)S(1)}, f32[3,42,3,24,128]{4,3,2,1,0:T(8,128)S(1)}, f32[3,42,3,24,128]{4,3,2,1,0:T(8,128)S(1)}, f32[3,42,3,24,128...) custom-call(f32[4]{0:T(128)S(1)} %copy-done.8, ...), custom_call_target="tpu_custom_call", output_to_operand_aliasing={{0}: (5, {}), {1}: (6, {}), {2}: (7, {}), {3}: (8, {}), {4}... | custom-call | tf_op jit(solution)/shard_map/rows/pallas_call | solution.py:737
  30.0 14.9 %window.1 = (f32[16,256]{1,0:T(8,128)S(1)}, f32[3,42,3,24,128]{4,3,2,1,0:T(8,128)S(1)}, f32[3,42,3,24,128]{4,3,2,1,0:T(8,128)S(1)}, f32[3,42,3,24,128]{4,3,2,1,0...) custom-call(f32[4]{0:T(128)S(1)} %copy-done.8, ...), custom_call_target="tpu_custom_call", output_to_operand_aliasing={{1}: (6, {}), {2}: (7, {}), {3}: (8, {}), {4}: (9, {}), {5}... | custom-call | tf_op jit(solution)/shard_map/window/pallas_call | solution.py:748
  44.9 1.3 %collective-permute-start.8 = (f32[16,256]{1,0:T(8,128)S(1)}, f32[16,256]{1,0:T(8,128)S(1)}, u32[]{:S(2)}, u32[]{:S(2)}) collective-permute-start(f32[16,256]{1,0:T(8,128)S(1)} %get-tuple-element.61), channel_id=1, source_target_pairs={{0,1},{1,0},{2,3},{3,2},{4,5},{5,4},{6,7},{7,6},{8,9},{9,8},{10,11... | collective-permute-start | bytes 49160 | tf_op jit(solution)/shard_map/ppermute | solution.py:45
  46.2 2.0 %dual.1 = f32[3,32,16,256]{3,2,1,0:T(8,128)} custom-call(f32[3,42,3,24,128]{4,3,2,1,0:T(8,128)S(1)} %get-tuple-element.62.third_e, f32[3,42,3,24,128]{4,3,2,1,0:T(8,128)S(1)} %get-tuple-element.63.dual_g), custom_call_target="tpu_custom_call" | custom-call | tf_op jit(solution)/shard_map/dual/pallas_call | solution.py:759
  48.2 0.6 %add.3 = f32[16,256]{1,0:T(8,128)} add(f32[16,256]{1,0:T(8,128)S(1)} %get-tuple-element.61, f32[16,256]{1,0:T(8,128)S(1)} %collective-permute-done.8) | non-fusion elementwise | flops 4096 | bytes 49152 | tf_op jit(solution)/shard_map/add | solution.py:767
  (20 shorter events, 0.1 us)
Async XLA Ops:
  0.6 20.7 %copy-start.5 = (bf16[2,48,128]{2,1,0:T(8,128)(2,1)S(1)}, bf16[2,48,128]{2,1,0:T(8,128)(2,1)}, u32[]{:S(2)}) copy-start(bf16[2,48,128]{2,1,0:T(8,128)(2,1)} %constant.12.clone.refs_3_) | copy-start | bytes 73732
  0.6 24.9 %copy-start.2 = (s32[2,8,128]{2,1,0:T(8,128)S(1)}, s32[2,8,128]{2,1,0:T(8,128)}, u32[]{:S(2)}) copy-start(s32[2,8,128]{2,1,0:T(8,128)} %constant.14.clone.refs_6_.others_3_) | copy-start | bytes 24580
  0.7 24.8 %copy-start.8 = (f32[4]{0:T(128)S(1)}, f32[4]{0:T(128)}, u32[]{:S(2)}) copy-start(f32[4]{0:T(128)} %inverse.7) | copy-start | bytes 52
  4.9 0.9 %copy-start = (bf16[3,32,16,256]{3,2,1,0:T(8,128)(2,1)}, bf16[3,32,16,256]{3,2,1,0:T(8,128)(2,1)S(1)}, u32[]{:S(2)}) copy-start(bf16[3,32,16,256]{3,2,1,0:T(8,128)(2,1)S(1)} %get-tuple-element.38.ae) | copy-start | bytes 2359300
  5.8 9.6 %collective-permute-start.3 = (f32[32,32,256]{2,1,0:T(8,128)S(1)}, f32[32,32,256]{2,1,0:T(8,128)S(1)}, u32[]{:S(2)}, u32[]{:S(2)}) collective-permute-start(f32[32,32,256]{2,1,0:T(8,128)S(1)} %get-tuple-element.41), channel_id=1, source_target_pairs={{0,2},{2,0},{4,6},{6,4},{8,10},{10,8},{12,14},{14,12},{1,3},{3,1},... | collective-permute-start | bytes 3145736 | tf_op jit(solution)/shard_map/ppermute | solution.py:45
  5.8 15.5 %collective-permute-start.2 = (f32[32,16,256]{2,1,0:T(8,128)S(1)}, f32[32,16,256]{2,1,0:T(8,128)S(1)}, u32[]{:S(2)}, u32[]{:S(2)}) collective-permute-start(f32[32,16,256]{2,1,0:T(8,128)S(1)} %get-tuple-element.35), channel_id=1, source_target_pairs={{0,1},{1,0},{2,3},{3,2},{4,5},{5,4},{6,7},{7,6},{8,9},{9,8},{10,11... | collective-permute-start | bytes 1572872 | tf_op jit(solution)/shard_map/ppermute | solution.py:45
  8.5 19.2 %collective-permute-start.6 = (f32[16,32,256]{2,1,0:T(8,128)S(1)}, f32[16,32,256]{2,1,0:T(8,128)S(1)}, u32[]{:S(2)}, u32[]{:S(2)}) collective-permute-start(f32[16,32,256]{2,1,0:T(8,128)S(1)} %get-tuple-element.45), channel_id=1, source_target_pairs={{2,4},{4,2},{6,8},{8,6},{10,12},{12,10},{3,5},{5,3},{7,9},{9,7},{1... | collective-permute-start | bytes 1572872 | tf_op jit(solution)/shard_map/ppermute | solution.py:45
  11.9 15.8 %collective-permute-start.7 = (f32[16,32,256]{2,1,0:T(8,128)S(1)}, f32[16,32,256]{2,1,0:T(8,128)S(1)}, u32[]{:S(2)}, u32[]{:S(2)}) collective-permute-start(f32[16,32,256]{2,1,0:T(8,128)S(1)} %get-tuple-element.46), channel_id=1, source_target_pairs={{2,4},{4,2},{6,8},{8,6},{10,12},{12,10},{3,5},{5,3},{7,9},{9,7},{1... | collective-permute-start | bytes 1572872 | tf_op jit(solution)/shard_map/ppermute | solution.py:45
  14.1 5.0 %collective-permute-start = (f32[8,16,128]{2,1,0:T(8,128)S(1)}, f32[8,16,128]{2,1,0:T(8,128)S(1)}, u32[]{:S(2)}, u32[]{:S(2)}) collective-permute-start(f32[8,16,128]{2,1,0:T(8,128)S(1)} %get-tuple-element.33), channel_id=1, source_target_pairs={{0,16},{16,0},{1,17},{17,1},{2,18},{18,2},{3,19},{19,3},{4,20},{20... | collective-permute-start | bytes 196616 | tf_op jit(solution)/shard_map/ppermute | solution.py:45
  15.4 3.7 %collective-permute-start.1 = (f32[3,16,128]{2,1,0:T(8,128)S(1)}, f32[3,16,128]{2,1,0:T(8,128)S(1)}, u32[]{:S(2)}, u32[]{:S(2)}) collective-permute-start(f32[3,16,128]{2,1,0:T(8,128)S(1)} %get-tuple-element.34), channel_id=1, source_target_pairs={{0,17},{1,16},{16,1},{17,0},{2,19},{3,18},{18,3},{19,2},{4,21},{5,... | collective-permute-start | bytes 73736 | tf_op jit(solution)/shard_map/ppermute | solution.py:655
  15.4 1.1 %copy-start.1 = (bf16[3,32,16,256]{3,2,1,0:T(8,128)(2,1)S(1)}, bf16[3,32,16,256]{3,2,1,0:T(8,128)(2,1)}, u32[]{:S(2)}) copy-start(bf16[3,32,16,256]{3,2,1,0:T(8,128)(2,1)} %copy-done) | copy-start | bytes 2359300
  16.5 0.7 %copy-start.7 = (f32[4]{0:T(128)S(1)}, f32[4]{0:T(128)}, u32[]{:S(2)}) copy-start(f32[4]{0:T(128)} %inverse.7) | copy-start | bytes 52
  21.5 8.4 %collective-permute-start.4 = (f32[35,8,128]{2,1,0:T(8,128)S(1)}, f32[35,8,128]{2,1,0:T(8,128)S(1)}, u32[]{:S(2)}, u32[]{:S(2)}) collective-permute-start(f32[35,8,128]{2,1,0:T(8,128)S(1)} %get-tuple-element.43), channel_id=1, source_target_pairs={{0,2},{2,0},{4,6},{6,4},{8,10},{10,8},{12,14},{14,12},{1,3},{3,1},... | collective-permute-start | bytes 430088 | tf_op jit(solution)/shard_map/ppermute | solution.py:45
  22.2 7.8 %collective-permute-start.5 = (f32[35,8,128]{2,1,0:T(8,128)S(1)}, f32[35,8,128]{2,1,0:T(8,128)S(1)}, u32[]{:S(2)}, u32[]{:S(2)}) collective-permute-start(f32[35,8,128]{2,1,0:T(8,128)S(1)} %get-tuple-element.44), channel_id=1, source_target_pairs={{2,4},{4,2},{6,8},{8,6},{10,12},{12,10},{3,5},{5,3},{7,9},{9,7},{1... | collective-permute-start | bytes 430088 | tf_op jit(solution)/shard_map/ppermute | solution.py:45
  25.5 2.2 %copy-start.3 = (bf16[2,104,64]{2,1,0:T(8,128)(2,1)S(1)}, bf16[2,104,64]{2,1,0:T(8,128)(2,1)}, u32[]{:S(2)}) copy-start(bf16[2,104,64]{2,1,0:T(8,128)(2,1)} %constant.11.clone.placer) | copy-start | bytes 79876
  27.8 2.2 %copy-start.4 = (bf16[2,64,48]{2,1,0:T(8,128)(2,1)S(1)}, bf16[2,64,48]{2,1,0:T(8,128)(2,1)}, u32[]{:S(2)}) copy-start(bf16[2,64,48]{2,1,0:T(8,128)(2,1)} %constant.13.clone.others_2_) | copy-start | bytes 36868
  27.8 2.2 %copy-start.6 = (s32[16,256]{1,0:T(8,128)S(1)}, s32[16,256]{1,0:T(8,128)}, u32[]{:S(2)}) copy-start(s32[16,256]{1,0:T(8,128)} %height.1) | copy-start | bytes 49156
  44.9 3.4 %collective-permute-start.8 = (f32[16,256]{1,0:T(8,128)S(1)}, f32[16,256]{1,0:T(8,128)S(1)}, u32[]{:S(2)}, u32[]{:S(2)}) collective-permute-start(f32[16,256]{1,0:T(8,128)S(1)} %get-tuple-element.61), channel_id=1, source_target_pairs={{0,1},{1,0},{2,3},{3,2},{4,5},{5,4},{6,7},{7,6},{8,9},{9,8},{10,11... | collective-permute-start | bytes 49160 | tf_op jit(solution)/shard_map/ppermute | solution.py:45

commit v7 on v6

--- a/solution.py
+++ b/solution.py
@@ -34,6 +34,17 @@
     return [(c, k, length + k) for c, d in enumerate(HIGH_DEPTH) for k in range(d)]
 
 
+def planes_to_next(depth):
+    return [e for e in layers_to_next(depth) if not (e[0] in (FH + 2, AH + 2) and -e[2] == LOW_DEPTH[e[0]])]
+
+
+def planes_to_previous(depth):
+    return [
+        e for e in layers_to_previous(depth)
+        if not (e[0] in (FE + 2, AE + 2) and e[1] == HIGH_DEPTH[e[0]] - 1)
+    ]
+
+
 def swap_pairs(length, offset):
     pairs = []
     for i in range(offset, length - 1, 2):
@@ -137,7 +148,7 @@
     copies = []
     for group in range(groups):
         planes = pl.ds(group * TILE, TILE)
-        parts = [(n, c, planes) for n in range(4) for c in range(3)] + [(4, planes)]
+        parts = [(n, slice(None), planes) for n in range(4)] + [(4, planes)]
         copies.append([
             pltpu.make_async_copy(
                 whole[n].at[at], fields[n].at[at], arrived.at[group, number]
@@ -191,11 +202,11 @@
 
     @pl.when(odd_z == 0)
     def _():
-        edges(layers_to_next(depth))
+        edges(planes_to_next(depth))
 
     @pl.when(odd_z == 1)
     def _():
-        edges(layers_to_previous(depth))
+        edges(planes_to_previous(depth))
 
 
 def edge_rows(array, to_next):
@@ -211,9 +222,11 @@
 def corner_kernel(x_messages, *refs):
     arrays = refs[:2 * x_messages]
     zr, picker, _, a_out, b_out = refs[2 * x_messages:]
-    _, rows, cols = zr.shape
+    sent, rows, cols = zr.shape
     odd_y = place_on("gy")[1]
-    arrived = zr[...].reshape(LAYERS * rows, cols).astype(BF16)
+    arrived = zr[...].reshape(sent * rows, cols).astype(BF16)
+    rest = jnp.zeros(((LAYERS - sent) * rows, cols), BF16)
+    arrived = jnp.concatenate([arrived, rest], axis=0)
     picked = [
         jnp.dot(picker[odd_y], arrived[n:n + LANES], preferred_element_type=F32)
         for n in range(0, LAYERS * rows, LANES)
@@ -281,7 +294,7 @@
     return spread(own_tiles, halo)
 
 
-def prepare_kernel(inverse, fe, fh, ae, ah, material, _, *state):
+def prepare_kernel(inverse, fe, fh, ae, ah, material, table, _, matrices, *state):
     depth, _, cols = material.shape
     refs = (fe, fh, ae, ah, material)
     zero = jnp.zeros((TILE, LANES), F32)
@@ -298,35 +311,61 @@
         return 0
 
     lax.fori_loop(0, depth // 4, planes, 0)
-
-
-def column_matrix(table, odd_x, number, c, group):
-    way = 1 - (odd_x ^ number)
-    of_field, of_target, of_group = (table[way, k:k + 1, :] for k in (0, 2, 3))
-    chosen = (of_field == c) & (of_group == group) & (of_target == row_of((LANES, LANES)))
-    return jnp.where(chosen, SCALE[c], 0.0).astype(BF16)
-
-
-def columns_of(table, odd_x, c, group, arrays, inverse):
+    column_matrices(table, place_on("gx")[1], matrices)
+
+
+def column_matrices(table, odd_x, out):
+    target = row_of((LANES, LANES))
+    for number in range(out.shape[0]):
+        way = 1 - (odd_x ^ number)
+        of_field, of_target, of_group = (table[way, k:k + 1, :] for k in (0, 2, 3))
+        lands = of_target == target
+        for c in range(COUNT):
+            for pair in range(out.shape[2]):
+                for n in range(2):
+                    chosen = jnp.where((of_field == c) & (of_group == 2 * pair + n), SCALE[c], 0.0)
+                    matrix = jnp.where(lands, chosen, 0.0).astype(BF16)
+                    out[number, c, pair, n * LANES:(n + 1) * LANES] = matrix
+
+
+def columns_of(matrices, c, arrays, inverse, pick):
     total = None
     for number, array in enumerate(arrays):
         part = lax.dot_general(
-            array, column_matrix(table, odd_x, number, c, group), (((1,), (1,)), ((), ())),
-            preferred_element_type=F32,
+            array, pick(matrices, number, c), (((1,), (1,)), ((), ())), preferred_element_type=F32
         )
         total = part if total is None else total + part
     return weight(total, inverse) if c == KAPPA else total
 
 
+def place_columns(matrices, own_arrays, halo_arrays, inverse, depth, odd_z, put):
+    groups = depth // TILE
+    begin_halo = jnp.where(odd_z == 1, BEFORE - WIDE, BEFORE + depth)
+    halo_group = jnp.where(odd_z == 1, groups - 1, 0)
+    half = pl.ds(pl.multiple_of(lax.rem(halo_group, 2) * LANES, LANES), LANES)
+    for c in range(COUNT):
+        for pair in range(groups // 2):
+            found = columns_of(
+                matrices, c, own_arrays, inverse, lambda m, number, c: m[number, c, pair]
+            )
+            for n in range(2):
+                put(c, BEFORE + (2 * pair + n) * TILE, TILE, lane_tile(found, n))
+        found = columns_of(
+            matrices, c, halo_arrays, inverse,
+            lambda m, number, c: m[number, c, halo_group // 2, half],
+        )
+        put(c, begin_halo, WIDE, found)
+
+
 def plane_kernel(x_messages, inverse, *others):
     xp, xz = others[:x_messages], others[x_messages:2 * x_messages]
-    zr, table = others[2 * x_messages:2 * x_messages + 2]
+    zr, matrices = others[2 * x_messages:2 * x_messages + 2]
     state = others[2 * x_messages + 7:]
     _, rows, cols = zr.shape
     own = cols // LANES
     blocks = rows // TILE + 1
     depth = state[0].shape[1] - BEFORE - AFTER
-    odd_x, odd_z = (place_on(axis)[1] for axis in ("gx", "gz"))
+    odd_z = place_on("gz")[1]
     zero = jnp.zeros((TILE, LANES), F32)
 
     for t in range(own + 1):
@@ -335,23 +374,18 @@
                 for ref, slot in zip(state, (depth + BEFORE, BEFORE - 1) * 2):
                     ref[c, slot, t, rows_at(b)] = zero
 
-    groups = depth // TILE
-    begin_halo = jnp.where(odd_z == 1, BEFORE - WIDE, BEFORE + depth)
-    halo_group = jnp.where(odd_z == 1, groups - 1, 0)
     wides = []
     for array in (*xp, *xz):
         parts = []
         for k in range(array.shape[0]):
             parts += spread(row_tiles(array[k]), zero)
         wides.append(jnp.concatenate(parts, axis=0).astype(BF16))
-    for c in range(COUNT):
-        ref, to = state[c // 3], c % 3
-        for group in range(groups):
-            found = columns_of(table, odd_x, c, group, wides[:x_messages], inverse)
-            found = found.reshape(TILE, blocks * TILE, LANES)
-            ref[to, pl.ds(BEFORE + group * TILE, TILE), own] = found
-        found = columns_of(table, odd_x, c, halo_group, wides[x_messages:], inverse)
-        ref[to, pl.ds(begin_halo, WIDE), own] = found.reshape(WIDE, blocks * TILE, LANES)
+
+    def put(c, slot, count, value):
+        value = value.reshape(count, blocks * TILE, LANES)
+        state[c // 3][c % 3, pl.ds(slot, count), own] = value
+
+    place_columns(matrices, wides[:x_messages], wides[x_messages:], inverse, depth, odd_z, put)
 
     def halo_planes(layers):
         for n, (c, _, position) in enumerate(layers):
@@ -362,11 +396,11 @@
 
     @pl.when(odd_z == 0)
     def _():
-        halo_planes(layers_to_previous(depth))
+        halo_planes(planes_to_previous(depth))
 
     @pl.when(odd_z == 1)
     def _():
-        halo_planes(layers_to_next(depth))
+        halo_planes(planes_to_next(depth))
 
 
 def first_slot(count, depth, odd_z):
@@ -451,7 +485,7 @@
     own = ya.shape[2] // LANES
     height = state[0].shape[3]
     below, above = pl.ds(0, SHIFT), pl.ds(height - SHIFT, SHIFT)
-    at_once = 4
+    at_once = 8
 
     def place(array, start):
         def step(number, _):
@@ -479,7 +513,7 @@
 
 
 def window_kernel(x_messages, inverse, height, *others):
-    corner_a, corner_b, corner_placing, table = others[:4]
+    corner_a, corner_b, corner_placing, matrices = others[:4]
     grad_out, forward_e, forward_g, dual_e, dual_g, factor, third_e, second_e = others[9:]
     rows, cols = height.shape
     depth = factor.shape[1] - BEFORE - AFTER
@@ -501,27 +535,20 @@
                 third_e[c, depth + BEFORE, t, rows_at(b)] = zero
 
     corner_tiles = LAYERS * WIDE // TILE
-    groups = depth // TILE
-    begin_halo = jnp.where(odd_z == 1, BEFORE - WIDE, BEFORE + depth)
-    halo_group = jnp.where(odd_z == 1, groups - 1, 0)
     at = own * corner_tiles
     wides = []
     for count in [TILE] * x_messages + [WIDE] * x_messages:
         parts = [corner_a[at + k] + corner_b[at + k] for k in range(count)]
         wides.append(jnp.concatenate(parts, axis=0).astype(BF16))
         at += count
-    for c in range(COUNT):
-        ref, to = state[c // 3], c % 3
-        for group in range(groups + 1):
-            if group < groups:
-                found = columns_of(table, odd_x, c, group, wides[:x_messages], inverse)
-                slots = pl.ds(BEFORE + group * TILE, TILE)
-            else:
-                found = columns_of(table, odd_x, c, halo_group, wides[x_messages:], inverse)
-                slots = pl.ds(begin_halo, WIDE)
-            found = found.reshape(-1, TILE, LANES)
-            ref[to, slots, own, below] = found[:, :SHIFT]
-            ref[to, slots, own, above] = found[:, SHIFT:]
+
+    def put(c, slot, count, value):
+        value = value.reshape(count, TILE, LANES)
+        slots = pl.ds(slot, count)
+        state[c // 3][c % 3, slots, own, below] = value[:, :SHIFT]
+        state[c // 3][c % 3, slots, own, above] = value[:, SHIFT:]
+
+    place_columns(matrices, wides[:x_messages], wides[x_messages:], inverse, depth, odd_z, put)
 
     group = LANES // rows
     group_tiles = group * WIDE // TILE
@@ -546,11 +573,11 @@
 
     @pl.when(odd_z == 0)
     def _():
-        halo_planes(layers_to_previous(depth))
+        halo_planes(planes_to_previous(depth))
 
     @pl.when(odd_z == 1)
     def _():
-        halo_planes(layers_to_next(depth))
+        halo_planes(planes_to_next(depth))
 
     keep_row = jnp.where((row < SHIFT) & (at_y == 0), 0.0, 1.0)
     keep_lane = jnp.where((lane >= LANES // 2) & (at_x == 0), 0.0, 1.0)
@@ -682,11 +709,11 @@
         functools.partial(pack_kernel, x_messages),
         out_shape=[pltpu.VMEM(f.shape, f.dtype) for f in fields]
         + [x_shape] * x_messages + [xz_shape] * x_messages
-        + [pltpu.VMEM((LAYERS, rows, cols), F32), y_shape, half_shape, half_shape],
+        + [pltpu.VMEM((len(planes_to_next(depth)), rows, cols), F32), y_shape, half_shape, half_shape],
         in_specs=[in_hbm] * 5 + [vmem] * 2,
         out_specs=[vmem] * (2 * x_messages + 9),
-        scratch_shapes=[pltpu.SemaphoreType.DMA((depth // TILE, COUNT))],
-        compiler_params=pltpu.CompilerParams(vmem_limit_bytes=56 * 1024 * 1024),
+        scratch_shapes=[pltpu.SemaphoreType.DMA((depth // TILE, 5))],
+        compiler_params=pltpu.CompilerParams(vmem_limit_bytes=54 * 1024 * 1024),
         name="pack",
     )(*fields, picker, table)
     fields, packed = packed[:5], packed[5:]
@@ -700,14 +727,15 @@
 
     block = (BEFORE + depth + AFTER, tiles + 1, (rows // TILE + 1) * TILE, LANES)
     state_shapes = [pltpu.VMEM((3,) + block, F32)] * 4 + [pltpu.VMEM((1,) + block, F32)]
-    state = pl.pallas_call(
+    matrix_shape = pltpu.VMEM((x_messages, COUNT, depth // TILE // 2, 2 * LANES, LANES), BF16)
+    matrices, *state = pl.pallas_call(
         prepare_kernel,
-        out_shape=state_shapes,
-        in_specs=[smem] + [vmem] * 5 + [anywhere],
-        out_specs=[vmem] * 5,
+        out_shape=[matrix_shape] + state_shapes,
+        in_specs=[smem] + [vmem] * 6 + [anywhere],
+        out_specs=[vmem] * 6,
         compiler_params=pltpu.CompilerParams(vmem_limit_bytes=8 * 1024 * 1024),
         name="prepare",
-    )(inv_permittivity, *fields, ya)
+    )(inv_permittivity, *fields, table, ya)
 
     corner_tiles = LAYERS * WIDE // TILE * tiles + x_messages * (chunk + WIDE)
     corner_shape = jax.ShapeDtypeStruct((corner_tiles, TILE, LANES), F32)
@@ -722,7 +750,7 @@
     corner_b = swap(corner_b, "gy", 1)
     corner_a = swap(corner_a, "gy", 0)
 
-    operands = (inv_permittivity, *xp, *xz, zr, table)
+    operands = (inv_permittivity, *xp, *xz, zr, matrices)
     state = pl.pallas_call(
         functools.partial(plane_kernel, x_messages),
         out_shape=state_shapes,
@@ -744,7 +772,7 @@
         name="rows",
     )(*operands, *state)
 
-    operands = (inv_permittivity, height, corner_a, corner_b, corner_placing, table)
+    operands = (inv_permittivity, height, corner_a, corner_b, corner_placing, matrices)
     results = pl.pallas_call(
         functools.partial(window_kernel, x_messages),
         out_shape=[jax.ShapeDtypeStruct((rows, cols), F32), *state_shapes, state_shapes[0]],

time: 49.1 us -> 47 us (0.957)
  local copies, waits for them, and re-layouts: 2.7 us -> 1.38 us
  Pallas kernels: 27.3 us -> 26.8 us
    unnamed x18 -> x12, local copies, waits for them, and re-layouts: 2.7 us -> 1.38 us
    pallas_call x1, Pallas kernels: 4.23 us -> 5.01 us  [local(): pl.pallas_call(functools.partial(pack_kernel, x_messages), out_shape=[plt...]
    ppermute x8, waiting for transfers between devices: 2.31 us -> 1.74 us  [swap(): return lax.ppermute(array, axis, swap_pairs(lax.axis_size(axis), offset))]
    pallas_call x1, Pallas kernels: 2.16 us -> 1.63 us  [local(): pl.pallas_call(row_kernel, out_shape=state_shapes, in_specs=[smem] + [vme...]
    pallas_call x1, Pallas kernels: 14.9 us -> 14.4 us  [local(): pl.pallas_call(functools.partial(window_kernel, x_messages), out_shape=[j...]
  transfers between devices with their start and end apart: 9 -> 9, of which waited for: 2 -> 2; matrix products, arithmetic and copies ran while one was open for 0% -> 0% of each run, Pallas kernels for 17% -> 16%
where the time goes in v7:
time: 47 us; the launch traced here: 46.7 us
  Pallas kernels  26.8 us (57%)
  starting transfers between devices  15 us (32%)
  waiting for transfers between devices  2.19 us (5%)
  local copies, waits for them, and re-layouts  1.38 us (3%)
  between operations  0.8 us (2%)
  other arithmetic  0.61 us (1%)
    ppermute x8, starting transfers between devices, swap(): return lax.ppermute(array, axis, swap_pairs(lax.axis_size(axis), offset))  15 us
    pallas_call x1, Pallas kernels, local(): pl.pallas_call(functools.partial(window_kernel, x_messages), out_shape=[j...  14.4 us
    pallas_call x1, Pallas kernels, local(): pl.pallas_call(functools.partial(pack_kernel, x_messages), out_shape=[plt...  5.01 us
    pallas_call x1, Pallas kernels, local(): pl.pallas_call(dual_kernel, out_shape=jax.ShapeDtypeStruct((3, depth, row...  2.01 us
    pallas_call x1, Pallas kernels, local(): pl.pallas_call(prepare_kernel, out_shape=[matrix_shape] + state_shapes, i...  1.84 us
    ppermute x8, waiting for transfers between devices, swap(): return lax.ppermute(array, axis, swap_pairs(lax.axis_size(axis), offset))  1.74 us
    pallas_call x1, Pallas kernels, local(): pl.pallas_call(functools.partial(plane_kernel, x_messages), out_shape=sta...  1.71 us
    pallas_call x1, Pallas kernels, local(): pl.pallas_call(row_kernel, out_shape=state_shapes, in_specs=[smem] + [vme...  1.63 us
  transfers between devices with their start and end apart: 9, of which 2 were waited for; matrix products, arithmetic and copies ran while one was open for 0% of the time, Pallas kernels for 16%

profile of v7, /device:TPU:1, one launch (start us, length us, event | category | flops | bytes accessed | tf_op | source)
XLA Modules:
  0.0 46.7 jit_solution(12056693238710439033)
XLA Ops:
  0.6 0.0 copy-start.3
  0.6 5.0 %pack.1 = (bf16[3,32,16,256]{3,2,1,0:T(8,128)(2,1)S(1)}, bf16[3,32,16,256]{3,2,1,0:T(8,128)(2,1)S(1)}, bf16[3,32,16,256]{3,2,1,0:T(8,128)(2,1)S(1)}, bf16[3,32,1...) custom-call(bf16[3,32,16,256]{3,2,1,0:T(8,128)(2,1)} %refs_0_.1, ...), custom_call_target="tpu_custom_call" | custom-call | tf_op jit(solution)/shard_map/pack/pallas_call | solution.py:708
  5.7 0.1 collective-permute-start.3
  5.8 2.7 %collective-permute-start.2 = (f32[30,16,256]{2,1,0:T(8,128)}, f32[30,16,256]{2,1,0:T(8,128)S(1)}, u32[]{:S(2)}, u32[]{:S(2)}) collective-permute-start(f32[30,16,256]{2,1,0:T(8,128)} %get-tuple-element.36), channel_id=1, source_target_pairs={{0,1},{1,0},{2,3},{3,2},{4,5},{5,4},{6,7},{7,6},{8,9},{9,8},{10,11... | collective-permute-start | bytes 1474568 | tf_op jit(solution)/shard_map/ppermute | solution.py:56
  8.5 3.4 %collective-permute-start.6 = (f32[16,32,256]{2,1,0:T(8,128)}, f32[16,32,256]{2,1,0:T(8,128)S(1)}, u32[]{:S(2)}, u32[]{:S(2)}) collective-permute-start(f32[16,32,256]{2,1,0:T(8,128)} %get-tuple-element.47), channel_id=1, source_target_pairs={{2,4},{4,2},{6,8},{8,6},{10,12},{12,10},{3,5},{5,3},{7,9},{9,7},{1... | collective-permute-start | bytes 1572872 | tf_op jit(solution)/shard_map/ppermute | solution.py:56
  11.9 2.1 %collective-permute-start.7 = (f32[16,32,256]{2,1,0:T(8,128)}, f32[16,32,256]{2,1,0:T(8,128)S(1)}, u32[]{:S(2)}, u32[]{:S(2)}) collective-permute-start(f32[16,32,256]{2,1,0:T(8,128)} %get-tuple-element.48), channel_id=1, source_target_pairs={{2,4},{4,2},{6,8},{8,6},{10,12},{12,10},{3,5},{5,3},{7,9},{9,7},{1... | collective-permute-start | bytes 1572872 | tf_op jit(solution)/shard_map/ppermute | solution.py:56
  14.1 1.3 %collective-permute-start = (f32[8,16,128]{2,1,0:T(8,128)S(1)}, f32[8,16,128]{2,1,0:T(8,128)S(1)}, u32[]{:S(2)}, u32[]{:S(2)}) collective-permute-start(f32[8,16,128]{2,1,0:T(8,128)S(1)} %get-tuple-element.34), channel_id=1, source_target_pairs={{0,16},{16,0},{1,17},{17,1},{2,18},{18,2},{3,19},{19,3},{4,20},{20... | collective-permute-start | bytes 196616 | tf_op jit(solution)/shard_map/ppermute | solution.py:56
  15.3 0.0 collective-permute-start.1
  15.4 0.7 %copy-done.2 = s32[2,8,128]{2,1,0:T(8,128)S(1)} copy-done((s32[2,8,128]{2,1,0:T(8,128)S(1)}, s32[2,8,128]{2,1,0:T(8,128)}, u32[]{:S(2)}) %copy-start.2) | copy-done | bytes 8216
  16.1 0.7 %copy-done.5 = f32[4]{0:T(128)S(1)} copy-done((f32[4]{0:T(128)S(1)}, f32[4]{0:T(128)}, u32[]{:S(2)}) %copy-start.5) | copy-done | bytes 40
  16.7 1.8 %prepare.1 = (bf16[1,13,2,256,128]{4,3,2,1,0:T(8,128)(2,1)S(1)}, f32[3,42,3,24,128]{4,3,2,1,0:T(8,128)S(1)}, f32[3,42,3,24,128]{4,3,2,1,0:T(8,128)S(1)}, f32[3,4...) custom-call(f32[4]{0:T(128)S(1)} %copy-done.5, ...), custom_call_target="tpu_custom_call" | custom-call | tf_op jit(solution)/shard_map/prepare/pallas_call | solution.py:731
  18.6 0.5 collective-permute-done.1.refs_1_.others_1_
  19.0 1.7 %collective-permute-done.2.refs_2_.others_2_ = f32[30,16,256]{2,1,0:T(8,128)S(1)} collective-permute-done((f32[30,16,256]{2,1,0:T(8,128)}, f32[30,16,256]{2,1,0:T(8,128)S(1)}, u32[]{:S(2)}, u32[]{:S(2)}) %collective-permute-start.2) | collective-permute-done | bytes 491552 | tf_op jit(solution)/shard_map/ppermute | solution.py:56
  20.7 0.2 corners.1
  20.9 0.7 %collective-permute-start.4 = (f32[35,8,128]{2,1,0:T(8,128)S(1)}, f32[35,8,128]{2,1,0:T(8,128)S(1)}, u32[]{:S(2)}, u32[]{:S(2)}) collective-permute-start(f32[35,8,128]{2,1,0:T(8,128)S(1)} %get-tuple-element.44), channel_id=1, source_target_pairs={{0,2},{2,0},{4,6},{6,4},{8,10},{10,8},{12,14},{14,12},{1,3},{3,1},... | collective-permute-start | bytes 430088 | tf_op jit(solution)/shard_map/ppermute | solution.py:56
  21.6 3.3 %collective-permute-start.5 = (f32[35,8,128]{2,1,0:T(8,128)S(1)}, f32[35,8,128]{2,1,0:T(8,128)S(1)}, u32[]{:S(2)}, u32[]{:S(2)}) collective-permute-start(f32[35,8,128]{2,1,0:T(8,128)S(1)} %get-tuple-element.45), channel_id=1, source_target_pairs={{2,4},{4,2},{6,8},{8,6},{10,12},{12,10},{3,5},{5,3},{7,9},{9,7},{1... | collective-permute-start | bytes 430088 | tf_op jit(solution)/shard_map/ppermute | solution.py:56
  25.0 0.0 copy-start
  25.0 1.7 %planes.1 = (f32[3,42,3,24,128]{4,3,2,1,0:T(8,128)S(1)}, f32[3,42,3,24,128]{4,3,2,1,0:T(8,128)S(1)}, f32[3,42,3,24,128]{4,3,2,1,0:T(8,128)S(1)}, f32[3,42,3,24,1...) custom-call(f32[4]{0:T(128)S(1)} %copy-done.5, ...), custom_call_target="tpu_custom_call", output_to_operand_aliasing={{0}: (5, {}), {1}: (6, {}), {2}: (7, {}), {3}: (8, {}), {4}... | custom-call | tf_op jit(solution)/shard_map/planes/pallas_call | solution.py:754
  26.7 0.0 copy-start.1
  26.8 1.6 %rows.1 = (f32[3,42,3,24,128]{4,3,2,1,0:T(8,128)S(1)}, f32[3,42,3,24,128]{4,3,2,1,0:T(8,128)S(1)}, f32[3,42,3,24,128]{4,3,2,1,0:T(8,128)S(1)}, f32[3,42,3,24,128...) custom-call(f32[4]{0:T(128)S(1)} %copy-done.5, ...), custom_call_target="tpu_custom_call", output_to_operand_aliasing={{0}: (5, {}), {1}: (6, {}), {2}: (7, {}), {3}: (8, {}), {4}... | custom-call | tf_op jit(solution)/shard_map/rows/pallas_call | solution.py:765
  28.4 14.4 %window.1 = (f32[16,256]{1,0:T(8,128)S(1)}, f32[3,42,3,24,128]{4,3,2,1,0:T(8,128)S(1)}, f32[3,42,3,24,128]{4,3,2,1,0:T(8,128)S(1)}, f32[3,42,3,24,128]{4,3,2,1,0...) custom-call(f32[4]{0:T(128)S(1)} %copy-done.5, ...), custom_call_target="tpu_custom_call", output_to_operand_aliasing={{1}: (6, {}), {2}: (7, {}), {3}: (8, {}), {4}: (9, {}), {5}... | custom-call | tf_op jit(solution)/shard_map/window/pallas_call | solution.py:776
  42.8 1.3 %collective-permute-start.8 = (f32[16,256]{1,0:T(8,128)S(1)}, f32[16,256]{1,0:T(8,128)S(1)}, u32[]{:S(2)}, u32[]{:S(2)}) collective-permute-start(f32[16,256]{1,0:T(8,128)S(1)} %get-tuple-element.63), channel_id=1, source_target_pairs={{0,1},{1,0},{2,3},{3,2},{4,5},{5,4},{6,7},{7,6},{8,9},{9,8},{10,11... | collective-permute-start | bytes 49160 | tf_op jit(solution)/shard_map/ppermute | solution.py:56
  44.1 2.0 %dual.1 = f32[3,32,16,256]{3,2,1,0:T(8,128)} custom-call(f32[3,42,3,24,128]{4,3,2,1,0:T(8,128)S(1)} %get-tuple-element.64.third_e, f32[3,42,3,24,128]{4,3,2,1,0:T(8,128)S(1)} %get-tuple-element.65.dual_g), custom_call_target="tpu_custom_call" | custom-call | tf_op jit(solution)/shard_map/dual/pallas_call | solution.py:787
  46.1 0.6 %add.3 = f32[16,256]{1,0:T(8,128)} add(f32[16,256]{1,0:T(8,128)S(1)} %get-tuple-element.63, f32[16,256]{1,0:T(8,128)S(1)} %collective-permute-done.8) | non-fusion elementwise | flops 4096 | bytes 49152 | tf_op jit(solution)/shard_map/add | solution.py:795
  (14 shorter events, 0.0 us)
Async XLA Ops:
  0.6 20.1 %copy-start.3 = (bf16[2,48,128]{2,1,0:T(8,128)(2,1)S(1)}, bf16[2,48,128]{2,1,0:T(8,128)(2,1)}, u32[]{:S(2)}) copy-start(bf16[2,48,128]{2,1,0:T(8,128)(2,1)} %constant.12.clone.refs_3_) | copy-start | bytes 73732
  5.7 9.7 %collective-permute-start.3 = (f32[32,32,256]{2,1,0:T(8,128)S(1)}, f32[32,32,256]{2,1,0:T(8,128)S(1)}, u32[]{:S(2)}, u32[]{:S(2)}) collective-permute-start(f32[32,32,256]{2,1,0:T(8,128)S(1)} %get-tuple-element.42), channel_id=1, source_target_pairs={{0,2},{2,0},{4,6},{6,4},{8,10},{10,8},{12,14},{14,12},{1,3},{3,1},... | collective-permute-start | bytes 3145736 | tf_op jit(solution)/shard_map/ppermute | solution.py:56
  5.8 15.0 %collective-permute-start.2 = (f32[30,16,256]{2,1,0:T(8,128)}, f32[30,16,256]{2,1,0:T(8,128)S(1)}, u32[]{:S(2)}, u32[]{:S(2)}) collective-permute-start(f32[30,16,256]{2,1,0:T(8,128)} %get-tuple-element.36), channel_id=1, source_target_pairs={{0,1},{1,0},{2,3},{3,2},{4,5},{5,4},{6,7},{7,6},{8,9},{9,8},{10,11... | collective-permute-start | bytes 1474568 | tf_op jit(solution)/shard_map/ppermute | solution.py:56
  8.5 18.2 %collective-permute-start.6 = (f32[16,32,256]{2,1,0:T(8,128)}, f32[16,32,256]{2,1,0:T(8,128)S(1)}, u32[]{:S(2)}, u32[]{:S(2)}) collective-permute-start(f32[16,32,256]{2,1,0:T(8,128)} %get-tuple-element.47), channel_id=1, source_target_pairs={{2,4},{4,2},{6,8},{8,6},{10,12},{12,10},{3,5},{5,3},{7,9},{9,7},{1... | collective-permute-start | bytes 1572872 | tf_op jit(solution)/shard_map/ppermute | solution.py:56
  11.9 14.8 %collective-permute-start.7 = (f32[16,32,256]{2,1,0:T(8,128)}, f32[16,32,256]{2,1,0:T(8,128)S(1)}, u32[]{:S(2)}, u32[]{:S(2)}) collective-permute-start(f32[16,32,256]{2,1,0:T(8,128)} %get-tuple-element.48), channel_id=1, source_target_pairs={{2,4},{4,2},{6,8},{8,6},{10,12},{12,10},{3,5},{5,3},{7,9},{9,7},{1... | collective-permute-start | bytes 1572872 | tf_op jit(solution)/shard_map/ppermute | solution.py:56
  14.1 5.0 %collective-permute-start = (f32[8,16,128]{2,1,0:T(8,128)S(1)}, f32[8,16,128]{2,1,0:T(8,128)S(1)}, u32[]{:S(2)}, u32[]{:S(2)}) collective-permute-start(f32[8,16,128]{2,1,0:T(8,128)S(1)} %get-tuple-element.34), channel_id=1, source_target_pairs={{0,16},{16,0},{1,17},{17,1},{2,18},{18,2},{3,19},{19,3},{4,20},{20... | collective-permute-start | bytes 196616 | tf_op jit(solution)/shard_map/ppermute | solution.py:56
  15.3 3.7 %collective-permute-start.1 = (f32[3,16,128]{2,1,0:T(8,128)S(1)}, f32[3,16,128]{2,1,0:T(8,128)S(1)}, u32[]{:S(2)}, u32[]{:S(2)}) collective-permute-start(f32[3,16,128]{2,1,0:T(8,128)S(1)} %get-tuple-element.35), channel_id=1, source_target_pairs={{0,17},{1,16},{16,1},{17,0},{2,19},{3,18},{18,3},{19,2},{4,21},{5,... | collective-permute-start | bytes 73736 | tf_op jit(solution)/shard_map/ppermute | solution.py:682
  15.4 0.7 %copy-start.2 = (s32[2,8,128]{2,1,0:T(8,128)S(1)}, s32[2,8,128]{2,1,0:T(8,128)}, u32[]{:S(2)}) copy-start(s32[2,8,128]{2,1,0:T(8,128)} %constant.14.clone.refs_6_.table) | copy-start | bytes 24580
  16.1 0.7 %copy-start.5 = (f32[4]{0:T(128)S(1)}, f32[4]{0:T(128)}, u32[]{:S(2)}) copy-start(f32[4]{0:T(128)} %inverse.7) | copy-start | bytes 52
  20.9 7.5 %collective-permute-start.4 = (f32[35,8,128]{2,1,0:T(8,128)S(1)}, f32[35,8,128]{2,1,0:T(8,128)S(1)}, u32[]{:S(2)}, u32[]{:S(2)}) collective-permute-start(f32[35,8,128]{2,1,0:T(8,128)S(1)} %get-tuple-element.44), channel_id=1, source_target_pairs={{0,2},{2,0},{4,6},{6,4},{8,10},{10,8},{12,14},{14,12},{1,3},{3,1},... | collective-permute-start | bytes 430088 | tf_op jit(solution)/shard_map/ppermute | solution.py:56
  21.6 6.8 %collective-permute-start.5 = (f32[35,8,128]{2,1,0:T(8,128)S(1)}, f32[35,8,128]{2,1,0:T(8,128)S(1)}, u32[]{:S(2)}, u32[]{:S(2)}) collective-permute-start(f32[35,8,128]{2,1,0:T(8,128)S(1)} %get-tuple-element.45), channel_id=1, source_target_pairs={{2,4},{4,2},{6,8},{8,6},{10,12},{12,10},{3,5},{5,3},{7,9},{9,7},{1... | collective-permute-start | bytes 430088 | tf_op jit(solution)/shard_map/ppermute | solution.py:56
  25.0 1.8 %copy-start = (bf16[2,104,64]{2,1,0:T(8,128)(2,1)S(1)}, bf16[2,104,64]{2,1,0:T(8,128)(2,1)}, u32[]{:S(2)}) copy-start(bf16[2,104,64]{2,1,0:T(8,128)(2,1)} %constant.11.clone.placer) | copy-start | bytes 79876
  26.7 1.7 %copy-start.1 = (bf16[2,64,48]{2,1,0:T(8,128)(2,1)S(1)}, bf16[2,64,48]{2,1,0:T(8,128)(2,1)}, u32[]{:S(2)}) copy-start(bf16[2,64,48]{2,1,0:T(8,128)(2,1)} %constant.13.clone.others_2_) | copy-start | bytes 36868
  26.7 1.7 %copy-start.4 = (s32[16,256]{1,0:T(8,128)S(1)}, s32[16,256]{1,0:T(8,128)}, u32[]{:S(2)}) copy-start(s32[16,256]{1,0:T(8,128)} %height.1) | copy-start | bytes 49156
  42.8 3.3 %collective-permute-start.8 = (f32[16,256]{1,0:T(8,128)S(1)}, f32[16,256]{1,0:T(8,128)S(1)}, u32[]{:S(2)}, u32[]{:S(2)}) collective-permute-start(f32[16,256]{1,0:T(8,128)S(1)} %get-tuple-element.63), channel_id=1, source_target_pairs={{0,1},{1,0},{2,3},{3,2},{4,5},{5,4},{6,7},{7,6},{8,9},{9,8},{10,11... | collective-permute-start | bytes 49160 | tf_op jit(solution)/shard_map/ppermute | solution.py:56
